TPU v7x, 32 devices: a whole 2x2x4 slice. The times are simulated.
32 devices in a mesh: dp: 8 (over y, x, core), tensor: 4 (over z).
Axes of the slice: x: 2, y: 2, z: 4, core: 2. Of those that a mesh axis runs over, the one named last changes fastest.
Arguments:
- inputs: bfloat16 [8192, 2048], P(('dp', 'tensor')), may hold values from -6 to 6
- gain_first: bfloat16 [2048], P('dp'), may hold values from 0.5 to 1.5
- shift_first: bfloat16 [2048], P('dp'), may hold values from -3 to 3
- projections: bfloat16 [3, 2048, 2048], P(None, 'dp', 'tensor'), may hold values from -0.125 to 0.125
- biases: bfloat16 [3, 2048], P(None, 'tensor'), may hold values from -3 to 3
- output_weight: bfloat16 [2048, 2048], P('tensor', 'dp'), may hold values from -0.5 to 0.5
- gain_second: bfloat16 [2048], P('dp'), may hold values from 0.5 to 1.5
- shift_second: bfloat16 [2048], P('dp'), may hold values from -3 to 3
- gate_up: bfloat16 [2, 2048, 5632], P(None, 'dp', 'tensor'), may hold values from -0.125 to 0.125
- down_weight: bfloat16 [5632, 2048], P('tensor', 'dp'), may hold values from -0.15625 to 0.15625
- cotangent: bfloat16 [8192, 2048], P(('dp', 'tensor')), may hold values from -6 to 6
Outputs:
- outputs: bfloat16 [8192, 2048], P(('dp', 'tensor'))
- input_grads: float32 [8192, 2048], P(('dp', 'tensor'))
- gain_first_grad: float32 [2048], P('dp')
- shift_first_grad: float32 [2048], P('dp')
- projections_grad: float32 [3, 2048, 2048], P(None, 'dp', 'tensor')
- biases_grad: float32 [3, 2048], P(None, 'tensor')
- output_weight_grad: float32 [2048, 2048], P('tensor', 'dp')
- gain_second_grad: float32 [2048], P('dp')
- shift_second_grad: float32 [2048], P('dp')
- gate_up_grad: float32 [2, 2048, 5632], P(None, 'dp', 'tensor')
- down_weight_grad: float32 [5632, 2048], P('tensor', 'dp')
All inputs are finite; a program needn't handle non-finite values.
Results may differ from a plain program's by a relative error of at most 0.014.
Values may be sent and summed in bfloat16 or wider, within the bound.
A program may use at most 192 MiB of HBM per device.

v0:
```python
import math

import jax
import jax.numpy as jnp
from jax import lax
from jax.sharding import PartitionSpec as P

HD = 64
ROTARY = 16
SEQ_LEN = 512


EPSILON = 1e-05
ANGLE_BASE = 10000.0
NEGATIVE = -1e30


def norm_rows(rows, gain, shift):
    average = jnp.mean(rows, axis=-1, keepdims=True)
    centred = rows - average
    inverse = lax.rsqrt(jnp.mean(centred * centred, axis=-1, keepdims=True) + EPSILON)
    unit_rows = centred * inverse
    return (unit_rows * gain + shift, unit_rows, inverse)


def norm_back(incoming, unit_rows, inverse, gain):
    scaled = incoming * gain
    inner = (
        scaled
        - jnp.mean(scaled, axis=-1, keepdims=True)
        - unit_rows * jnp.mean(scaled * unit_rows, axis=-1, keepdims=True)
    )
    return (inner * inverse, jnp.sum(incoming * unit_rows, axis=0), jnp.sum(incoming, axis=0))


def angle_tables():
    freqs = 1.0 / ANGLE_BASE ** (jnp.arange(0, ROTARY, 2).astype(jnp.float32) / ROTARY)
    angles = jnp.arange(SEQ_LEN).astype(jnp.float32)[:, None] * freqs[None, :]
    return (jnp.cos(angles), jnp.sin(angles))


def rotate(heads, cosine, sine, sign):
    half_rot = ROTARY // 2
    first = heads[..., :half_rot]
    latter = heads[..., half_rot:ROTARY]
    cos_part = cosine[:, None, :]
    sin_part = sine[:, None, :] * sign
    return jnp.concatenate(
        [
            first * cos_part - latter * sin_part,
            latter * cos_part + first * sin_part,
            heads[..., ROTARY:],
        ],
        axis=-1,
    )


def causal_scores(queries, key_rows):
    scaling = 1.0 / math.sqrt(HD)
    scores = scaling * jnp.einsum(
        "qhd,khd->hqk", queries, key_rows, preferred_element_type=jnp.float32
    )
    causal = jnp.arange(SEQ_LEN)[:, None] >= jnp.arange(SEQ_LEN)[None, :]
    return jnp.where(causal[None], scores, NEGATIVE)


def attend_forward(pieces):
    queries, key_rows, value_rows = pieces
    scores = causal_scores(queries, key_rows)
    row_top = jnp.max(scores, axis=-1, keepdims=True)
    exponent = jnp.exp(scores - row_top)
    totals = jnp.sum(exponent, axis=-1, keepdims=True)
    weights = (exponent / totals).astype(jnp.bfloat16)
    mixed = jnp.einsum("hqk,khd->qhd", weights, value_rows, preferred_element_type=jnp.float32)
    return (mixed.astype(jnp.bfloat16), (row_top + jnp.log(totals))[..., 0])


def attend_back(pieces):
    queries, key_rows, value_rows, grad_mixed, log_totals = pieces
    scaling = 1.0 / math.sqrt(HD)
    scores = causal_scores(queries, key_rows)
    weights = jnp.exp(scores - log_totals[..., None])
    grad_values = jnp.einsum(
        "hqk,qhd->khd", weights.astype(jnp.bfloat16), grad_mixed, preferred_element_type=jnp.float32
    )
    grad_weights = jnp.einsum(
        "qhd,khd->hqk", grad_mixed, value_rows, preferred_element_type=jnp.float32
    )
    grad_scores = weights * (grad_weights - jnp.sum(weights * grad_weights, axis=-1, keepdims=True))
    grad_scores = grad_scores.astype(jnp.bfloat16)
    grad_queries = scaling * jnp.einsum(
        "hqk,khd->qhd", grad_scores, key_rows, preferred_element_type=jnp.float32
    )
    grad_keys = scaling * jnp.einsum(
        "hqk,qhd->khd", grad_scores, queries, preferred_element_type=jnp.float32
    )
    return (grad_queries, grad_keys, grad_values)


def local(
    inputs,
    gain_first,
    shift_first,
    projections,
    biases,
    output_weight,
    gain_second,
    shift_second,
    gate_up,
    down_weight,
    cotangent,
):
    tensor_ways = lax.axis_size("tensor")
    row_count = inputs.shape[0]
    group_rows = row_count * tensor_ways
    sequences = group_rows // SEQ_LEN
    head_width = output_weight.shape[0]
    local_heads = head_width // HD
    head_shape = (sequences, SEQ_LEN, local_heads, HD)
    cosine, sine = angle_tables()
    proj_full, out_full, gain_one, shift_one = (
        lax.all_gather(projections, "dp", axis=1, tiled=True),
        lax.all_gather(output_weight, "dp", axis=1, tiled=True),
        lax.all_gather(gain_first, "dp", axis=0, tiled=True),
        lax.all_gather(shift_first, "dp", axis=0, tiled=True),
    )
    gain_one = gain_one.astype(jnp.float32)
    residual = inputs.astype(jnp.float32)
    normed_one, unit_one, inverse_one = norm_rows(residual, gain_one, shift_one.astype(jnp.float32))
    gathered_one = lax.all_gather(normed_one.astype(jnp.bfloat16), "tensor", axis=0, tiled=True)
    pre_all = jnp.einsum("gd,jde->jge", gathered_one, proj_full, preferred_element_type=jnp.float32)
    pre_all = pre_all + biases.astype(jnp.float32)[:, None, :]
    queries = rotate(pre_all[0].reshape(head_shape), cosine, sine, 1.0).astype(jnp.bfloat16)
    key_rows = rotate(pre_all[1].reshape(head_shape), cosine, sine, 1.0).astype(jnp.bfloat16)
    value_rows = pre_all[2].reshape(head_shape).astype(jnp.bfloat16)
    mixed, log_totals = lax.map(attend_forward, (queries, key_rows, value_rows))
    mixed_rows = mixed.reshape(group_rows, head_width)
    part = mixed_rows
    middle = residual + lax.psum_scatter(
        jnp.dot(part, out_full, preferred_element_type=jnp.float32),
        "tensor",
        scatter_dimension=0,
        tiled=True,
    )
    gu_full, down_full, gain_two, shift_two = (
        lax.all_gather(gate_up, "dp", axis=1, tiled=True),
        lax.all_gather(down_weight, "dp", axis=1, tiled=True),
        lax.all_gather(gain_second, "dp", axis=0, tiled=True),
        lax.all_gather(shift_second, "dp", axis=0, tiled=True),
    )
    gain_two = gain_two.astype(jnp.float32)
    normed_two, unit_two, inverse_two = norm_rows(middle, gain_two, shift_two.astype(jnp.float32))
    gathered_two = lax.all_gather(normed_two.astype(jnp.bfloat16), "tensor", axis=0, tiled=True)
    gate_act = jnp.dot(gathered_two, gu_full[0], preferred_element_type=jnp.float32)
    up_act = jnp.dot(gathered_two, gu_full[1], preferred_element_type=jnp.float32)
    sigmoid_gate = jax.nn.sigmoid(gate_act)
    hidden = (gate_act * sigmoid_gate * up_act).astype(jnp.bfloat16)
    part = hidden
    outputs = (
        middle
        + lax.psum_scatter(
            jnp.dot(part, down_full, preferred_element_type=jnp.float32),
            "tensor",
            scatter_dimension=0,
            tiled=True,
        )
    ).astype(jnp.bfloat16)
    gu_back, down_back, gain_two_back = (
        lax.all_gather(gate_up, "dp", axis=1, tiled=True),
        lax.all_gather(down_weight, "dp", axis=1, tiled=True),
        lax.all_gather(gain_second, "dp", axis=0, tiled=True),
    )
    gain_two_back = gain_two_back.astype(jnp.float32)
    gathered_cot = lax.all_gather(cotangent, "tensor", axis=0, tiled=True)
    grad_hidden = jnp.einsum(
        "gd,fd->gf", gathered_cot, down_back, preferred_element_type=jnp.float32
    )
    down_grad = jnp.einsum("gf,gd->fd", hidden, gathered_cot, preferred_element_type=jnp.float32)
    grad_up = (grad_hidden * gate_act * sigmoid_gate).astype(jnp.bfloat16)
    grad_gate = (
        grad_hidden * up_act * sigmoid_gate * (1.0 + gate_act * (1.0 - sigmoid_gate))
    ).astype(jnp.bfloat16)
    gu_grad = jnp.stack(
        [
            jnp.einsum("gd,gf->df", gathered_two, grad_gate, preferred_element_type=jnp.float32),
            jnp.einsum("gd,gf->df", gathered_two, grad_up, preferred_element_type=jnp.float32),
        ]
    )
    first_term = jnp.einsum("gf,df->gd", grad_gate, gu_back[0], preferred_element_type=jnp.float32)
    grad_second = lax.psum_scatter(
        first_term
        + jnp.einsum("gf,df->gd", grad_up, gu_back[1], preferred_element_type=jnp.float32),
        "tensor",
        scatter_dimension=0,
        tiled=True,
    )
    gu_owned, down_owned = (
        lax.psum_scatter(gu_grad, "dp", scatter_dimension=1, tiled=True),
        lax.psum_scatter(down_grad, "dp", scatter_dimension=1, tiled=True),
    )
    grad_mid_norm, gain_two_part, shift_two_part = norm_back(
        grad_second, unit_two, inverse_two, gain_two_back
    )
    grad_middle = cotangent.astype(jnp.float32) + grad_mid_norm
    proj_back, out_back, gain_one_back = (
        lax.all_gather(projections, "dp", axis=1, tiled=True),
        lax.all_gather(output_weight, "dp", axis=1, tiled=True),
        lax.all_gather(gain_first, "dp", axis=0, tiled=True),
    )
    gain_one_back = gain_one_back.astype(jnp.float32)
    gathered_branch = lax.all_gather(grad_middle.astype(jnp.bfloat16), "tensor", axis=0, tiled=True)
    out_grad = jnp.einsum(
        "ge,gd->ed", mixed_rows, gathered_branch, preferred_element_type=jnp.float32
    )
    grad_mixed = jnp.einsum(
        "gd,ed->ge", gathered_branch, out_back, preferred_element_type=jnp.float32
    ).astype(jnp.bfloat16)
    grad_queries, grad_keys, grad_values = lax.map(
        attend_back, (queries, key_rows, value_rows, grad_mixed.reshape(head_shape), log_totals)
    )
    grad_queries = rotate(grad_queries, cosine, sine, -1.0)
    grad_keys = rotate(grad_keys, cosine, sine, -1.0)
    grad_pre = (
        jnp.stack([grad_queries, grad_keys, grad_values])
        .reshape(3, group_rows, head_width)
        .astype(jnp.bfloat16)
    )
    bias_part = jnp.sum(grad_pre, axis=1, dtype=jnp.float32)
    proj_grad = jnp.einsum(
        "gd,jge->jde", gathered_one, grad_pre, preferred_element_type=jnp.float32
    )
    part = grad_pre
    grad_normed = lax.psum_scatter(
        jnp.einsum("jge,jde->gd", part, proj_back, preferred_element_type=jnp.float32),
        "tensor",
        scatter_dimension=0,
        tiled=True,
    )
    proj_owned, out_owned = (
        lax.psum_scatter(proj_grad, "dp", scatter_dimension=1, tiled=True),
        lax.psum_scatter(out_grad, "dp", scatter_dimension=1, tiled=True),
    )
    grad_in_norm, gain_one_part, shift_one_part = norm_back(
        grad_normed, unit_one, inverse_one, gain_one_back
    )
    input_grads = grad_middle + grad_in_norm
    one_hot = (jnp.arange(tensor_ways) == lax.axis_index("tensor")).astype(jnp.float32)
    spread_bias = (bias_part[:, None, :] * one_hot[None, :, None]).reshape(
        3, tensor_ways * head_width
    )
    summed = lax.psum(
        (gain_one_part, shift_one_part, gain_two_part, shift_two_part, spread_bias),
        ("dp", "tensor"),
    )
    own_width = gain_first.shape[0]
    own_offset = lax.axis_index("dp") * own_width

    def own_part(vector):
        return lax.dynamic_slice_in_dim(vector, own_offset, own_width, 0)

    bias_grad = jnp.sum(
        summed[4].reshape(3, tensor_ways, head_width) * one_hot[None, :, None], axis=1
    )
    return (
        outputs,
        input_grads,
        own_part(summed[0]),
        own_part(summed[1]),
        proj_owned,
        bias_grad,
        out_owned,
        own_part(summed[2]),
        own_part(summed[3]),
        gu_owned,
        down_owned,
    )


def solution(mesh):
    return jax.shard_map(
        local,
        mesh=mesh,
        in_specs=(
            P(("dp", "tensor"), None),
            P("dp"),
            P("dp"),
            P(None, "dp", "tensor"),
            P(None, "tensor"),
            P("tensor", "dp"),
            P("dp"),
            P("dp"),
            P(None, "dp", "tensor"),
            P("tensor", "dp"),
            P(("dp", "tensor"), None),
        ),
        out_specs=(
            P(("dp", "tensor"), None),
            P(("dp", "tensor"), None),
            P("dp"),
            P("dp"),
            P(None, "dp", "tensor"),
            P(None, "tensor"),
            P("tensor", "dp"),
            P("dp"),
            P("dp"),
            P(None, "dp", "tensor"),
            P("tensor", "dp"),
        ),
        check_vma=False,
    )
```

profile of v0, /device:TPU:9, one launch (start us, length us, event | category | flops | bytes accessed | tf_op | source)
XLA Modules:
  0.0 1679.7 jit_solution(7815647067529716616)
XLA Ops:
  35.5 75.7 %all-gather.13.cloned.1.call-done = bf16[1024,2048]{1,0:T(8,128)(2,1)} async-done(((bf16[256,2048]{1,0:T(8,128)(2,1)}), bf16[1024,2048]{1,0:T(8,128)(2,1)}) %all-gather.13.cloned.1.call-update) | async-done | bytes 4194320 | tf_op jit(solution)/shard_map/all_gather | solution.py:130
  111.3 48.9 %all-gather.15.cloned.1.call-done = bf16[3,2048,512]{2,1,0:T(8,128)(2,1)} async-done(((bf16[3,256,512]{2,1,0:T(8,128)(2,1)}), bf16[3,2048,512]{2,1,0:T(8,128)(2,1)}) %all-gather.15.cloned.1.call-update) | async-done | bytes 6291472 | tf_op jit(solution)/shard_map/all_gather | solution.py:122
  195.2 13.9 while.26
  238.0 126.4 %reduce-scatter.9.cloned.1.call-done = f32[256,2048]{1,0:T(8,128)} async-done(((f32[1024,2048]{1,0:T(8,128)}), f32[256,2048]{1,0:T(8,128)}) %reduce-scatter.9.cloned.1.call-update) | async-done | bytes 2097168 | tf_op jit(solution)/shard_map/reduce_scatter | solution.py:139
  370.7 64.7 %all-gather.21.cloned.1.call-done = bf16[2,2048,1408]{2,1,0:T(8,128)(2,1)} async-done(((bf16[2,256,1408]{2,1,0:T(8,128)(2,1)}), bf16[2,2048,1408]{2,1,0:T(8,128)(2,1)}) %all-gather.21.cloned.1.call-update) | async-done | bytes 11534352 | tf_op jit(solution)/shard_map/all_gather | solution.py:146
  435.3 79.8 %all-gather.19.cloned.1.call-done = bf16[1024,2048]{1,0:T(8,128)(2,1)} async-done(((bf16[256,2048]{1,0:T(8,128)(2,1)}), bf16[1024,2048]{1,0:T(8,128)(2,1)}) %all-gather.19.cloned.1.call-update) | async-done | bytes 4194320 | tf_op jit(solution)/shard_map/all_gather | solution.py:153
  515.2 12.3 fusion.55
  536.0 60.1 %all-gather.25.cloned.1.call-done = bf16[1024,2048]{1,0:T(8,128)(2,1)} async-done(((bf16[256,2048]{1,0:T(8,128)(2,1)}), bf16[1024,2048]{1,0:T(8,128)(2,1)}) %all-gather.25.cloned.1.call-update) | async-done | bytes 4194320 | tf_op jit(solution)/shard_map/all_gather | solution.py:174
  596.1 47.7 %all-gather.23.cloned.1.call-done = bf16[1408,2048]{1,0:T(8,128)(2,1)} async-done(((bf16[1408,256]{1,0:T(8,128)(2,1)}), bf16[1408,2048]{1,0:T(8,128)(2,1)}) %all-gather.23.cloned.1.call-update) | async-done | bytes 5767184 | tf_op jit(solution)/shard_map/all_gather | solution.py:147
  643.8 15.7 multiply_convert_fusion.1
  659.5 10.8 fusion.54
  681.1 11.7 fusion.82
  692.9 132.1 %reduce-scatter.13.cloned.1.call-done = f32[256,2048]{1,0:T(8,128)} async-done(((f32[1024,2048]{1,0:T(8,128)}), f32[256,2048]{1,0:T(8,128)}) %reduce-scatter.13.cloned.1.call-update) | async-done | bytes 2097168 | tf_op jit(solution)/shard_map/reduce_scatter | solution.py:190
  828.8 143.7 %reduce-scatter.11.cloned.1.call-done = f32[256,2048]{1,0:T(8,128)} async-done(((f32[1024,2048]{1,0:T(8,128)}), f32[256,2048]{1,0:T(8,128)}) %reduce-scatter.11.cloned.1.call-update) | async-done | bytes 2097168 | tf_op jit(solution)/shard_map/reduce_scatter | solution.py:161
  978.5 79.3 %all-gather.27.cloned.1.call-done = bf16[1024,2048]{1,0:T(8,128)(2,1)} async-done(((bf16[256,2048]{1,0:T(8,128)(2,1)}), bf16[1024,2048]{1,0:T(8,128)(2,1)}) %all-gather.27.cloned.1.call-update) | async-done | bytes 4194320 | tf_op jit(solution)/shard_map/all_gather | solution.py:211
  1071.3 26.9 %while.27 = (s32[]{:T(128)}, f32[2,512,8,64]{1,3,2,0:T(8,128)}, f32[2,512,8,64]{1,3,2,0:T(8,128)}, bf16[2,512,8,64]{1,3,2,0:T(8,128)(2,1)}, bf16[2,512,8,64]{1,3...) while((s32[]{:T(128)}, f32[2,512,8,64]{1,3,2,0:T(8,128)}, ...), condition=%wide.region_15.16_spmd, body=%wide.region_13.15_spmd.sunk | while | flops 1374416896 | bytes 117036352 | solution.py:218
  1121.9 11.8 convolution_bitcast_fusion.3
  1135.6 11.7 convolution_bitcast_fusion.2
  1195.3 83.8 %reduce-scatter.15.cloned.1.call-done = f32[256,2048]{1,0:T(8,128)} async-done(((f32[1024,2048]{1,0:T(8,128)}), f32[256,2048]{1,0:T(8,128)}) %reduce-scatter.15.cloned.1.call-update) | async-done | bytes 2097168 | tf_op jit(solution)/shard_map/reduce_scatter | solution.py:233
  1281.9 41.5 %all-reduce = (f32[2048]{0:T(1024)S(1)}, f32[2048]{0:T(1024)S(1)}, f32[3,4,512]{2,1,0:T(4,128)S(1)}, f32[2048]{0:T(1024)S(1)}, f32[2048]{0:T(1024)S(1)}) all-reduce(f32[2048]{0:T(1024)S(1)} %get-tuple-element.204, f32[2048]{0:T(1024)S(1)} %get-tuple-element.209, ...), channel_id=1, replica_groups=mesh['dp'=8,'tensor'=4] {'dp','tensor'}, use_global_device_ids=true, to_apply=%region_20.21 | all-reduce | flops 14336 | bytes 114688 | tf_op jit(solution)/shard_map/psum | solution.py:251
  1330.4 46.3 %reduce-scatter.17.cloned.1.call-done = f32[3,256,512]{1,2,0:T(8,128)} async-done(((f32[3,2048,512]{1,2,0:T(8,128)}), f32[3,256,512]{1,2,0:T(8,128)}) %reduce-scatter.17.cloned.1.call-update) | async-done | bytes 1572880 | tf_op jit(solution)/shard_map/reduce_scatter | solution.py:240
  1379.7 87.7 %reduce-scatter.23.cloned.1.call-done = f32[1408,256]{1,0:T(8,128)} async-done(((f32[1408,2048]{1,0:T(8,128)}), f32[1408,256]{1,0:T(8,128)}) %reduce-scatter.23.cloned.1.call-update) | async-done | bytes 1441808 | tf_op jit(solution)/shard_map/reduce_scatter | solution.py:199
  1467.4 55.1 %reduce-scatter.19.cloned.1.call-done = f32[512,256]{1,0:T(8,128)} async-done(((f32[512,2048]{1,0:T(8,128)}), f32[512,256]{1,0:T(8,128)}) %reduce-scatter.19.cloned.1.call-update) | async-done | bytes 524304 | tf_op jit(solution)/shard_map/reduce_scatter | solution.py:241
  1522.6 150.4 %reduce-scatter.21.cloned.1.call-done = f32[2,256,1408]{2,1,0:T(8,128)} async-done(((f32[2,2048,1408]{2,1,0:T(8,128)}), f32[2,256,1408]{2,1,0:T(8,128)}) %reduce-scatter.21.cloned.1.call-update) | async-done | bytes 2883600 | tf_op jit(solution)/shard_map/reduce_scatter | solution.py:198
  (262 shorter events, 266.7 us)
Async XLA Ops:
  7.2 104.1 %all-gather.13.cloned.1.call-start = ((), (), s32[]{:S(2)}) async-start(), calls=%async_computation.8 | async-start | bytes 5242880 | tf_op jit(solution)/shard_map/all_gather | solution.py:130
  33.2 127.0 %all-gather.15.cloned.1.call-start = ((), (), s32[]{:S(2)}) async-start(), calls=%async_computation.9 | async-start | bytes 7077888 | tf_op jit(solution)/shard_map/all_gather | solution.py:122
  33.9 179.0 %all-gather.17.cloned.1.call-start = ((), (), s32[]{:S(2)}) async-start(), calls=%async_computation.10 | async-start | bytes 2359296 | tf_op jit(solution)/shard_map/all_gather | solution.py:123
  34.7 329.8 %reduce-scatter.9.cloned.1.call-start = ((), (), s32[]{:S(2)}) async-start(), calls=%async_computation.11 | async-start | bytes 10485760 | tf_op jit(solution)/shard_map/reduce_scatter | solution.py:139
  35.5 154.6 %copy-start.21 = (f32[512,8]{0,1:T(8,128)}, f32[512,8]{0,1:T(8,128)S(1)}, u32[]{:S(2)}) copy-start(f32[512,8]{0,1:T(8,128)S(1)} %get-tuple-element.273) | copy-start | bytes 49156
  220.5 143.9 %copy-start.1 = (bf16[256,2048]{1,0:T(8,128)(2,1)S(1)}, bf16[256,2048]{1,0:T(8,128)(2,1)}, u32[]{:S(2)}) copy-start(bf16[256,2048]{1,0:T(8,128)(2,1)} %param.15) | copy-start | bytes 3145732
  220.6 214.8 %all-gather.21.cloned.1.call-start = ((), (), s32[]{:S(2)}) async-start(), calls=%async_computation.13 | async-start | bytes 12976128 | tf_op jit(solution)/shard_map/all_gather | solution.py:146
  221.1 294.0 %all-gather.19.cloned.1.call-start = ((), (), s32[]{:S(2)}) async-start(), calls=%async_computation.12 | async-start | bytes 5242880 | tf_op jit(solution)/shard_map/all_gather | solution.py:153
  369.1 227.0 %all-gather.25.cloned.1.call-start = ((), (), s32[]{:S(2)}) async-start(), calls=%async_computation.16 | async-start | bytes 5242880 | tf_op jit(solution)/shard_map/all_gather | solution.py:174
  369.9 273.9 %all-gather.23.cloned.1.call-start = ((), (), s32[]{:S(2)}) async-start(), calls=%async_computation.14 | async-start | bytes 6488064 | tf_op jit(solution)/shard_map/all_gather | solution.py:147
  370.6 454.4 %reduce-scatter.13.cloned.1.call-start = ((), (), s32[]{:S(2)}) async-start(), calls=%async_computation.17 | async-start | bytes 10485760 | tf_op jit(solution)/shard_map/reduce_scatter | solution.py:190
  681.1 291.4 %reduce-scatter.11.cloned.1.call-start = ((), (), s32[]{:S(2)}) async-start(), calls=%async_computation.15 | async-start | bytes 10485760 | tf_op jit(solution)/shard_map/reduce_scatter | solution.py:161
  692.9 279.6 %copy-start.8 = (bf16[256,2048]{1,0:T(8,128)(2,1)S(1)}, bf16[256,2048]{1,0:T(8,128)(2,1)}, u32[]{:S(2)}) copy-start(bf16[256,2048]{1,0:T(8,128)(2,1)} %param.25) | copy-start | bytes 3145732
  692.9 364.9 %all-gather.27.cloned.1.call-start = ((), (), s32[]{:S(2)}) async-start(), calls=%async_computation.18 | async-start | bytes 5242880 | tf_op jit(solution)/shard_map/all_gather | solution.py:211
  978.4 300.7 %reduce-scatter.15.cloned.1.call-start = ((), (), s32[]{:S(2)}) async-start(), calls=%async_computation.19 | async-start | bytes 10485760 | tf_op jit(solution)/shard_map/reduce_scatter | solution.py:233
  1133.7 243.0 %reduce-scatter.17.cloned.1.call-start = ((), (), s32[]{:S(2)}) async-start(), calls=%async_computation.20 | async-start | bytes 14155776 | tf_op jit(solution)/shard_map/reduce_scatter | solution.py:240
  1147.3 320.2 %reduce-scatter.23.cloned.1.call-start = ((), (), s32[]{:S(2)}) async-start(), calls=%async_computation.23 | async-start | bytes 12976128 | tf_op jit(solution)/shard_map/reduce_scatter | solution.py:199
  1159.7 362.9 %reduce-scatter.19.cloned.1.call-start = ((), (), s32[]{:S(2)}) async-start(), calls=%async_computation.21 | async-start | bytes 4718592 | tf_op jit(solution)/shard_map/reduce_scatter | solution.py:241
  1167.5 505.4 %reduce-scatter.21.cloned.1.call-start = ((), (), s32[]{:S(2)}) async-start(), calls=%async_computation.22 | async-start | bytes 25952256 | tf_op jit(solution)/shard_map/reduce_scatter | solution.py:198
  1192.7 86.5 %copy-start.2 = (bf16[256,2048]{1,0:T(8,128)(2,1)S(1)}, bf16[256,2048]{1,0:T(8,128)(2,1)}, u32[]{:S(2)}) copy-start(bf16[256,2048]{1,0:T(8,128)(2,1)} %param.15) | copy-start | bytes 3145732
  1192.7 86.5 %copy-start.24 = (f32[8,1,256]{2,1,0:T(1,128)S(1)}, f32[8,1,256]{2,1,0:T(1,128)}, u32[]{:S(2)}) copy-start(f32[8,1,256]{2,1,0:T(1,128)} %copy-done.23) | copy-start | bytes 24580
  1192.7 86.4 %copy-start.29 = (f32[256]{0:T(256)S(1)}, f32[256]{0:T(256)}, u32[]{:S(2)}) copy-start(f32[256]{0:T(256)} %copy-done.28) | copy-start | bytes 3076
  1192.8 89.1 %copy-start.26 = (f32[2048]{0:T(1024)S(1)}, f32[2048]{0:T(1024)}, u32[]{:S(2)}) copy-start(f32[2048]{0:T(1024)} %get-tuple-element.202) | copy-start | bytes 24580
  1192.8 89.1 %copy-start.27 = (f32[2048]{0:T(1024)S(1)}, f32[2048]{0:T(1024)}, u32[]{:S(2)}) copy-start(f32[2048]{0:T(1024)} %get-tuple-element.208) | copy-start | bytes 24580
  (43 other events, 301.2 us)
Sparse Core Ops, SparseCore 0:
  33.3 77.9 all-gather.12
  113.2 46.9 all-gather.14
  162.1 28.2 all-gather.16
  220.7 143.7 reduce-scatter.8
  366.2 69.0 all-gather.20
  437.3 77.8 all-gather.18
  516.7 79.2 all-gather.24
  597.9 45.8 all-gather.22
  681.2 143.7 reduce-scatter.12
  827.2 145.1 reduce-scatter.10
  978.6 79.2 all-gather.26
  1133.8 145.2 reduce-scatter.14
  1282.6 94.0 reduce-scatter.16
  1380.6 86.7 reduce-scatter.22
  1471.2 51.3 reduce-scatter.18
  1527.0 145.8 reduce-scatter.20
where the time goes:
time: 1690 us; the launch traced here: 1680 us
  waiting for transfers between devices  1290 us (76%)
  matrix products  177 us (10%)
  blocking collectives  76.5 us (5%)
  local copies, waits for them, and re-layouts  72.9 us (4%)
  other arithmetic  52 us (3%)
    reduce_scatter x1, waiting for transfers between devices, local(): lax.psum_scatter(gu_grad, 'dp', scatter_dimension=1, tiled=True)  150 us
    reduce_scatter x1, waiting for transfers between devices, local(): lax.psum_scatter(jnp.dot(part, down_full, preferred_element_type=jnp.floa...  144 us
    reduce_scatter x1, waiting for transfers between devices, local(): lax.psum_scatter(first_term + jnp.einsum('gf,df->gd', grad_up, gu_back[1]...  132 us
    reduce_scatter x1, waiting for transfers between devices, local(): lax.psum_scatter(jnp.dot(part, out_full, preferred_element_type=jnp.float...  126 us
    reduce_scatter x1, waiting for transfers between devices, local(): lax.psum_scatter(down_grad, 'dp', scatter_dimension=1, tiled=True)  87.7 us
    reduce_scatter x1, waiting for transfers between devices, local(): lax.psum_scatter(jnp.einsum('jge,jde->gd', part, proj_back, preferred_ele...  83.8 us
    all_gather x1, waiting for transfers between devices, local(): lax.all_gather(normed_two.astype(jnp.bfloat16), 'tensor', axis=0, tiled=T...  79.8 us
    all_gather x1, waiting for transfers between devices, local(): lax.all_gather(grad_middle.astype(jnp.bfloat16), 'tensor', axis=0, tiled=...  79.3 us
  transfers between devices with their start and end apart: 16, of which 15 were waited for; matrix products, arithmetic and copies ran while one was open for 10% of the time, Pallas kernels for 0%

commit v1 on v0

--- a/solution.py
+++ b/solution.py
@@ -95,6 +95,13 @@
         "hqk,qhd->khd", grad_scores, queries, preferred_element_type=jnp.float32
     )
     return (grad_queries, grad_keys, grad_values)
+
+
+def scatter_sum(terms, axis, dimension):
+    owned = lax.psum_scatter(
+        terms.astype(jnp.bfloat16), axis, scatter_dimension=dimension, tiled=True
+    )
+    return owned.astype(jnp.float32)
 
 
 def local(
@@ -136,11 +143,8 @@
     mixed, log_totals = lax.map(attend_forward, (queries, key_rows, value_rows))
     mixed_rows = mixed.reshape(group_rows, head_width)
     part = mixed_rows
-    middle = residual + lax.psum_scatter(
-        jnp.dot(part, out_full, preferred_element_type=jnp.float32),
-        "tensor",
-        scatter_dimension=0,
-        tiled=True,
+    middle = residual + scatter_sum(
+        jnp.dot(part, out_full, preferred_element_type=jnp.float32), "tensor", 0
     )
     gu_full, down_full, gain_two, shift_two = (
         lax.all_gather(gate_up, "dp", axis=1, tiled=True),
@@ -158,12 +162,7 @@
     part = hidden
     outputs = (
         middle
-        + lax.psum_scatter(
-            jnp.dot(part, down_full, preferred_element_type=jnp.float32),
-            "tensor",
-            scatter_dimension=0,
-            tiled=True,
-        )
+        + scatter_sum(jnp.dot(part, down_full, preferred_element_type=jnp.float32), "tensor", 0)
     ).astype(jnp.bfloat16)
     gu_back, down_back, gain_two_back = (
         lax.all_gather(gate_up, "dp", axis=1, tiled=True),
@@ -187,16 +186,15 @@
         ]
     )
     first_term = jnp.einsum("gf,df->gd", grad_gate, gu_back[0], preferred_element_type=jnp.float32)
-    grad_second = lax.psum_scatter(
+    grad_second = scatter_sum(
         first_term
         + jnp.einsum("gf,df->gd", grad_up, gu_back[1], preferred_element_type=jnp.float32),
         "tensor",
-        scatter_dimension=0,
-        tiled=True,
+        0,
     )
     gu_owned, down_owned = (
-        lax.psum_scatter(gu_grad, "dp", scatter_dimension=1, tiled=True),
-        lax.psum_scatter(down_grad, "dp", scatter_dimension=1, tiled=True),
+        scatter_sum(gu_grad, "dp", 1),
+        scatter_sum(down_grad, "dp", 1),
     )
     grad_mid_norm, gain_two_part, shift_two_part = norm_back(
         grad_second, unit_two, inverse_two, gain_two_back
@@ -230,15 +228,14 @@
         "gd,jge->jde", gathered_one, grad_pre, preferred_element_type=jnp.float32
     )
     part = grad_pre
-    grad_normed = lax.psum_scatter(
+    grad_normed = scatter_sum(
         jnp.einsum("jge,jde->gd", part, proj_back, preferred_element_type=jnp.float32),
         "tensor",
-        scatter_dimension=0,
-        tiled=True,
+        0,
     )
     proj_owned, out_owned = (
-        lax.psum_scatter(proj_grad, "dp", scatter_dimension=1, tiled=True),
-        lax.psum_scatter(out_grad, "dp", scatter_dimension=1, tiled=True),
+        scatter_sum(proj_grad, "dp", 1),
+        scatter_sum(out_grad, "dp", 1),
     )
     grad_in_norm, gain_one_part, shift_one_part = norm_back(
         grad_normed, unit_one, inverse_one, gain_one_back

time: 1690 us -> 1220 us (0.72)
  waiting for transfers between devices: 1290 us -> 818 us
    reduce_scatter x8, waiting for transfers between devices: 826 us -> 392 us  [scatter_sum(): lax.psum_scatter(terms.astype(jnp.bfloat16), axis, scatter_dimension=dime...]
    all_gather x1, waiting for transfers between devices: 79.3 us -> 45.9 us  [local(): lax.all_gather(grad_middle.astype(jnp.bfloat16), 'tensor', axis=0, tiled=...]
  transfers between devices with their start and end apart: 16 -> 16, of which waited for: 15 -> 14; matrix products, arithmetic and copies ran while one was open for 10% -> 19% of each run, Pallas kernels for 0% -> 0%
where the time goes in v1:
time: 1220 us; the launch traced here: 1210 us
  waiting for transfers between devices  818 us (67%)
  matrix products  174 us (14%)
  blocking collectives  80.4 us (7%)
  local copies, waits for them, and re-layouts  64.8 us (5%)
  other arithmetic  53.3 us (4%)
  between operations  15 us (1%)
    reduce_scatter x8, waiting for transfers between devices, scatter_sum(): lax.psum_scatter(terms.astype(jnp.bfloat16), axis, scatter_dimension=dime...  392 us
    all_gather x1, waiting for transfers between devices, local(): lax.all_gather(normed_two.astype(jnp.bfloat16), 'tensor', axis=0, tiled=T...  79.9 us
    all_gather x1, waiting for transfers between devices, local(): lax.all_gather(normed_one.astype(jnp.bfloat16), 'tensor', axis=0, tiled=T...  75.7 us
    all_gather x1, waiting for transfers between devices, local(): lax.all_gather(gate_up, 'dp', axis=1, tiled=True)  63.9 us
    all_gather x1, waiting for transfers between devices, local(): gathered_cot = lax.all_gather(cotangent, 'tensor', axis=0, tiled=True)  60.2 us
    all_gather x1, waiting for transfers between devices, local(): lax.all_gather(projections, 'dp', axis=1, tiled=True)  48.9 us
    all_gather x1, waiting for transfers between devices, local(): lax.all_gather(down_weight, 'dp', axis=1, tiled=True)  47.9 us
    all_gather x1, waiting for transfers between devices, local(): lax.all_gather(grad_middle.astype(jnp.bfloat16), 'tensor', axis=0, tiled=...  45.9 us
  transfers between devices with their start and end apart: 16, of which 14 were waited for; matrix products, arithmetic and copies ran while one was open for 19% of the time, Pallas kernels for 0%

profile of v1, /device:TPU:9, one launch (start us, length us, event | category | flops | bytes accessed | tf_op | source)
XLA Modules:
  0.0 1206.9 jit_solution(12776352936327379189)
XLA Ops:
  35.6 75.7 %all-gather.13.cloned.1.call-done = bf16[1024,2048]{1,0:T(8,128)(2,1)} async-done(((bf16[256,2048]{1,0:T(8,128)(2,1)}), bf16[1024,2048]{1,0:T(8,128)(2,1)}) %all-gather.13.cloned.1.call-update) | async-done | bytes 4194320 | tf_op jit(solution)/shard_map/all_gather | solution.py:137
  111.3 48.9 %all-gather.15.cloned.1.call-done = bf16[3,2048,512]{2,1,0:T(8,128)(2,1)} async-done(((bf16[3,256,512]{2,1,0:T(8,128)(2,1)}), bf16[3,2048,512]{2,1,0:T(8,128)(2,1)}) %all-gather.15.cloned.1.call-update) | async-done | bytes 6291472 | tf_op jit(solution)/shard_map/all_gather | solution.py:129
  195.0 13.9 %while.26 = (s32[]{:T(128)}, bf16[2,512,8,64]{1,3,2,0:T(8,128)(2,1)}, f32[2,8,512]{2,1,0:T(8,128)S(1)}, bf16[2,512,8,64]{1,3,2,0:T(8,128)(2,1)S(1)}, bf16[2,512,...) while((s32[]{:T(128)}, bf16[2,512,8,64]{1,3,2,0:T(8,128)(2,1)}, ...), condition=%wide.region_5.6_spmd, body=%wide.region_2.5_spmd.sunk | while | flops 562556928 | bytes 36833424 | solution.py:143
  236.6 59.0 %reduce-scatter.9.cloned.1.call-done = bf16[256,2048]{1,0:T(8,128)(2,1)} async-done(((bf16[1024,2048]{1,0:T(8,128)(2,1)}), bf16[256,2048]{1,0:T(8,128)(2,1)}) %reduce-scatter.9.cloned.1.call-update) | async-done | bytes 1048592 | tf_op jit(solution)/shard_map/reduce_scatter | solution.py:101
  302.1 63.9 %all-gather.21.cloned.1.call-done = bf16[2,2048,1408]{2,1,0:T(8,128)(2,1)} async-done(((bf16[2,256,1408]{2,1,0:T(8,128)(2,1)}), bf16[2,2048,1408]{2,1,0:T(8,128)(2,1)}) %all-gather.21.cloned.1.call-update) | async-done | bytes 11534352 | tf_op jit(solution)/shard_map/all_gather | solution.py:150
  366.1 79.9 %all-gather.19.cloned.1.call-done = bf16[1024,2048]{1,0:T(8,128)(2,1)} async-done(((bf16[256,2048]{1,0:T(8,128)(2,1)}), bf16[1024,2048]{1,0:T(8,128)(2,1)}) %all-gather.19.cloned.1.call-update) | async-done | bytes 4194320 | tf_op jit(solution)/shard_map/all_gather | solution.py:157
  446.0 12.3 %fusion.59 = f32[1024,1408]{1,0:T(8,128)} fusion(bf16[1024,2048]{1,0:T(8,128)(2,1)} %all-gather.19.cloned.1.call-done, bf16[2,2048,1408]{2,1,0:T(8,128)(2,1)} %all-gather.21.cloned.1.call-done), kind=kOutput, calls=%fused_computation.81 | convolution fusion | flops 5905580032 | bytes 15728640 | tf_op jit(solution)/shard_map/dot_general | solution.py:159
  466.8 60.2 %all-gather.25.cloned.1.call-done = bf16[1024,2048]{1,0:T(8,128)(2,1)} async-done(((bf16[256,2048]{1,0:T(8,128)(2,1)}), bf16[1024,2048]{1,0:T(8,128)(2,1)}) %all-gather.25.cloned.1.call-update) | async-done | bytes 4194320 | tf_op jit(solution)/shard_map/all_gather | solution.py:173
  527.0 47.9 %all-gather.23.cloned.1.call-done = bf16[1408,2048]{1,0:T(8,128)(2,1)} async-done(((bf16[1408,256]{1,0:T(8,128)(2,1)}), bf16[1408,2048]{1,0:T(8,128)(2,1)}) %all-gather.23.cloned.1.call-update) | async-done | bytes 5767184 | tf_op jit(solution)/shard_map/all_gather | solution.py:151
  574.9 15.7 %multiply_convert_fusion.1 = (bf16[1024,1408]{1,0:T(8,128)(2,1)S(1)}, bf16[1024,1408]{1,0:T(8,128)(2,1)S(1)}, bf16[1024,1408]{1,0:T(8,128)(2,1)}) fusion(f32[1024,1408]{1,0:T(8,128)} %fusion.57, f32[1024,1408]{1,0:T(8,128)} %fusion.59, bf16[1024,2048]{1,0:T(8,128)(2,1)} %all-gather.25.cloned.1.call-done, bf16[1408,2048]{1,0:T(8,128)(2,1)} %all-gather.23.cloned.1.call-done), kind=kOutput, calls=%fused_computation.74 | convolution fusion | flops 5928648704 | bytes 30146560 | tf_op jit(solution)/shard_map/gd,fd->gf/dot_general | solution.py:174
  590.5 10.8 fusion.56
  601.4 11.1 add_convert_fusion
  612.7 76.3 %reduce-scatter.13.cloned.1.call-done = bf16[256,2048]{1,0:T(8,128)(2,1)} async-done(((bf16[1024,2048]{1,0:T(8,128)(2,1)}), bf16[256,2048]{1,0:T(8,128)(2,1)}) %reduce-scatter.13.cloned.1.call-update) | async-done | bytes 1048592 | tf_op jit(solution)/shard_map/reduce_scatter | solution.py:101
  727.7 45.9 %all-gather.27.cloned.1.call-done = bf16[1024,2048]{1,0:T(8,128)(2,1)} async-done(((bf16[256,2048]{1,0:T(8,128)(2,1)}), bf16[1024,2048]{1,0:T(8,128)(2,1)}) %all-gather.27.cloned.1.call-update) | async-done | bytes 4194320 | tf_op jit(solution)/shard_map/all_gather | solution.py:209
  790.8 28.4 %while.27 = (s32[]{:T(128)}, f32[2,512,8,64]{1,3,2,0:T(8,128)}, f32[2,512,8,64]{1,3,2,0:T(8,128)}, bf16[2,512,8,64]{1,3,2,0:T(8,128)(2,1)}, bf16[2,512,8,64]{1,3...) while((s32[]{:T(128)}, f32[2,512,8,64]{1,3,2,0:T(8,128)}, ...), condition=%wide.region_15.16_spmd, body=%wide.region_13.15_spmd.sunk | while | flops 1374416896 | bytes 117036352 | solution.py:216
  842.8 11.0 bitcast_convert_fusion
  853.9 12.4 %convolution_convert_fusion.3 = bf16[1024,2048]{1,0:T(8,128)(2,1)} fusion(bf16[1024,1408]{1,0:T(8,128)(2,1)} %get-tuple-element.251, bf16[1408,2048]{1,0:T(8,128)(2,1)} %all-gather.23.cloned.1.call-done), kind=kOutput, calls=%fused_computation.85 | convolution fusion | flops 5907677184 | bytes 12845056 | tf_op jit(solution)/shard_map/dot_general | solution.py:165
  866.4 10.9 convert_bitcast_fusion
  880.3 47.3 %reduce-scatter.21.cloned.1.call-done = bf16[2,256,1408]{2,1,0:T(8,128)(2,1)} async-done(((bf16[2,2048,1408]{2,1,0:T(8,128)(2,1)}), bf16[2,256,1408]{2,1,0:T(8,128)(2,1)}) %reduce-scatter.21.cloned.1.call-update) | async-done | bytes 1441808 | tf_op jit(solution)/shard_map/reduce_scatter | solution.py:101
  930.8 41.8 %reduce-scatter.19.cloned.1.call-done = bf16[512,256]{1,0:T(8,128)(2,1)} async-done(((bf16[512,2048]{1,0:T(8,128)(2,1)}), bf16[512,256]{1,0:T(8,128)(2,1)}) %reduce-scatter.19.cloned.1.call-update) | async-done | bytes 262160 | tf_op jit(solution)/shard_map/reduce_scatter | solution.py:101
  974.3 77.2 %reduce-scatter.15.cloned.1.call-done = bf16[256,2048]{1,0:T(8,128)(2,1)} async-done(((bf16[1024,2048]{1,0:T(8,128)(2,1)}), bf16[256,2048]{1,0:T(8,128)(2,1)}) %reduce-scatter.15.cloned.1.call-update) | async-done | bytes 1048592 | tf_op jit(solution)/shard_map/reduce_scatter | solution.py:101
  1053.9 45.3 %all-reduce = (f32[2048]{0:T(1024)S(1)}, f32[2048]{0:T(1024)S(1)}, f32[3,4,512]{2,1,0:T(4,128)S(1)}, f32[2048]{0:T(1024)S(1)}, f32[2048]{0:T(1024)S(1)}) all-reduce(f32[2048]{0:T(1024)S(1)} %get-tuple-element.204, f32[2048]{0:T(1024)S(1)} %get-tuple-element.209, ...), channel_id=1, replica_groups=mesh['dp'=8,'tensor'=4] {'dp','tensor'}, use_global_device_ids=true, to_apply=%region_20.21 | all-reduce | flops 14336 | bytes 114688 | tf_op jit(solution)/shard_map/psum | solution.py:248
  1102.4 29.7 %reduce-scatter.11.cloned.1.call-done = bf16[256,2048]{1,0:T(8,128)(2,1)} async-done(((bf16[1024,2048]{1,0:T(8,128)(2,1)}), bf16[256,2048]{1,0:T(8,128)(2,1)}) %reduce-scatter.11.cloned.1.call-update) | async-done | bytes 1048592 | tf_op jit(solution)/shard_map/reduce_scatter | solution.py:101
  1137.1 60.5 %reduce-scatter.17.cloned.1.call-done = bf16[3,256,512]{1,2,0:T(8,128)(2,1)} async-done(((bf16[3,2048,512]{1,2,0:T(8,128)(2,1)}), bf16[3,256,512]{1,2,0:T(8,128)(2,1)}) %reduce-scatter.17.cloned.1.call-update) | async-done | bytes 786448 | tf_op jit(solution)/shard_map/reduce_scatter | solution.py:101
  (287 shorter events, 247.2 us)
Async XLA Ops:
  7.2 104.2 %all-gather.13.cloned.1.call-start = ((), (), s32[]{:S(2)}) async-start(), calls=%async_computation.8 | async-start | bytes 5242880 | tf_op jit(solution)/shard_map/all_gather | solution.py:137
  33.2 127.0 %all-gather.15.cloned.1.call-start = ((), (), s32[]{:S(2)}) async-start(), calls=%async_computation.9 | async-start | bytes 7077888 | tf_op jit(solution)/shard_map/all_gather | solution.py:129
  34.0 178.8 %all-gather.17.cloned.1.call-start = ((), (), s32[]{:S(2)}) async-start(), calls=%async_computation.10 | async-start | bytes 2359296 | tf_op jit(solution)/shard_map/all_gather | solution.py:130
  34.7 260.8 %reduce-scatter.9.cloned.1.call-start = ((), (), s32[]{:S(2)}) async-start(), calls=%async_computation.11 | async-start | bytes 5242880 | tf_op jit(solution)/shard_map/reduce_scatter | solution.py:101
  219.0 147.0 %all-gather.21.cloned.1.call-start = ((), (), s32[]{:S(2)}) async-start(), calls=%async_computation.13 | async-start | bytes 12976128 | tf_op jit(solution)/shard_map/all_gather | solution.py:150
  219.6 226.4 %all-gather.19.cloned.1.call-start = ((), (), s32[]{:S(2)}) async-start(), calls=%async_computation.12 | async-start | bytes 5242880 | tf_op jit(solution)/shard_map/all_gather | solution.py:157
  236.6 455.9 %copy-start.23 = (f32[8,1,256]{2,1,0:T(1,128)}, f32[8,1,256]{2,1,0:T(1,128)S(1)}, u32[]{:S(2)}) copy-start(f32[8,1,256]{2,1,0:T(1,128)S(1)} %convert_element_type.240) | copy-start | bytes 24580
  297.2 395.2 %copy-start.30 = (f32[256]{0:T(256)}, f32[256]{0:T(256)S(1)}, u32[]{:S(2)}) copy-start(f32[256]{0:T(256)S(1)} %broadcast_multiply_fusion.6) | copy-start | bytes 3076
  299.0 393.5 %copy-start.36 = (f32[256]{0:T(256)}, f32[256]{0:T(256)S(1)}, u32[]{:S(2)}) copy-start(f32[256]{0:T(256)S(1)} %add_rsqrt_fusion) | copy-start | bytes 3076
  300.6 226.4 %all-gather.25.cloned.1.call-start = ((), (), s32[]{:S(2)}) async-start(), calls=%async_computation.16 | async-start | bytes 5242880 | tf_op jit(solution)/shard_map/all_gather | solution.py:173
  301.3 273.5 %all-gather.23.cloned.1.call-start = ((), (), s32[]{:S(2)}) async-start(), calls=%async_computation.14 | async-start | bytes 6488064 | tf_op jit(solution)/shard_map/all_gather | solution.py:151
  302.1 386.9 %reduce-scatter.13.cloned.1.call-start = ((), (), s32[]{:S(2)}) async-start(), calls=%async_computation.17 | async-start | bytes 5242880 | tf_op jit(solution)/shard_map/reduce_scatter | solution.py:101
  612.5 161.1 %all-gather.27.cloned.1.call-start = ((), (), s32[]{:S(2)}) async-start(), calls=%async_computation.18 | async-start | bytes 5242880 | tf_op jit(solution)/shard_map/all_gather | solution.py:209
  694.7 182.7 %reduce-scatter.23.cloned.1.call-start = ((), (), s32[]{:S(2)}) async-start(), calls=%async_computation.23 | async-start | bytes 6488064 | tf_op jit(solution)/shard_map/reduce_scatter | solution.py:101
  705.3 222.4 %reduce-scatter.21.cloned.1.call-start = ((), (), s32[]{:S(2)}) async-start(), calls=%async_computation.22 | async-start | bytes 12976128 | tf_op jit(solution)/shard_map/reduce_scatter | solution.py:101
  727.4 245.2 %reduce-scatter.19.cloned.1.call-start = ((), (), s32[]{:S(2)}) async-start(), calls=%async_computation.21 | async-start | bytes 2359296 | tf_op jit(solution)/shard_map/reduce_scatter | solution.py:101
  790.7 260.8 %reduce-scatter.15.cloned.1.call-start = ((), (), s32[]{:S(2)}) async-start(), calls=%async_computation.19 | async-start | bytes 5242880 | tf_op jit(solution)/shard_map/reduce_scatter | solution.py:101
  853.8 278.3 %reduce-scatter.11.cloned.1.call-start = ((), (), s32[]{:S(2)}) async-start(), calls=%async_computation.15 | async-start | bytes 5242880 | tf_op jit(solution)/shard_map/reduce_scatter | solution.py:101
  866.3 331.3 %reduce-scatter.17.cloned.1.call-start = ((), (), s32[]{:S(2)}) async-start(), calls=%async_computation.20 | async-start | bytes 7077888 | tf_op jit(solution)/shard_map/reduce_scatter | solution.py:101
  880.3 251.9 %copy-start.4 = (bf16[256,2048]{1,0:T(8,128)(2,1)S(1)}, bf16[256,2048]{1,0:T(8,128)(2,1)}, u32[]{:S(2)}) copy-start(bf16[256,2048]{1,0:T(8,128)(2,1)} %reduce-scatter.9.cloned.1.call-done) | copy-start | bytes 3145732
  880.3 251.9 %copy-start.9 = (bf16[256,2048]{1,0:T(8,128)(2,1)S(1)}, bf16[256,2048]{1,0:T(8,128)(2,1)}, u32[]{:S(2)}) copy-start(bf16[256,2048]{1,0:T(8,128)(2,1)} %param.25) | copy-start | bytes 3145732
  880.3 251.9 %copy-start.24 = (f32[8,1,256]{2,1,0:T(1,128)S(1)}, f32[8,1,256]{2,1,0:T(1,128)}, u32[]{:S(2)}) copy-start(f32[8,1,256]{2,1,0:T(1,128)} %copy-done.23) | copy-start | bytes 24580
  880.3 251.8 %copy-start.31 = (f32[256]{0:T(256)S(1)}, f32[256]{0:T(256)}, u32[]{:S(2)}) copy-start(f32[256]{0:T(256)} %copy-done.30) | copy-start | bytes 3076
  880.3 251.8 %copy-start.37 = (f32[256]{0:T(256)S(1)}, f32[256]{0:T(256)}, u32[]{:S(2)}) copy-start(f32[256]{0:T(256)} %copy-done.36) | copy-start | bytes 3076
  (54 other events, 1978.6 us)
Sparse Core Ops, SparseCore 0:
  33.4 77.9 all-gather.12
  113.2 46.9 all-gather.14
  162.2 28.1 all-gather.16
  219.2 76.3 reduce-scatter.8
  297.5 68.5 all-gather.20
  368.1 77.8 all-gather.18
  447.6 79.2 all-gather.24
  529.0 45.8 all-gather.22
  612.6 76.3 reduce-scatter.12
  694.8 78.6 all-gather.26
  777.0 60.1 reduce-scatter.22
  840.9 86.7 reduce-scatter.20
  931.3 41.2 reduce-scatter.18
  974.7 76.7 reduce-scatter.14
  1053.8 78.3 reduce-scatter.10
  1135.4 62.1 reduce-scatter.16

commit v2 on v1

--- a/solution.py
+++ b/solution.py
@@ -55,18 +55,18 @@
     )
 
 
-def causal_scores(queries, key_rows):
+def causal_scores(queries, key_rows, positions):
     scaling = 1.0 / math.sqrt(HD)
     scores = scaling * jnp.einsum(
         "qhd,khd->hqk", queries, key_rows, preferred_element_type=jnp.float32
     )
-    causal = jnp.arange(SEQ_LEN)[:, None] >= jnp.arange(SEQ_LEN)[None, :]
+    causal = positions[:, None] >= positions[None, :]
     return jnp.where(causal[None], scores, NEGATIVE)
 
 
-def attend_forward(pieces):
+def attend_forward(pieces, positions):
     queries, key_rows, value_rows = pieces
-    scores = causal_scores(queries, key_rows)
+    scores = causal_scores(queries, key_rows, positions)
     row_top = jnp.max(scores, axis=-1, keepdims=True)
     exponent = jnp.exp(scores - row_top)
     totals = jnp.sum(exponent, axis=-1, keepdims=True)
@@ -75,10 +75,10 @@
     return (mixed.astype(jnp.bfloat16), (row_top + jnp.log(totals))[..., 0])
 
 
-def attend_back(pieces):
+def attend_back(pieces, positions):
     queries, key_rows, value_rows, grad_mixed, log_totals = pieces
     scaling = 1.0 / math.sqrt(HD)
-    scores = causal_scores(queries, key_rows)
+    scores = causal_scores(queries, key_rows, positions)
     weights = jnp.exp(scores - log_totals[..., None])
     grad_values = jnp.einsum(
         "hqk,qhd->khd", weights.astype(jnp.bfloat16), grad_mixed, preferred_element_type=jnp.float32
@@ -125,6 +125,7 @@
     local_heads = head_width // HD
     head_shape = (sequences, SEQ_LEN, local_heads, HD)
     cosine, sine = angle_tables()
+    positions = jnp.arange(SEQ_LEN)
     proj_full, out_full, gain_one, shift_one = (
         lax.all_gather(projections, "dp", axis=1, tiled=True),
         lax.all_gather(output_weight, "dp", axis=1, tiled=True),
@@ -140,7 +141,9 @@
     queries = rotate(pre_all[0].reshape(head_shape), cosine, sine, 1.0).astype(jnp.bfloat16)
     key_rows = rotate(pre_all[1].reshape(head_shape), cosine, sine, 1.0).astype(jnp.bfloat16)
     value_rows = pre_all[2].reshape(head_shape).astype(jnp.bfloat16)
-    mixed, log_totals = lax.map(attend_forward, (queries, key_rows, value_rows))
+    mixed, log_totals = lax.map(
+        lambda pieces: attend_forward(pieces, positions), (queries, key_rows, value_rows)
+    )
     mixed_rows = mixed.reshape(group_rows, head_width)
     part = mixed_rows
     middle = residual + scatter_sum(
@@ -214,7 +217,8 @@
         "gd,ed->ge", gathered_branch, out_back, preferred_element_type=jnp.float32
     ).astype(jnp.bfloat16)
     grad_queries, grad_keys, grad_values = lax.map(
-        attend_back, (queries, key_rows, value_rows, grad_mixed.reshape(head_shape), log_totals)
+        lambda pieces: attend_back(pieces, positions),
+        (queries, key_rows, value_rows, grad_mixed.reshape(head_shape), log_totals),
     )
     grad_queries = rotate(grad_queries, cosine, sine, -1.0)
     grad_keys = rotate(grad_keys, cosine, sine, -1.0)
@@ -273,9 +277,322 @@
     )
 
 
+def swap(array, dp_bit, tensor_bit):
+    dp_ways, tensor_ways = lax.axis_size("dp"), lax.axis_size("tensor")
+    pairs = [
+        (d * tensor_ways + t, (d ^ dp_bit) * tensor_ways + (t ^ tensor_bit))
+        for d in range(dp_ways)
+        for t in range(tensor_ways)
+    ]
+    return lax.ppermute(array, ("dp", "tensor"), pairs)
+
+
+def send_between(array, routes):
+    tensor_ways = lax.axis_size("tensor")
+    pairs = [(d * tensor_ways + t, e * tensor_ways + s) for (d, t), (e, s) in routes]
+    return lax.ppermute(array, ("dp", "tensor"), pairs)
+
+
+CORE, X_BIT, Y_BIT = 1, 2, 4
+
+
+def places():
+    return [(d, t) for d in range(lax.axis_size("dp")) for t in range(lax.axis_size("tensor"))]
+
+
+def own_quarter(array):
+    return send_between(
+        array,
+        [((d, t), (d ^ 1, t) if d & 1 else (d ^ 1, t ^ 2)) for d, t in places()],
+    )
+
+
+def far_quarter(array):
+    return send_between(array, [((d, t), (d, t ^ 2)) for d, t in places() if d & 1])
+
+
+def quarter_home(array):
+    return send_between(
+        array,
+        [((d ^ 1, t) if d & 1 else (d ^ 1, t ^ 2), (d, t)) for d, t in places()],
+    )
+
+
+def gather_weight(shard, axis, first_core):
+    near = own_quarter(shard)
+    far = far_quarter(shard)
+    even = jnp.where(first_core, shard, near)
+    odd = jnp.where(first_core, near, far)
+    even_x, odd_y = swap(even, X_BIT, 0), swap(odd, Y_BIT, 0)
+    even_y, odd_x = swap(even, Y_BIT, 0), swap(odd, X_BIT, 0)
+    even_xy, odd_xy = swap(even_x, Y_BIT, 0), swap(odd_y, X_BIT, 0)
+    return jnp.concatenate([even_y, even_xy, odd_x, odd_xy, even, even_x, odd, odd_y], axis=axis)
+
+
+def scatter_weight(part, axis, first_core):
+    send_even = part(0).astype(jnp.bfloat16)
+    got_even = swap(send_even, Y_BIT, 0)
+    send_odd = part(1).astype(jnp.bfloat16)
+    got_odd = swap(send_odd, X_BIT, 0)
+    keep_even = part(2).astype(jnp.bfloat16)
+    keep_odd = part(3).astype(jnp.bfloat16)
+
+    def halves(array):
+        return [h.astype(jnp.float32) for h in jnp.split(array, 2, axis=axis)]
+
+    even_here, even_there = [a + b for a, b in zip(halves(keep_even), halves(got_even))]
+    odd_here, odd_there = [a + b for a, b in zip(halves(keep_odd), halves(got_odd))]
+    even_last = swap(even_there.astype(jnp.bfloat16), X_BIT, 0)
+    odd_last = swap(odd_there.astype(jnp.bfloat16), Y_BIT, 0)
+    even_sum = even_here + even_last.astype(jnp.float32)
+    odd_sum = odd_here + odd_last.astype(jnp.float32)
+    return home_sum(even_sum, odd_sum, first_core)
+
+
+def home_sum(even_sum, odd_sum, first_core):
+    odd_out = odd_sum.astype(jnp.bfloat16)
+    crossing = quarter_home(jnp.where(first_core, odd_out, even_sum.astype(jnp.bfloat16)))
+    far = far_quarter(odd_out)
+    return jnp.where(first_core, even_sum, far.astype(jnp.float32)) + crossing.astype(jnp.float32)
+
+
+def gather_rows(own):
+    beside = swap(own, 0, 1)
+    sibling = swap(own, CORE, 0)
+    return jnp.concatenate([own, beside, sibling, swap(beside, CORE, 0)], axis=0)
+
+
+def scatter_rows(product, rows):
+    count = rows // 4
+    far = product(slice(2 * count, rows)).astype(jnp.bfloat16)
+    got = swap(far, CORE, 0).astype(jnp.float32)
+    near = product(slice(0, 2 * count))
+    beside = (near[count:] + got[count:]).astype(jnp.bfloat16)
+    return near[:count] + got[:count] + swap(beside, 0, 1).astype(jnp.float32)
+
+
+ORDER = ((1, 0, 0), (1, 1, 0), (0, 1, 1), (1, 1, 1), (0, 0, 0), (0, 1, 0), (0, 0, 1), (1, 0, 1))
+
+
+def flip(array, y_here, x_here, axis):
+    array = jnp.where(x_here, jnp.flip(array, axis + 1), array)
+    return jnp.where(y_here, jnp.flip(array, axis), array)
+
+
+def to_local(array, y_here, x_here):
+    lead, width = array.shape[:-1], array.shape[-1]
+    k = len(lead)
+    blocks = flip(array.reshape(*lead, 2, 2, 2, width // 8), y_here, x_here, k)
+    return jnp.concatenate([blocks[..., a, b, c, :] for a, b, c in ORDER], axis=-1)
+
+
+def from_local(array, y_here, x_here):
+    lead, width = array.shape[:-1], array.shape[-1]
+    pieces = dict(zip(ORDER, jnp.split(array, 8, axis=-1)))
+    natural = jnp.concatenate([pieces[key] for key in sorted(pieces)], axis=-1)
+    blocks = flip(natural.reshape(*lead, 2, 2, 2, width // 8), y_here, x_here, len(lead))
+    return blocks.reshape(*lead, width)
+
+
+def local_pairs(
+    inputs,
+    gain_first,
+    shift_first,
+    projections,
+    biases,
+    output_weight,
+    gain_second,
+    shift_second,
+    gate_up,
+    down_weight,
+    cotangent,
+):
+    dp_index, tensor_index = lax.axis_index("dp"), lax.axis_index("tensor")
+    first_core = dp_index % 2 == 0
+    x_here = (dp_index // 2) % 2 == 1
+    y_here = dp_index // 4 == 1
+    late_half = tensor_index % 2 == 1
+    row_count, model_width = inputs.shape
+    group_rows = 4 * row_count
+    head_width = output_weight.shape[0]
+    local_heads = head_width // HD
+    head_shape = (2, SEQ_LEN, local_heads, HD)
+    quarter_width = model_width // 4
+
+    def width_part(array, k):
+        return array[:, k * quarter_width : (k + 1) * quarter_width]
+
+    positions = jnp.arange(SEQ_LEN)
+    positions = jnp.where(late_half, (positions + SEQ_LEN // 2) % SEQ_LEN, positions)
+    cosine, sine = (
+        jnp.where(late_half, jnp.roll(table, SEQ_LEN // 2, axis=0), table)
+        for table in angle_tables()
+    )
+    vectors = lax.all_gather(
+        jnp.stack([gain_first, shift_first, gain_second, shift_second]), "dp", axis=1, tiled=True
+    )
+    gain_one, shift_one, gain_two, shift_two = to_local(
+        vectors.astype(jnp.float32), y_here, x_here
+    )
+    far_biases = own_quarter(biases)
+    quarter_biases = jnp.where(first_core, biases, far_biases).astype(jnp.float32)
+
+    proj_full = gather_weight(projections, 1, first_core)
+    residual = to_local(inputs, y_here, x_here).astype(jnp.float32)
+    normed_one, unit_one, inverse_one = norm_rows(residual, gain_one, shift_one)
+    gathered_one = gather_rows(normed_one.astype(jnp.bfloat16))
+    own_cot = to_local(cotangent, y_here, x_here)
+    gathered_cot = gather_rows(own_cot)
+    out_full = gather_weight(output_weight, 1, first_core)
+    gu_full = gather_weight(gate_up, 1, first_core)
+    down_full = gather_weight(down_weight, 1, first_core)
+
+    pre_all = jnp.einsum("gd,jde->jge", gathered_one, proj_full, preferred_element_type=jnp.float32)
+    pre_all = pre_all + quarter_biases[:, None, :]
+    queries = rotate(pre_all[0].reshape(head_shape), cosine, sine, 1.0).astype(jnp.bfloat16)
+    key_rows = rotate(pre_all[1].reshape(head_shape), cosine, sine, 1.0).astype(jnp.bfloat16)
+    value_rows = pre_all[2].reshape(head_shape).astype(jnp.bfloat16)
+    mixed, log_totals = lax.map(
+        lambda pieces: attend_forward(pieces, positions), (queries, key_rows, value_rows)
+    )
+    mixed_rows = mixed.reshape(group_rows, head_width)
+    middle = residual + scatter_rows(
+        lambda rows: jnp.dot(mixed_rows[rows], out_full, preferred_element_type=jnp.float32),
+        group_rows,
+    )
+    normed_two, unit_two, inverse_two = norm_rows(middle, gain_two, shift_two)
+    gathered_two = gather_rows(normed_two.astype(jnp.bfloat16))
+    gate_act = jnp.dot(gathered_two, gu_full[0], preferred_element_type=jnp.float32)
+    up_act = jnp.dot(gathered_two, gu_full[1], preferred_element_type=jnp.float32)
+    sigmoid_gate = jax.nn.sigmoid(gate_act)
+    hidden = (gate_act * sigmoid_gate * up_act).astype(jnp.bfloat16)
+
+    down_owned = scatter_weight(
+        lambda k: jnp.einsum(
+            "gf,gd->fd", hidden, width_part(gathered_cot, k), preferred_element_type=jnp.float32
+        ),
+        1,
+        first_core,
+    )
+    grad_hidden = jnp.einsum(
+        "gd,fd->gf", gathered_cot, down_full, preferred_element_type=jnp.float32
+    )
+    grad_up = (grad_hidden * gate_act * sigmoid_gate).astype(jnp.bfloat16)
+    grad_gate = (
+        grad_hidden * up_act * sigmoid_gate * (1.0 + gate_act * (1.0 - sigmoid_gate))
+    ).astype(jnp.bfloat16)
+    grad_second = scatter_rows(
+        lambda rows: jnp.einsum(
+            "gf,df->gd", grad_gate[rows], gu_full[0], preferred_element_type=jnp.float32
+        )
+        + jnp.einsum("gf,df->gd", grad_up[rows], gu_full[1], preferred_element_type=jnp.float32),
+        group_rows,
+    )
+    gate_owned, up_owned = (
+        scatter_weight(
+            lambda k: jnp.einsum(
+                "gd,gf->df",
+                width_part(gathered_two, k),
+                incoming,
+                preferred_element_type=jnp.float32,
+            ),
+            0,
+            first_core,
+        )
+        for incoming in (grad_gate, grad_up)
+    )
+    outputs = middle + scatter_rows(
+        lambda rows: jnp.dot(hidden[rows], down_full, preferred_element_type=jnp.float32),
+        group_rows,
+    )
+    outputs = from_local(outputs.astype(jnp.bfloat16), y_here, x_here)
+
+    grad_mid_norm, gain_two_part, shift_two_part = norm_back(
+        grad_second, unit_two, inverse_two, gain_two
+    )
+    grad_middle = own_cot.astype(jnp.float32) + grad_mid_norm
+    gathered_branch = gather_rows(grad_middle.astype(jnp.bfloat16))
+    grad_mixed = jnp.einsum(
+        "gd,ed->ge", gathered_branch, out_full, preferred_element_type=jnp.float32
+    ).astype(jnp.bfloat16)
+    out_owned = scatter_weight(
+        lambda k: jnp.einsum(
+            "ge,gd->ed",
+            mixed_rows,
+            width_part(gathered_branch, k),
+            preferred_element_type=jnp.float32,
+        ),
+        1,
+        first_core,
+    )
+    grad_queries, grad_keys, grad_values = lax.map(
+        lambda pieces: attend_back(pieces, positions),
+        (queries, key_rows, value_rows, grad_mixed.reshape(head_shape), log_totals),
+    )
+    grad_queries = rotate(grad_queries, cosine, sine, -1.0)
+    grad_keys = rotate(grad_keys, cosine, sine, -1.0)
+    grad_pre = (
+        jnp.stack([grad_queries, grad_keys, grad_values])
+        .reshape(3, group_rows, head_width)
+        .astype(jnp.bfloat16)
+    )
+    proj_owned = scatter_weight(
+        lambda k: jnp.einsum(
+            "gd,jge->jde",
+            width_part(gathered_one, k),
+            grad_pre,
+            preferred_element_type=jnp.float32,
+        ),
+        1,
+        first_core,
+    )
+    grad_normed = scatter_rows(
+        lambda rows: jnp.einsum(
+            "jge,jde->gd", grad_pre[:, rows], proj_full, preferred_element_type=jnp.float32
+        ),
+        group_rows,
+    )
+    bias_part = jnp.sum(grad_pre, axis=1, dtype=jnp.float32)
+    bias_part = bias_part + swap(bias_part, X_BIT, 0)
+    bias_part = bias_part + swap(bias_part, Y_BIT, 0)
+    bias_grad = quarter_home(bias_part) + jnp.where(
+        first_core, bias_part, far_quarter(bias_part)
+    )
+
+    grad_in_norm, gain_one_part, shift_one_part = norm_back(
+        grad_normed, unit_one, inverse_one, gain_one
+    )
+    input_grads = from_local(grad_middle + grad_in_norm, y_here, x_here)
+
+    sums = from_local(
+        jnp.stack([gain_one_part, shift_one_part, gain_two_part, shift_two_part]), y_here, x_here
+    )
+    sums = flip(sums.reshape(4, 2, 2, 2, model_width // 8), y_here, x_here, 1)
+    sums = sums[:, 0] + swap(sums[:, 1], Y_BIT, 0)
+    sums = sums[:, 0] + swap(sums[:, 1], X_BIT, 0)
+    sums = sums + swap(sums, 0, 1)
+    sums = sums + swap(sums, 0, 2)
+    sums = sums + swap(sums, CORE, 0)
+    sums = jnp.where(first_core, sums[:, 0], sums[:, 1])
+    return (
+        outputs,
+        input_grads,
+        sums[0],
+        sums[1],
+        proj_owned,
+        bias_grad,
+        out_owned,
+        sums[2],
+        sums[3],
+        jnp.stack([gate_owned, up_owned]),
+        down_owned,
+    )
+
+
 def solution(mesh):
+    whole_pairs = dict(mesh.shape) == {"dp": 8, "tensor": 4}
     return jax.shard_map(
-        local,
+        local_pairs if whole_pairs else local,
         mesh=mesh,
         in_specs=(
             P(("dp", "tensor"), None),

time: 1220 us -> 989 us (0.81)
  waiting for transfers between devices: 818 us -> 397 us
  starting transfers between devices: 1.03 us -> 158 us
  local copies, waits for them, and re-layouts: 64.8 us -> 134 us
  blocking collectives: 80.4 us -> 11.4 us
  other arithmetic: 53.3 us -> 86.5 us
  matrix products: 174 us -> 187 us
    all_gather x8 -> x0, waiting for transfers between devices: 422 us -> none  [the longest x1 79.9 us: local(): lax.all_gather(normed_two.astype(jnp.bfloat16), 'tensor', axis=0, tiled=T...]
    ppermute x0 -> x92, waiting for transfers between devices: none -> 397 us  [the longest x71 311 us: swap(): return lax.ppermute(array, ('dp', 'tensor'), pairs)]
    reduce_scatter x8 -> x0, waiting for transfers between devices: 392 us -> none  [scatter_sum(): lax.psum_scatter(terms.astype(jnp.bfloat16), axis, scatter_dimension=dime...]
    ppermute x0 -> x92, starting transfers between devices: none -> 158 us  [the longest x21 83.7 us: send_between(): return lax.ppermute(array, ('dp', 'tensor'), pairs)]
    unnamed x100 -> x265, local copies, waits for them, and re-layouts: 8.62 us -> 70.7 us
    psum x1 -> x0, blocking collectives: 45.3 us -> none  [local(): lax.psum((gain_one_part, shift_one_part, gain_two_part, shift_two_part, s...]
    all_gather x4 -> x1, blocking collectives: 35.1 us -> 11.4 us  [local_pairs(): lax.all_gather(jnp.stack([gain_first, shift_first, gain_second, shift_sec...]
    select_n x0 -> x28, other arithmetic: none -> 20.4 us  [the longest x5 10.3 us: home_sum(): jnp.where(first_core, odd_out, even_sum.astype(jnp.bfloat16))]
  transfers between devices with their start and end apart: 16 -> 92, of which waited for: 14 -> 41; matrix products, arithmetic and copies ran while one was open for 19% -> 23% of each run, Pallas kernels for 0% -> 0%
where the time goes in v2:
time: 989 us; the launch traced here: 979 us
  waiting for transfers between devices  397 us (40%)
  matrix products  187 us (19%)
  starting transfers between devices  158 us (16%)
  local copies, waits for them, and re-layouts  134 us (14%)
  other arithmetic  86.5 us (9%)
  blocking collectives  11.4 us (1%)
    ppermute x71, waiting for transfers between devices, swap(): return lax.ppermute(array, ('dp', 'tensor'), pairs)  311 us
    ppermute x21, waiting for transfers between devices, send_between(): return lax.ppermute(array, ('dp', 'tensor'), pairs)  86.5 us
    ppermute x21, starting transfers between devices, send_between(): return lax.ppermute(array, ('dp', 'tensor'), pairs)  83.7 us
    ppermute x71, starting transfers between devices, swap(): return lax.ppermute(array, ('dp', 'tensor'), pairs)  74.5 us
    unnamed x265, local copies, waits for them, and re-layouts  70.7 us
    dot_general x8, matrix products, local_pairs(): jnp.einsum('gd,gf->df', width_part(gathered_two, k), incoming, preferred_...  20.1 us
  transfers between devices with their start and end apart: 92, of which 41 were waited for; matrix products, arithmetic and copies ran while one was open for 23% of the time, Pallas kernels for 0%

profile of v2, /device:TPU:9, one launch (start us, length us, event | category | flops | bytes accessed | tf_op | source)
XLA Modules:
  0.0 978.8 jit_solution(2216160918758530652)
XLA Ops:
  13.9 11.4 %all_gather.3 = bf16[4,2048]{1,0:T(4,128)(2,1)S(1)} all-gather(bf16[4,256]{1,0:T(4,128)(2,1)S(1)} %pad_maximum_fusion.10), channel_id=1, replica_groups=mesh['dp'=8,'tensor'=4] {'dp'}, dimensions={1}, use_global_device_ids=true | all-gather | bytes 18432 | tf_op jit(solution)/shard_map/all_gather | solution.py:431
  37.8 17.4 %collective-permute-start = (bf16[3,256,512]{1,2,0:T(8,128)(2,1)}, bf16[3,256,512]{1,2,0:T(8,128)(2,1)}, u32[]{:S(2)}, u32[]{:S(2)}) collective-permute-start(bf16[3,256,512]{1,2,0:T(8,128)(2,1)} %copy.69), channel_id=1, source_target_pairs={{0,6},{1,7},{2,4},{3,5},{4,0},{5,1},{6,2},{7,3},{8,14},{9,15},{10,... | collective-permute-start | bytes 2359304 | tf_op jit(solution)/shard_map/ppermute | solution.py:293
  75.2 10.2 %collective-permute-start.29 = (bf16[2,256,1408]{2,1,0:T(8,128)(2,1)}, bf16[2,256,1408]{2,1,0:T(8,128)(2,1)S(1)}, u32[]{:S(2)}, u32[]{:S(2)}) collective-permute-start(bf16[2,256,1408]{2,1,0:T(8,128)(2,1)} %param.23), channel_id=1, source_target_pairs={{4,6},{5,7},{6,4},{7,5},{12,14},{13,15},{14,12},{15,13},{20,22},{2... | collective-permute-start | bytes 4325384 | tf_op jit(solution)/shard_map/ppermute | solution.py:293
  89.0 20.2 %collective-permute-done.43 = bf16[256,2048]{1,0:T(8,128)(2,1)S(1)} collective-permute-done((bf16[256,2048]{1,0:T(8,128)(2,1)S(1)}, bf16[256,2048]{1,0:T(8,128)(2,1)S(1)}, u32[]{:S(2)}, u32[]{:S(2)}) %collective-permute-start.43) | collective-permute-done | bytes 1048608 | tf_op jit(solution)/shard_map/ppermute | solution.py:287
  116.9 31.7 %collective-permute-done.8 = bf16[256,2048]{1,0:T(8,128)(2,1)S(1)} collective-permute-done((bf16[256,2048]{1,0:T(8,128)(2,1)S(1)}, bf16[256,2048]{1,0:T(8,128)(2,1)S(1)}, u32[]{:S(2)}, u32[]{:S(2)}) %collective-permute-start.8) | collective-permute-done | bytes 1048608 | tf_op jit(solution)/shard_map/ppermute | solution.py:287
  154.8 14.4 %collective-permute-done.1 = bf16[3,256,512]{1,2,0:T(8,128)(2,1)S(1)} collective-permute-done((bf16[3,256,512]{1,2,0:T(8,128)(2,1)S(1)}, bf16[3,256,512]{1,2,0:T(8,128)(2,1)S(1)}, u32[]{:S(2)}, u32[]{:S(2)}) %collective-permute-start.1) | collective-permute-done | bytes 786464 | tf_op jit(solution)/shard_map/ppermute | solution.py:287
  172.7 13.5 %collective-permute-done.6 = bf16[3,256,512]{1,2,0:T(8,128)(2,1)S(1)} collective-permute-done((bf16[3,256,512]{1,2,0:T(8,128)(2,1)S(1)}, bf16[3,256,512]{1,2,0:T(8,128)(2,1)S(1)}, u32[]{:S(2)}, u32[]{:S(2)}) %collective-permute-start.6) | collective-permute-done | bytes 786464 | tf_op jit(solution)/shard_map/ppermute | solution.py:287
  193.7 9.3 collective-permute-done.3
  207.7 10.8 %collective-permute-done.39 = bf16[1408,256]{1,0:T(8,128)(2,1)} collective-permute-done((bf16[1408,256]{1,0:T(8,128)(2,1)}, bf16[1408,256]{1,0:T(8,128)(2,1)}, u32[]{:S(2)}, u32[]{:S(2)}) %collective-permute-start.39) | collective-permute-done | bytes 720928 | tf_op jit(solution)/shard_map/ppermute | solution.py:287
  228.3 9.5 add_bitcast_fusion
  263.6 13.8 %while.28 = (s32[]{:T(128)}, bf16[2,512,8,64]{1,3,2,0:T(8,128)(2,1)}, f32[2,8,512]{2,1,0:T(8,128)S(1)}, bf16[2,512,8,64]{1,3,2,0:T(8,128)(2,1)}, bf16[2,512,8,64...) while((s32[]{:T(128)}, ...), condition=%wide.region_5.6_spmd.clone, body=%wide.region_2.5_spmd.clone.sunk | while | flops 562563584 | bytes 32643188 | solution.py:455
  305.4 13.8 %fusion.138 = f32[1024,1408]{1,0:T(8,128)} fusion(bf16[1408,2048]{1,0:T(8,128)(2,1)} %constant_dynamic-update-slice_fusion.40, bf16[256,2048]{1,0:T(8,128)(2,1)S(1)} %copy-done.54, bf16[256,2048]{1,0:T(8,128)(2,1)S(1)} %copy-done.52, bf16[256,2048]{1,0:T(8,128)(2,1)S(1)} %copy-done.50, bf16[256,2048]{1,0:T(8,128)(2,1)S(1)} %copy-done.13), kind=kOutput, calls=%fused_computation.403 | convolution fusion | flops 5922357248 | bytes 15728640 | tf_op jit(solution)/shard_map/gd,fd->gf/dot_general | solution.py:477
  332.5 22.6 %collective-permute-done.28 = bf16[2,256,1408]{2,1,0:T(8,128)(2,1)S(1)} collective-permute-done((bf16[2,256,1408]{2,1,0:T(8,128)(2,1)}, bf16[2,256,1408]{2,1,0:T(8,128)(2,1)S(1)}, u32[]{:S(2)}, u32[]{:S(2)}) %collective-permute-start.28) | collective-permute-done | bytes 1441824 | tf_op jit(solution)/shard_map/ppermute | solution.py:287
  368.4 11.6 %fusion.67 = f32[1024,1408]{1,0:T(8,128)} fusion(bf16[2,2048,1408]{2,1,0:T(8,128)(2,1)S(1)} %constant_dynamic-update-slice_fusion.32, bf16[256,2048]{1,0:T(8,128)(2,1)S(1)} %collective-permute-done.24, bf16[256,2048]{1,0:T(8,128)(2,1)S(1)} %collective-permute-done.23, bf16[256,2048]{1,0:T(8,128)(2,1)S(1)} %collective-permute-done.22, ...), kind=kOutput, calls=%fused_computation.86 | convolution fusion | flops 5922357248 | bytes 15728640 | tf_op jit(solution)/shard_map/dot_general | solution.py:466
  380.0 17.4 %multiply_convert_fusion.2 = (bf16[1024,1408]{1,0:T(8,128)(2,1)}, bf16[1024,1408]{1,0:T(8,128)(2,1)}, bf16[1024,1408]{1,0:T(8,128)(2,1)}) fusion(f32[1024,1408]{1,0:T(8,128)} %fusion.138, f32[1024,1408]{1,0:T(8,128)} %fusion.67, bf16[2,2048,1408]{2,1,0:T(8,128)(2,1)} %copy-done.67, bf16[256,2048]{1,0:T(8,128)(2,1)} %copy-done.57, ...), kind=kOutput, calls=%fused_computation.78 | convolution fusion | flops 5945425920 | bytes 30146560 | tf_op jit(solution)/shard_map/dot_general | solution.py:465
  484.3 25.7 %collective-permute-done.76 = bf16[512,1408]{1,0:T(8,128)(2,1)} collective-permute-done((bf16[512,1408]{1,0:T(8,128)(2,1)}, bf16[512,1408]{1,0:T(8,128)(2,1)}, u32[]{:S(2)}, u32[]{:S(2)}) %collective-permute-start.76) | collective-permute-done | bytes 1441824 | tf_op jit(solution)/shard_map/ppermute | solution.py:287
  516.5 24.4 %collective-permute-done.82 = bf16[512,1408]{1,0:T(8,128)(2,1)} collective-permute-done((bf16[512,1408]{1,0:T(8,128)(2,1)}, bf16[512,1408]{1,0:T(8,128)(2,1)}, u32[]{:S(2)}, u32[]{:S(2)}) %collective-permute-start.82) | collective-permute-done | bytes 1441824 | tf_op jit(solution)/shard_map/ppermute | solution.py:287
  560.8 11.8 %collective-permute-done.77 = bf16[256,1408]{1,0:T(8,128)(2,1)S(1)} collective-permute-done((bf16[256,1408]{1,0:T(8,128)(2,1)}, bf16[256,1408]{1,0:T(8,128)(2,1)S(1)}, u32[]{:S(2)}, u32[]{:S(2)}) %collective-permute-start.77) | collective-permute-done | bytes 720928 | tf_op jit(solution)/shard_map/ppermute | solution.py:287
  597.6 20.8 %collective-permute-done.90 = bf16[1408,256]{1,0:T(8,128)(2,1)S(1)} collective-permute-done((bf16[1408,256]{1,0:T(8,128)(2,1)S(1)}, bf16[1408,256]{1,0:T(8,128)(2,1)S(1)}, u32[]{:S(2)}, u32[]{:S(2)}) %collective-permute-start.90) | collective-permute-done | bytes 720928 | tf_op jit(solution)/shard_map/ppermute | solution.py:293
  623.1 18.5 %collective-permute-done.91 = bf16[1408,256]{1,0:T(8,128)(2,1)S(1)} collective-permute-done((bf16[1408,256]{1,0:T(8,128)(2,1)S(1)}, bf16[1408,256]{1,0:T(8,128)(2,1)S(1)}, u32[]{:S(2)}, u32[]{:S(2)}) %collective-permute-start.91) | collective-permute-done | bytes 720928 | tf_op jit(solution)/shard_map/ppermute | solution.py:293
  672.9 20.7 %collective-permute-done.47 = bf16[256,2048]{1,0:T(8,128)(2,1)S(1)} collective-permute-done((bf16[256,2048]{1,0:T(8,128)(2,1)S(1)}, bf16[256,2048]{1,0:T(8,128)(2,1)S(1)}, u32[]{:S(2)}, u32[]{:S(2)}) %collective-permute-start.47) | collective-permute-done | bytes 1048608 | tf_op jit(solution)/shard_map/ppermute | solution.py:287
  703.9 20.8 %collective-permute-done.48 = bf16[256,2048]{1,0:T(8,128)(2,1)} collective-permute-done((bf16[256,2048]{1,0:T(8,128)(2,1)S(1)}, bf16[256,2048]{1,0:T(8,128)(2,1)}, u32[]{:S(2)}, u32[]{:S(2)}) %collective-permute-start.48) | collective-permute-done | bytes 1048608 | tf_op jit(solution)/shard_map/ppermute | solution.py:287
  743.0 29.1 %while.29 = (s32[]{:T(128)}, f32[2,512,8,64]{1,3,2,0:T(8,128)}, f32[2,512,8,64]{1,3,2,0:T(8,128)}, bf16[2,512,8,64]{1,3,2,0:T(8,128)(2,1)}, bf16[2,512,8,64]{1,3...) while((s32[]{:T(128)}, f32[2,512,8,64]{1,3,2,0:T(8,128)}, ...), condition=%wide.region_12.13_spmd.clone, body=%wide.region_10.12_spmd.clone.sunk | while | flops 1374423552 | bytes 108651784 | solution.py:528
  838.3 31.4 %collective-permute-done.65 = f32[3,512]{1,0:T(4,128)S(1)} collective-permute-done((f32[3,512]{1,0:T(4,128)S(1)}, f32[3,512]{1,0:T(4,128)S(1)}, u32[]{:S(2)}, u32[]{:S(2)}) %collective-permute-start.65) | collective-permute-done | bytes 6176 | tf_op jit(solution)/shard_map/ppermute | solution.py:287
  (667 shorter events, 586.8 us)
Async XLA Ops:
  5.6 59.3 %collective-permute-start.33 = (bf16[1408,256]{1,0:T(8,128)(2,1)}, bf16[1408,256]{1,0:T(8,128)(2,1)}, u32[]{:S(2)}, u32[]{:S(2)}) collective-permute-start(bf16[1408,256]{1,0:T(8,128)(2,1)} %param.24), channel_id=1, source_target_pairs={{0,6},{1,7},{2,4},{3,5},{4,0},{5,1},{6,2},{7,3},{8,14},{9,15},{10,... | collective-permute-start | bytes 2162696 | tf_op jit(solution)/shard_map/ppermute | solution.py:293
  5.7 60.6 %collective-permute-start.37 = (bf16[1408,256]{1,0:T(8,128)(2,1)}, bf16[1408,256]{1,0:T(8,128)(2,1)}, u32[]{:S(2)}, u32[]{:S(2)}) collective-permute-start(bf16[1408,256]{1,0:T(8,128)(2,1)} %param.24), channel_id=1, source_target_pairs={{4,6},{5,7},{6,4},{7,5},{12,14},{13,15},{14,12},{15,13},{20,22},{2... | collective-permute-start | bytes 2162696 | tf_op jit(solution)/shard_map/ppermute | solution.py:293
  73.9 76.1 %collective-permute-start.25 = (bf16[2,256,1408]{2,1,0:T(8,128)(2,1)}, bf16[2,256,1408]{2,1,0:T(8,128)(2,1)S(1)}, u32[]{:S(2)}, u32[]{:S(2)}) collective-permute-start(bf16[2,256,1408]{2,1,0:T(8,128)(2,1)} %param.23), channel_id=1, source_target_pairs={{0,6},{1,7},{2,4},{3,5},{4,0},{5,1},{6,2},{7,3},{8,14},{9,15},{10,... | collective-permute-start | bytes 4325384 | tf_op jit(solution)/shard_map/ppermute | solution.py:293
  75.2 76.1 %collective-permute-start.29 = (bf16[2,256,1408]{2,1,0:T(8,128)(2,1)}, bf16[2,256,1408]{2,1,0:T(8,128)(2,1)S(1)}, u32[]{:S(2)}, u32[]{:S(2)}) collective-permute-start(bf16[2,256,1408]{2,1,0:T(8,128)(2,1)} %param.23), channel_id=1, source_target_pairs={{4,6},{5,7},{6,4},{7,5},{12,14},{13,15},{14,12},{15,13},{20,22},{2... | collective-permute-start | bytes 4325384 | tf_op jit(solution)/shard_map/ppermute | solution.py:293
  88.0 60.6 %collective-permute-start.8 = (bf16[256,2048]{1,0:T(8,128)(2,1)S(1)}, bf16[256,2048]{1,0:T(8,128)(2,1)S(1)}, u32[]{:S(2)}, u32[]{:S(2)}) collective-permute-start(bf16[256,2048]{1,0:T(8,128)(2,1)S(1)} %copy-done.21), channel_id=1, source_target_pairs={{0,1},{1,0},{2,3},{3,2},{4,5},{5,4},{6,7},{7,6},{8,9},{9,8},{10,11... | collective-permute-start | bytes 3145736 | tf_op jit(solution)/shard_map/ppermute | solution.py:287
  202.9 86.0 %collective-permute-start.38 = (bf16[1408,256]{1,0:T(8,128)(2,1)}, bf16[1408,256]{1,0:T(8,128)(2,1)}, u32[]{:S(2)}, u32[]{:S(2)}) collective-permute-start(bf16[1408,256]{1,0:T(8,128)(2,1)} %get-tuple-element.288), channel_id=1, source_target_pairs={{0,8},{1,9},{2,10},{3,11},{4,12},{5,13},{6,14},{7,15},{8,0},{9,1},... | collective-permute-start | bytes 2162696 | tf_op jit(solution)/shard_map/ppermute | solution.py:287
  205.2 117.5 %collective-permute-start.27 = (bf16[2,256,1408]{2,1,0:T(8,128)(2,1)}, bf16[2,256,1408]{2,1,0:T(8,128)(2,1)}, u32[]{:S(2)}, u32[]{:S(2)}) collective-permute-start(bf16[2,256,1408]{2,1,0:T(8,128)(2,1)} %get-tuple-element.283), channel_id=1, source_target_pairs={{0,8},{1,9},{2,10},{3,11},{4,12},{5,13},{6,14},{7,15},{8,0},{9,1},... | collective-permute-start | bytes 4325384 | tf_op jit(solution)/shard_map/ppermute | solution.py:287
  207.5 123.6 %collective-permute-start.26 = (bf16[2,256,1408]{2,1,0:T(8,128)(2,1)}, bf16[2,256,1408]{2,1,0:T(8,128)(2,1)}, u32[]{:S(2)}, u32[]{:S(2)}) collective-permute-start(bf16[2,256,1408]{2,1,0:T(8,128)(2,1)} %get-tuple-element.283), channel_id=1, source_target_pairs={{0,16},{1,17},{2,18},{3,19},{4,20},{5,21},{6,22},{7,23},{8,24},{9,... | collective-permute-start | bytes 4325384 | tf_op jit(solution)/shard_map/ppermute | solution.py:287
  218.5 64.0 %collective-permute-start.36 = (bf16[1408,256]{1,0:T(8,128)(2,1)}, bf16[1408,256]{1,0:T(8,128)(2,1)}, u32[]{:S(2)}, u32[]{:S(2)}) collective-permute-start(bf16[1408,256]{1,0:T(8,128)(2,1)} %collective-permute-done.35), channel_id=1, source_target_pairs={{0,16},{1,17},{2,18},{3,19},{4,20},{5,21},{6,22},{7,23},{8,24},{9,... | collective-permute-start | bytes 2162696 | tf_op jit(solution)/shard_map/ppermute | solution.py:287
  222.1 69.3 %collective-permute-start.40 = (bf16[1408,256]{1,0:T(8,128)(2,1)}, bf16[1408,256]{1,0:T(8,128)(2,1)}, u32[]{:S(2)}, u32[]{:S(2)}) collective-permute-start(bf16[1408,256]{1,0:T(8,128)(2,1)} %collective-permute-done.39), channel_id=1, source_target_pairs={{0,8},{1,9},{2,10},{3,11},{4,12},{5,13},{6,14},{7,15},{8,0},{9,1},... | collective-permute-start | bytes 2162696 | tf_op jit(solution)/shard_map/ppermute | solution.py:287
  289.0 66.3 %collective-permute-start.30 = (bf16[2,256,1408]{2,1,0:T(8,128)(2,1)S(1)}, bf16[2,256,1408]{2,1,0:T(8,128)(2,1)}, u32[]{:S(2)}, u32[]{:S(2)}) collective-permute-start(bf16[2,256,1408]{2,1,0:T(8,128)(2,1)S(1)} %copy-done.10), channel_id=1, source_target_pairs={{0,8},{1,9},{2,10},{3,11},{4,12},{5,13},{6,14},{7,15},{8,0},{9,1},... | collective-permute-start | bytes 4325384 | tf_op jit(solution)/shard_map/ppermute | solution.py:287
  448.4 61.6 %collective-permute-start.76 = (bf16[512,1408]{1,0:T(8,128)(2,1)}, bf16[512,1408]{1,0:T(8,128)(2,1)}, u32[]{:S(2)}, u32[]{:S(2)}) collective-permute-start(bf16[512,1408]{1,0:T(8,128)(2,1)} %convolution_convert_fusion.8), channel_id=1, source_target_pairs={{0,8},{1,9},{2,10},{3,11},{4,12},{5,13},{6,14},{7,15},{8,0},{9,1},... | collective-permute-start | bytes 4325384 | tf_op jit(solution)/shard_map/ppermute | solution.py:287
  448.7 65.5 %collective-permute-start.74 = (bf16[512,1408]{1,0:T(8,128)(2,1)}, bf16[512,1408]{1,0:T(8,128)(2,1)S(1)}, u32[]{:S(2)}, u32[]{:S(2)}) collective-permute-start(bf16[512,1408]{1,0:T(8,128)(2,1)} %convolution_convert_fusion.10), channel_id=1, source_target_pairs={{0,16},{1,17},{2,18},{3,19},{4,20},{5,21},{6,22},{7,23},{8,24},{9,... | collective-permute-start | bytes 4325384 | tf_op jit(solution)/shard_map/ppermute | solution.py:287
  448.9 91.9 %collective-permute-start.82 = (bf16[512,1408]{1,0:T(8,128)(2,1)}, bf16[512,1408]{1,0:T(8,128)(2,1)}, u32[]{:S(2)}, u32[]{:S(2)}) collective-permute-start(bf16[512,1408]{1,0:T(8,128)(2,1)} %convolution_convert_fusion.4), channel_id=1, source_target_pairs={{0,8},{1,9},{2,10},{3,11},{4,12},{5,13},{6,14},{7,15},{8,0},{9,1},... | collective-permute-start | bytes 4325384 | tf_op jit(solution)/shard_map/ppermute | solution.py:287
  479.1 65.1 %collective-permute-start.80 = (bf16[512,1408]{1,0:T(8,128)(2,1)S(1)}, bf16[512,1408]{1,0:T(8,128)(2,1)S(1)}, u32[]{:S(2)}, u32[]{:S(2)}) collective-permute-start(bf16[512,1408]{1,0:T(8,128)(2,1)S(1)} %convolution_convert_fusion.6), channel_id=1, source_target_pairs={{0,16},{1,17},{2,18},{3,19},{4,20},{5,21},{6,22},{7,23},{8,24},{9,... | collective-permute-start | bytes 4325384 | tf_op jit(solution)/shard_map/ppermute | solution.py:287
  481.6 64.8 %collective-permute-start.41 = (bf16[512,2048]{1,0:T(8,128)(2,1)S(1)}, bf16[512,2048]{1,0:T(8,128)(2,1)S(1)}, u32[]{:S(2)}, u32[]{:S(2)}) collective-permute-start(bf16[512,2048]{1,0:T(8,128)(2,1)S(1)} %copy-done.84), channel_id=1, source_target_pairs={{0,4},{1,5},{2,6},{3,7},{4,0},{5,1},{6,2},{7,3},{8,12},{9,13},{10,... | collective-permute-start | bytes 6291464 | tf_op jit(solution)/shard_map/ppermute | solution.py:287
  557.3 138.0 %collective-permute-start.42 = (bf16[256,2048]{1,0:T(8,128)(2,1)}, bf16[256,2048]{1,0:T(8,128)(2,1)}, u32[]{:S(2)}, u32[]{:S(2)}) collective-permute-start(bf16[256,2048]{1,0:T(8,128)(2,1)} %fusion.91), channel_id=1, source_target_pairs={{0,1},{1,0},{2,3},{3,2},{4,5},{5,4},{6,7},{7,6},{8,9},{9,8},{10,11... | collective-permute-start | bytes 3145736 | tf_op jit(solution)/shard_map/ppermute | solution.py:287
  579.5 62.1 %collective-permute-start.91 = (bf16[1408,256]{1,0:T(8,128)(2,1)S(1)}, bf16[1408,256]{1,0:T(8,128)(2,1)S(1)}, u32[]{:S(2)}, u32[]{:S(2)}) collective-permute-start(bf16[1408,256]{1,0:T(8,128)(2,1)S(1)} %get-tuple-element.246), channel_id=1, source_target_pairs={{6,0},{7,1},{4,2},{5,3},{0,4},{1,5},{2,6},{3,7},{14,8},{15,9},{12,... | collective-permute-start | bytes 2162696 | tf_op jit(solution)/shard_map/ppermute | solution.py:293
  587.9 61.4 %collective-permute-start.78 = (bf16[256,1408]{1,0:T(8,128)(2,1)S(1)}, bf16[256,1408]{1,0:T(8,128)(2,1)S(1)}, u32[]{:S(2)}, u32[]{:S(2)}) collective-permute-start(bf16[256,1408]{1,0:T(8,128)(2,1)S(1)} %get-tuple-element.249), channel_id=1, source_target_pairs={{4,6},{5,7},{6,4},{7,5},{12,14},{13,15},{14,12},{15,13},{20,22},{2... | collective-permute-start | bytes 2162696 | tf_op jit(solution)/shard_map/ppermute | solution.py:293
  594.8 62.2 %collective-permute-start.79 = (bf16[256,1408]{1,0:T(8,128)(2,1)S(1)}, bf16[256,1408]{1,0:T(8,128)(2,1)S(1)}, u32[]{:S(2)}, u32[]{:S(2)}) collective-permute-start(bf16[256,1408]{1,0:T(8,128)(2,1)S(1)} %get-tuple-element.248), channel_id=1, source_target_pairs={{6,0},{7,1},{4,2},{5,3},{0,4},{1,5},{2,6},{3,7},{14,8},{15,9},{12,... | collective-permute-start | bytes 2162696 | tf_op jit(solution)/shard_map/ppermute | solution.py:293
  618.4 46.4 %collective-permute-start.84 = (bf16[256,1408]{1,0:T(8,128)(2,1)S(1)}, bf16[256,1408]{1,0:T(8,128)(2,1)S(1)}, u32[]{:S(2)}, u32[]{:S(2)}) collective-permute-start(bf16[256,1408]{1,0:T(8,128)(2,1)S(1)} %get-tuple-element.251), channel_id=1, source_target_pairs={{4,6},{5,7},{6,4},{7,5},{12,14},{13,15},{14,12},{15,13},{20,22},{2... | collective-permute-start | bytes 2162696 | tf_op jit(solution)/shard_map/ppermute | solution.py:293
  821.9 62.5 %collective-permute-start.60 = (bf16[3,512,512]{1,2,0:T(8,128)(2,1)S(1)}, bf16[3,512,512]{1,2,0:T(8,128)(2,1)S(1)}, u32[]{:S(2)}, u32[]{:S(2)}) collective-permute-start(bf16[3,512,512]{1,2,0:T(8,128)(2,1)S(1)} %fusion.102), channel_id=1, source_target_pairs={{0,8},{1,9},{2,10},{3,11},{4,12},{5,13},{6,14},{7,15},{8,0},{9,1},... | collective-permute-start | bytes 4718600 | tf_op jit(solution)/shard_map/ppermute | solution.py:287
  824.9 64.8 %collective-permute-start.58 = (bf16[3,512,512]{1,2,0:T(8,128)(2,1)S(1)}, bf16[3,512,512]{1,2,0:T(8,128)(2,1)S(1)}, u32[]{:S(2)}, u32[]{:S(2)}) collective-permute-start(bf16[3,512,512]{1,2,0:T(8,128)(2,1)S(1)} %fusion.100), channel_id=1, source_target_pairs={{0,16},{1,17},{2,18},{3,19},{4,20},{5,21},{6,22},{7,23},{8,24},{9,... | collective-permute-start | bytes 4718600 | tf_op jit(solution)/shard_map/ppermute | solution.py:287
  833.7 58.3 %collective-permute-start.51 = (bf16[512,2048]{1,0:T(8,128)(2,1)S(1)}, bf16[512,2048]{1,0:T(8,128)(2,1)S(1)}, u32[]{:S(2)}, u32[]{:S(2)}) collective-permute-start(bf16[512,2048]{1,0:T(8,128)(2,1)S(1)} %bitcast_convert_fusion), channel_id=1, source_target_pairs={{0,4},{1,5},{2,6},{3,7},{4,0},{5,1},{6,2},{7,3},{8,12},{9,13},{10,... | collective-permute-start | bytes 6291464 | tf_op jit(solution)/shard_map/ppermute | solution.py:287
  (171 other events, 3984.8 us)

commit v3 on v1

--- a/solution.py
+++ b/solution.py
@@ -3,6 +3,8 @@
 import jax
 import jax.numpy as jnp
 from jax import lax
+from jax.experimental import pallas as pl
+from jax.experimental.pallas import tpu as pltpu
 from jax.sharding import PartitionSpec as P
 
 HD = 64
@@ -55,18 +57,18 @@
     )
 
 
-def causal_scores(queries, key_rows):
+def causal_scores(queries, key_rows, positions):
     scaling = 1.0 / math.sqrt(HD)
     scores = scaling * jnp.einsum(
         "qhd,khd->hqk", queries, key_rows, preferred_element_type=jnp.float32
     )
-    causal = jnp.arange(SEQ_LEN)[:, None] >= jnp.arange(SEQ_LEN)[None, :]
+    causal = positions[:, None] >= positions[None, :]
     return jnp.where(causal[None], scores, NEGATIVE)
 
 
-def attend_forward(pieces):
+def attend_forward(pieces, positions):
     queries, key_rows, value_rows = pieces
-    scores = causal_scores(queries, key_rows)
+    scores = causal_scores(queries, key_rows, positions)
     row_top = jnp.max(scores, axis=-1, keepdims=True)
     exponent = jnp.exp(scores - row_top)
     totals = jnp.sum(exponent, axis=-1, keepdims=True)
@@ -75,10 +77,10 @@
     return (mixed.astype(jnp.bfloat16), (row_top + jnp.log(totals))[..., 0])
 
 
-def attend_back(pieces):
+def attend_back(pieces, positions):
     queries, key_rows, value_rows, grad_mixed, log_totals = pieces
     scaling = 1.0 / math.sqrt(HD)
-    scores = causal_scores(queries, key_rows)
+    scores = causal_scores(queries, key_rows, positions)
     weights = jnp.exp(scores - log_totals[..., None])
     grad_values = jnp.einsum(
         "hqk,qhd->khd", weights.astype(jnp.bfloat16), grad_mixed, preferred_element_type=jnp.float32
@@ -125,6 +127,7 @@
     local_heads = head_width // HD
     head_shape = (sequences, SEQ_LEN, local_heads, HD)
     cosine, sine = angle_tables()
+    positions = jnp.arange(SEQ_LEN)
     proj_full, out_full, gain_one, shift_one = (
         lax.all_gather(projections, "dp", axis=1, tiled=True),
         lax.all_gather(output_weight, "dp", axis=1, tiled=True),
@@ -140,7 +143,9 @@
     queries = rotate(pre_all[0].reshape(head_shape), cosine, sine, 1.0).astype(jnp.bfloat16)
     key_rows = rotate(pre_all[1].reshape(head_shape), cosine, sine, 1.0).astype(jnp.bfloat16)
     value_rows = pre_all[2].reshape(head_shape).astype(jnp.bfloat16)
-    mixed, log_totals = lax.map(attend_forward, (queries, key_rows, value_rows))
+    mixed, log_totals = lax.map(
+        lambda pieces: attend_forward(pieces, positions), (queries, key_rows, value_rows)
+    )
     mixed_rows = mixed.reshape(group_rows, head_width)
     part = mixed_rows
     middle = residual + scatter_sum(
@@ -214,7 +219,8 @@
         "gd,ed->ge", gathered_branch, out_back, preferred_element_type=jnp.float32
     ).astype(jnp.bfloat16)
     grad_queries, grad_keys, grad_values = lax.map(
-        attend_back, (queries, key_rows, value_rows, grad_mixed.reshape(head_shape), log_totals)
+        lambda pieces: attend_back(pieces, positions),
+        (queries, key_rows, value_rows, grad_mixed.reshape(head_shape), log_totals),
     )
     grad_queries = rotate(grad_queries, cosine, sine, -1.0)
     grad_keys = rotate(grad_keys, cosine, sine, -1.0)
@@ -273,9 +279,988 @@
     )
 
 
+def send_between(array, routes):
+    tensor_ways = lax.axis_size("tensor")
+    pairs = [(d * tensor_ways + t, e * tensor_ways + s) for (d, t), (e, s) in routes]
+    return lax.ppermute(array, ("dp", "tensor"), pairs)
+
+
+def places():
+    return [(d, t) for d in range(lax.axis_size("dp")) for t in range(lax.axis_size("tensor"))]
+
+
+def own_quarter(array):
+    return send_between(
+        array,
+        [((d, t), (d ^ 1, t) if d & 1 else (d ^ 1, t ^ 2)) for d, t in places()],
+    )
+
+
+ORDER = ((1, 0, 0), (1, 1, 0), (0, 1, 1), (1, 1, 1), (0, 0, 0), (0, 1, 0), (0, 0, 1), (1, 0, 1))
+EVEN_Y, EVEN_XY, ODD_X, ODD_XY, EVEN, EVEN_X, ODD, ODD_Y = range(8)
+ANY = pl.BlockSpec(memory_space=pl.ANY)
+VMEM_BYTES = 60 * 1024 * 1024
+
+
+class Place:
+    def __init__(self, send_sems, recv_sems, local_sems):
+        self.dp, self.tensor = lax.axis_index("dp"), lax.axis_index("tensor")
+        self.core = lax.rem(self.dp, 2)
+        self.x = lax.rem(self.dp // 2, 2)
+        self.y = self.dp // 4
+        self.pools = {"send": send_sems, "recv": recv_sems, "local": local_sems}
+        self.used = {"send": 0, "recv": 0, "local": 0}
+
+    def take(self, kind):
+        self.used[kind] += 1
+        return self.pools[kind].at[self.used[kind] - 1]
+
+    def at(self, x=0, y=0, core=0, near=0, far=0):
+        dp = self.dp
+        dp = dp + x * (2 - 4 * self.x) + y * (4 - 8 * self.y) + core * (1 - 2 * self.core)
+        tensor = self.tensor
+        tensor = tensor + near * (1 - 2 * lax.rem(tensor, 2)) + far * (2 - 4 * (tensor // 2))
+        return (dp, tensor)
+
+    def column(self, key):
+        dy, dx, core = key
+        y = self.y + dy * (1 - 2 * self.y)
+        x = self.x + dx * (1 - 2 * self.x)
+        return pl.multiple_of((y * 4 + x * 2 + core) * EIGHTH, EIGHTH)
+
+    def greet(self):
+        barrier = pltpu.get_barrier_semaphore()
+        partners = [
+            self.at(x=x, y=y, core=core)
+            for x in (0, 1)
+            for y in (0, 1)
+            for core in (0, 1)
+            if x or y or core
+        ] + [self.at(near=1), self.at(far=1), self.at(far=1, core=1)]
+        for partner in partners:
+            pl.semaphore_signal(
+                barrier, inc=1, device_id=partner, device_id_type=pl.DeviceIdType.MESH
+            )
+        pl.semaphore_wait(barrier, len(partners))
+
+    def send(self, source, target, device, recv_sem=None, when=None):
+        return Sent(
+            pltpu.make_async_remote_copy(
+                src_ref=source,
+                dst_ref=target,
+                send_sem=self.take("send"),
+                recv_sem=self.take("recv") if recv_sem is None else recv_sem,
+                device_id=device,
+                device_id_type=pl.DeviceIdType.MESH,
+            ),
+            when,
+        )
+
+    def copy(self, source, target, when=None):
+        return Copied(pltpu.make_async_copy(source, target, self.take("local")), when)
+
+
+def guarded(when, action):
+    if when is None:
+        action()
+    else:
+        pl.when(when)(action)
+
+
+class Sent:
+    def __init__(self, copy, when):
+        self.copy, self.when = copy, when
+
+    def start(self):
+        guarded(self.when, self.copy.start)
+        return self
+
+    def arrived(self, when=None):
+        guarded(when, self.copy.wait_recv)
+
+    def left(self):
+        guarded(self.when, self.copy.wait_send)
+
+
+class Copied:
+    def __init__(self, copy, when):
+        self.copy, self.when = copy, when
+
+    def start(self):
+        guarded(self.when, self.copy.start)
+        return self
+
+    def wait(self):
+        guarded(self.when, self.copy.wait)
+
+
+class GatherWeight:
+    def __init__(self, place, shard, block, pair=None):
+        self.place, self.shard, self.block = place, shard, block
+        self.sent = []
+        self.pair = pair
+
+    def fetch(self, even=None, odd=None):
+        p = self.place
+        even = self.block(EVEN) if even is None else even
+        odd = self.block(ODD) if odd is None else odd
+        first, second = p.core == 0, p.core == 1
+        self.own = p.copy(self.shard, even, first).start()
+        even_sem, odd_sem = p.take("recv"), p.take("recv")
+        self.to_far_even = p.send(self.shard, even, p.at(core=1, far=1), even_sem, first).start()
+        self.to_sibling = p.send(self.shard, odd, p.at(core=1), odd_sem, second).start()
+        self.to_far_odd = p.send(self.shard, odd, p.at(far=1), odd_sem, second).start()
+        return self
+
+    def fetched(self):
+        p = self.place
+        self.own.wait()
+        self.to_far_even.arrived(p.core == 1)
+        self.to_sibling.arrived()
+        return self
+
+    def fetch_left(self):
+        self.to_far_even.left()
+        self.to_sibling.left()
+        self.to_far_odd.left()
+
+    def spread(self, even=None, odd=None):
+        p, block = self.place, self.block
+        even = block(EVEN) if even is None else even
+        odd = block(ODD) if odd is None else odd
+        self.even_x = p.send(even, block(EVEN_X), p.at(x=1)).start()
+        self.odd_y = p.send(odd, block(ODD_Y), p.at(y=1)).start()
+        self.odd_x = p.send(odd, block(ODD_X), p.at(x=1)).start()
+        self.even_y = p.send(even, block(EVEN_Y), p.at(y=1)).start()
+        return self
+
+    def relay(self):
+        p, block = self.place, self.block
+        self.even_x.arrived()
+        self.even_xy = p.send(block(EVEN_X), block(EVEN_XY), p.at(y=1)).start()
+        self.odd_y.arrived()
+        self.odd_xy = p.send(block(ODD_Y), block(ODD_XY), p.at(x=1)).start()
+        return self
+
+    def finish(self):
+        for copy in (self.odd_x, self.even_y, self.even_xy, self.odd_xy):
+            copy.arrived()
+        for copy in (
+            self.even_x, self.odd_y, self.odd_x, self.even_y, self.even_xy, self.odd_xy,
+        ):
+            copy.left()
+
+
+class GatherRows:
+    def __init__(self, place, own, rows):
+        self.place, self.own, self.rows = place, own, rows
+        self.count = own.shape[0]
+
+    def slot(self, k):
+        return self.rows.at[pl.ds(k * self.count, self.count)]
+
+    def start(self):
+        p = self.place
+        self.beside = p.send(self.own, self.slot(1), p.at(near=1)).start()
+        self.sibling = p.send(self.own, self.slot(2), p.at(core=1)).start()
+        self.here = p.copy(self.own, self.slot(0)).start()
+        return self
+
+    def relay(self):
+        p = self.place
+        self.beside.arrived()
+        self.across = p.send(self.slot(1), self.slot(3), p.at(core=1)).start()
+        return self
+
+    def finish(self):
+        self.sibling.arrived()
+        self.across.arrived()
+        self.here.wait()
+        for copy in (self.beside, self.sibling, self.across):
+            copy.left()
+
+
+def combine(target, terms, chunk):
+    @pl.loop(0, target.shape[0] // chunk)
+    def _(i):
+        rows = pl.ds(pl.multiple_of(i * chunk, chunk), chunk)
+        total = terms[0][rows].astype(jnp.float32)
+        for term in terms[1:]:
+            total = total + term[rows].astype(jnp.float32)
+        target[rows] = total.astype(target.dtype)
+
+
+class ScatterRows:
+    def __init__(self, place, term, near, got, got_beside):
+        self.place, self.term, self.near = place, term, near
+        self.got, self.got_beside = got, got_beside
+        self.count = term.shape[0] // 4
+
+    def start(self):
+        p, n = self.place, self.count
+        self.sibling = p.send(self.term.at[pl.ds(2 * n, 2 * n)], self.got, p.at(core=1)).start()
+        self.load = p.copy(self.term.at[pl.ds(0, 2 * n)], self.near).start()
+        return self
+
+    def relay(self):
+        p, n = self.place, self.count
+        self.load.wait()
+        self.sibling.arrived()
+        late = pl.ds(n, n)
+        combine(self.near.at[late], [self.near.at[late], self.got.at[late]], 32)
+        self.beside = p.send(self.near.at[late], self.got_beside, p.at(near=1)).start()
+        return self
+
+    def total(self, rows):
+        return (
+            self.near[rows].astype(jnp.float32)
+            + self.got[rows].astype(jnp.float32)
+            + self.got_beside[rows].astype(jnp.float32)
+        )
+
+    def arrived(self):
+        self.beside.arrived()
+
+    def finish(self):
+        self.sibling.left()
+        self.beside.left()
+
+
+class ScatterWeight:
+    def __init__(self, place, parts, rows, keep, got, last, home, result):
+        self.place, self.parts, self.rows = place, parts, rows
+        self.keep, self.got, self.last, self.home, self.result = keep, got, last, home, result
+
+    def half(self, ref, k):
+        if self.rows:
+            size = ref.shape[0] // 2
+            return ref.at[pl.ds(k * size, size)]
+        size = ref.shape[1] // 2
+        return ref.at[:, pl.ds(k * size, size)]
+
+    def start(self):
+        p = self.place
+        self.even = p.send(self.parts[0], self.got.at[0], p.at(y=1)).start()
+        self.odd = p.send(self.parts[1], self.got.at[1], p.at(x=1)).start()
+        self.loads = [p.copy(self.parts[2 + k], self.keep.at[k]).start() for k in (0, 1)]
+        return self
+
+    def relay(self):
+        p = self.place
+        for k, arrival in enumerate((self.even, self.odd)):
+            self.loads[k].wait()
+            arrival.arrived()
+            there = self.half(self.keep.at[k], 1)
+            combine(there, [there, self.half(self.got.at[k], 1)], 64)
+            sent = p.send(there, self.last.at[k], p.at(x=1) if k == 0 else p.at(y=1)).start()
+            if k == 0:
+                self.even_last = sent
+            else:
+                self.odd_last = sent
+        return self
+
+    def settle(self):
+        p = self.place
+        self.even_last.arrived()
+        self.odd_last.arrived()
+
+        def terms(k):
+            return [self.half(self.keep.at[k], 0), self.half(self.got.at[k], 0), self.last.at[k]]
+
+        even_out, odd_out = self.half(self.keep.at[0], 0), self.half(self.keep.at[1], 0)
+        combine(odd_out, terms(1), 64)
+        first, second = p.core == 0, p.core == 1
+        pl.when(first)(lambda: combine(self.result, terms(0), 64))
+        pl.when(second)(lambda: combine(even_out, terms(0), 64))
+        near_sem, far_sem = p.take("recv"), p.take("recv")
+        self.to_sibling = p.send(odd_out, self.home.at[0], p.at(core=1), near_sem, first).start()
+        self.to_first = p.send(
+            even_out, self.home.at[0], p.at(core=1, far=1), near_sem, second
+        ).start()
+        self.to_far = p.send(odd_out, self.home.at[1], p.at(far=1), far_sem, second).start()
+        return self
+
+    def finish(self, output):
+        p = self.place
+        first, second = p.core == 0, p.core == 1
+        self.to_sibling.arrived()
+        self.to_far.arrived(second)
+        pl.when(first)(lambda: combine(self.result, [self.result, self.home.at[0]], 64))
+        pl.when(second)(lambda: combine(self.result, [self.home.at[0], self.home.at[1]], 64))
+        self.store = p.copy(self.result, output).start()
+        for copy in (
+            self.even, self.odd, self.even_last, self.odd_last,
+            self.to_sibling, self.to_first, self.to_far,
+        ):
+            copy.left()
+
+    def stored(self):
+        self.store.wait()
+
+
+def load_local(place, source, target):
+    return [
+        place.copy(
+            source.at[:, pl.ds(place.column(key), EIGHTH)], target.at[:, pl.ds(j * EIGHTH, EIGHTH)]
+        ).start()
+        for j, key in enumerate(ORDER)
+    ]
+
+
+def store_natural(place, source, target):
+    return [
+        place.copy(
+            source.at[:, pl.ds(j * EIGHTH, EIGHTH)], target.at[:, pl.ds(place.column(key), EIGHTH)]
+        ).start()
+        for j, key in enumerate(ORDER)
+    ]
+
+
+def wait_all(copies):
+    for copy in copies:
+        copy.wait()
+
+
+CHUNK = 32
+
+
+def norm_into(count, rows_of, gain, shift, target):
+    @pl.loop(0, count // CHUNK)
+    def _(i):
+        rows = pl.ds(pl.multiple_of(i * CHUNK, CHUNK), CHUNK)
+        target[rows] = norm_rows(rows_of(rows), gain, shift)[0].astype(target.dtype)
+
+
+def front_kernel(
+    inputs, cotangent, vectors, projections, output_weight, gate_up,
+    proj_full, out_full, gate_pair, vectors_full, rows_one, rows_cot,
+    own, normed, own_cot, vectors_here, send_sems, recv_sems, local_sems,
+):
+    p = Place(send_sems, recv_sems, local_sems)
+    loads = load_local(p, inputs, own)
+    cot_loads = load_local(p, cotangent, own_cot)
+    p.greet()
+    slots = {key: j for j, key in enumerate(ORDER)}
+    vector_sem = [p.take("recv") for _ in ORDER]
+    del vector_sem
+    vector_base = p.used["recv"] - len(ORDER)
+
+    def vector_copy(dy, dx, core):
+        here, there = slots[(dy, dx, 0)], slots[(dy, dx, 1)]
+        slot = here + p.core * (there - here)
+        columns = pl.ds(pl.multiple_of(slot * EIGHTH, EIGHTH), EIGHTH)
+        return p.send(
+            vectors, vectors_here.at[:, columns], p.at(x=dx, y=dy, core=core),
+            recv_sems.at[vector_base + slot],
+        )
+
+    vector_sends = [
+        vector_copy(dy, dx, core).start()
+        for dy in (0, 1) for dx in (0, 1) for core in (0, 1) if dy or dx or core
+    ]
+    own_slot = slots[(0, 0, 0)] + p.core * (slots[(0, 0, 1)] - slots[(0, 0, 0)])
+    own_vectors = p.copy(
+        vectors, vectors_here.at[:, pl.ds(pl.multiple_of(own_slot * EIGHTH, EIGHTH), EIGHTH)]
+    ).start()
+
+    def quarter(j):
+        return GatherWeight(
+            p, projections.at[j], lambda k: proj_full.at[j, pl.ds(k * EIGHTH, EIGHTH)]
+        )
+
+    weights = [quarter(0), quarter(1), quarter(2)]
+    weights.append(
+        GatherWeight(p, output_weight, lambda k: out_full.at[:, pl.ds(k * EIGHTH, EIGHTH)])
+    )
+    gate = GatherWeight(p, gate_up.at[0], lambda k: gate_pair.at[k])
+    weights[0].fetch()
+    weights[1].fetch()
+    wait_all(cot_loads)
+    wait_all(loads)
+    own_vectors.wait()
+    sibling_slot = slots[(0, 0, 1)] + p.core * (slots[(0, 0, 0)] - slots[(0, 0, 1)])
+    for dy in (0, 1):
+        for dx in (0, 1):
+            for core in (0, 1):
+                if dy or dx:
+                    slot = slots[(dy, dx, core)]
+                elif core:
+                    slot = sibling_slot
+                else:
+                    continue
+                pltpu.make_async_copy(
+                    vectors, vectors_here.at[:, pl.ds(0, EIGHTH)], recv_sems.at[vector_base + slot]
+                ).wait()
+    gain, shift = vectors_here[0:1], vectors_here[1:2]
+    norm_into(own.shape[0], lambda rows: own[rows].astype(jnp.float32), gain, shift, normed)
+    gather_one = GatherRows(p, normed, rows_one).start()
+    gather_cot = GatherRows(p, own_cot, rows_cot)
+    vector_store = p.copy(vectors_here, vectors_full).start()
+
+    weights[0].fetched().spread()
+    weights[2].fetch()
+    weights[1].fetched().spread()
+    weights[3].fetch()
+    weights[0].relay()
+    weights[2].fetched().spread()
+    gather_one.relay()
+    gather_cot.start()
+    weights[1].relay()
+    gate.fetch(gate_pair.at[0], gate_pair.at[1])
+    weights[3].fetched().spread()
+    weights[2].relay()
+    weights[3].relay()
+    gather_cot.relay()
+    for weight in weights:
+        weight.finish()
+        weight.fetch_left()
+    gather_one.finish()
+    gather_cot.finish()
+    gate.fetched()
+    gate.fetch_left()
+    for sent in vector_sends:
+        sent.left()
+    vector_store.wait()
+
+
+def middle_kernel(
+    term, inputs, vectors, gate_pair, gate_up, down_weight,
+    gu_full, down_full, middle, rows_two,
+    own, near, got, got_beside, total, normed, send_sems, recv_sems, local_sems,
+):
+    p = Place(send_sems, recv_sems, local_sems)
+    loads = load_local(p, inputs, own)
+    p.greet()
+    scatter = ScatterRows(p, term, near, got, got_beside).start()
+
+    def gu_block(j):
+        return lambda k: gu_full.at[j, pl.ds(k * EIGHTH, EIGHTH)]
+
+    gate = GatherWeight(p, None, gu_block(0))
+    up = GatherWeight(p, gate_up.at[1], gu_block(1))
+    down = GatherWeight(p, down_weight, lambda k: down_full.at[:, pl.ds(k * EIGHTH, EIGHTH)])
+    gate.spread(gate_pair.at[0], gate_pair.at[1])
+    places = [
+        p.copy(gate_pair.at[0], gate.block(EVEN)).start(),
+        p.copy(gate_pair.at[1], gate.block(ODD)).start(),
+    ]
+    up.fetch()
+    scatter.relay()
+    wait_all(loads)
+    scatter.arrived()
+    count = own.shape[0]
+    gain, shift = vectors[2:3], vectors[3:4]
+
+    @pl.loop(0, count // CHUNK)
+    def _(i):
+        rows = pl.ds(pl.multiple_of(i * CHUNK, CHUNK), CHUNK)
+        value = own[rows].astype(jnp.float32) + scatter.total(rows)
+        total[rows] = value
+        normed[rows] = norm_rows(value, gain, shift)[0].astype(normed.dtype)
+
+    gather = GatherRows(p, normed, rows_two).start()
+    store = p.copy(total, middle).start()
+    up.fetched()
+    down.fetch()
+    up.spread()
+    gate.relay()
+    gather.relay()
+    down.fetched()
+    up.relay()
+    down.spread()
+    down.relay()
+    for weight in (gate, up, down):
+        weight.finish()
+    up.fetch_left()
+    down.fetch_left()
+    scatter.finish()
+    gather.finish()
+    wait_all(places)
+    store.wait()
+
+
+def norm_back_rows(value, incoming, gain):
+    average = jnp.mean(value, axis=-1, keepdims=True)
+    centred = value - average
+    inverse = lax.rsqrt(jnp.mean(centred * centred, axis=-1, keepdims=True) + EPSILON)
+    unit = centred * inverse
+    scaled = incoming * gain
+    inner = (
+        scaled
+        - jnp.mean(scaled, axis=-1, keepdims=True)
+        - unit * jnp.mean(scaled * unit, axis=-1, keepdims=True)
+    )
+    return inner * inverse, incoming * unit
+
+
+def fold(array):
+    return jnp.sum(array.reshape(array.shape[0] // 8, 8, array.shape[1]), axis=0)
+
+
+def back_kernel(
+    term, out_term, middle, cotangent, vectors, *rest,
+):
+    down_parts, gate_parts, up_parts = rest[0:4], rest[4:8], rest[8:12]
+    (
+        outputs, grad_middle, rows_branch, sums, gu_owned, down_owned,
+        value, own_cot, near, got, got_beside, near_out, got_out, got_out_beside, branch, result,
+        gain_sum, shift_sum,
+        d_keep, d_got, d_last, d_home, d_result,
+        g_keep, g_got, g_last, g_home, g_result,
+        u_keep, u_got, u_last, u_home, u_result,
+        send_sems, recv_sems, local_sems,
+    ) = rest[12:]
+    p = Place(send_sems, recv_sems, local_sems)
+    cot_loads = load_local(p, cotangent, own_cot)
+    value_load = p.copy(middle, value).start()
+    p.greet()
+    scatter = ScatterRows(p, term, near, got, got_beside).start()
+    out_scatter = ScatterRows(p, out_term, near_out, got_out, got_out_beside)
+    down = ScatterWeight(p, down_parts, False, d_keep, d_got, d_last, d_home, d_result).start()
+    gate = ScatterWeight(p, gate_parts, True, g_keep, g_got, g_last, g_home, g_result)
+    up = ScatterWeight(p, up_parts, True, u_keep, u_got, u_last, u_home, u_result)
+    scatter.relay()
+    out_scatter.start()
+    wait_all(cot_loads)
+    value_load.wait()
+    scatter.arrived()
+    out_scatter.relay()
+    count = value.shape[0]
+    gain = vectors[2:3]
+    gain_sum[...] = jnp.zeros_like(gain_sum)
+    shift_sum[...] = jnp.zeros_like(shift_sum)
+
+    @pl.loop(0, count // CHUNK)
+    def _(i):
+        rows = pl.ds(pl.multiple_of(i * CHUNK, CHUNK), CHUNK)
+        incoming = scatter.total(rows)
+        back, product = norm_back_rows(value[rows], incoming, gain)
+        gain_sum[...] += fold(product)
+        shift_sum[...] += fold(incoming)
+        grad = own_cot[rows].astype(jnp.float32) + back
+        result[rows] = grad
+        branch[rows] = grad.astype(branch.dtype)
+
+    gather = GatherRows(p, branch, rows_branch).start()
+    grad_store = p.copy(result, grad_middle).start()
+    gain_sum[0:1] = jnp.sum(gain_sum[...], axis=0, keepdims=True)
+    gain_sum[1:2] = jnp.sum(shift_sum[...], axis=0, keepdims=True)
+    sum_store = p.copy(gain_sum, sums).start()
+    gate.start()
+    down.relay()
+    out_scatter.arrived()
+
+    @pl.loop(0, count // CHUNK)
+    def _(i):
+        rows = pl.ds(pl.multiple_of(i * CHUNK, CHUNK), CHUNK)
+        own_cot[rows] = (value[rows] + out_scatter.total(rows)).astype(own_cot.dtype)
+
+    out_stores = store_natural(p, own_cot, outputs)
+    gather.relay()
+    up.start()
+    gate.relay()
+    down.settle()
+    up.relay()
+    gate.settle()
+    down.finish(down_owned)
+    up.settle()
+    gate.finish(gu_owned.at[0])
+    up.finish(gu_owned.at[1])
+    for weight in (down, gate, up):
+        weight.stored()
+    scatter.finish()
+    out_scatter.finish()
+    gather.finish()
+    wait_all(out_stores)
+    grad_store.wait()
+    sum_store.wait()
+
+
+def last_kernel(
+    term, inputs, vectors, grad_middle, sums, bias_part, *rest,
+):
+    out_parts, proj_parts = rest[0:4], rest[4:8]
+    (
+        input_grads, proj_owned, out_owned, vector_grads, bias_grad,
+        own, near, got, got_beside, result, all_sums, shift_sum, vector_got, vector_total, z_got,
+        bias_here, bias_got,
+        o_keep, o_got, o_last, o_home, o_result,
+        q_keep, q_got, q_last, q_home, q_result,
+        k_keep, k_got, k_last, k_home, k_result,
+        v_keep, v_got, v_last, v_home, v_result,
+        send_sems, recv_sems, local_sems,
+    ) = rest[8:]
+    p = Place(send_sems, recv_sems, local_sems)
+    loads = load_local(p, inputs, own)
+    loads.append(p.copy(grad_middle, result).start())
+    p.greet()
+    first, second = p.core == 0, p.core == 1
+    scatter = ScatterRows(p, term, near, got, got_beside).start()
+    out = ScatterWeight(p, out_parts, False, o_keep, o_got, o_last, o_home, o_result).start()
+    thirds = [
+        ScatterWeight(p, [part.at[j] for part in proj_parts], True, *refs)
+        for j, refs in enumerate(
+            (
+                (q_keep, q_got, q_last, q_home, q_result),
+                (k_keep, k_got, k_last, k_home, k_result),
+                (v_keep, v_got, v_last, v_home, v_result),
+            )
+        )
+    ]
+    thirds[0].start()
+    bias_load = p.copy(bias_part, bias_here).start()
+    scatter.relay()
+    bias_load.wait()
+    bias_x = p.send(bias_here, bias_got.at[0], p.at(x=1)).start()
+    bias_x.arrived()
+    bias_x.left()
+    bias_here[...] += bias_got[0]
+    bias_y = p.send(bias_here, bias_got.at[1], p.at(y=1)).start()
+    out.relay()
+    thirds[1].start()
+    bias_y.arrived()
+    bias_y.left()
+    bias_here[...] += bias_got[1]
+    near_sem, far_sem = p.take("recv"), p.take("recv")
+    bias_home = [
+        p.send(bias_here, bias_got.at[2], p.at(core=1), near_sem, first).start(),
+        p.send(bias_here, bias_got.at[2], p.at(core=1, far=1), near_sem, second).start(),
+        p.send(bias_here, bias_got.at[3], p.at(far=1), far_sem, second).start(),
+    ]
+    wait_all(loads)
+    scatter.arrived()
+    count = own.shape[0]
+    gain = vectors[0:1]
+    all_sums[...] = jnp.zeros_like(all_sums)
+    shift_sum[...] = jnp.zeros_like(shift_sum)
+
+    @pl.loop(0, count // CHUNK)
+    def _(i):
+        rows = pl.ds(pl.multiple_of(i * CHUNK, CHUNK), CHUNK)
+        incoming = scatter.total(rows)
+        back, product = norm_back_rows(own[rows].astype(jnp.float32), incoming, gain)
+        all_sums[...] += fold(product)
+        shift_sum[...] += fold(incoming)
+        result[rows] = result[rows] + back
+
+    stores = store_natural(p, result, input_grads)
+    all_sums[0:1] = jnp.sum(all_sums[...], axis=0, keepdims=True)
+    all_sums[1:2] = jnp.sum(shift_sum[...], axis=0, keepdims=True)
+    all_sums[2:4] = sums[0:2]
+    slots = {key: j for j, key in enumerate(ORDER)}
+    vector_sends = []
+    n = 0
+    for dy in (0, 1):
+        for dx in (0, 1):
+            for core in (0, 1):
+                if not (dy or dx or core):
+                    continue
+                straight, crossed = slots[(dy, dx, core)], slots[(dy, dx, 1 - core)]
+                slot = straight + p.core * (crossed - straight)
+                columns = pl.ds(pl.multiple_of(slot * EIGHTH, EIGHTH), EIGHTH)
+                vector_sends.append(
+                    p.send(
+                        all_sums.at[:, columns], vector_got.at[n], p.at(x=dx, y=dy, core=core)
+                    ).start()
+                )
+                n += 1
+    thirds[0].relay()
+    thirds[2].start()
+    own_slot = slots[(0, 0, 0)] + p.core * (slots[(0, 0, 1)] - slots[(0, 0, 0)])
+    total = all_sums[:, pl.ds(pl.multiple_of(own_slot * EIGHTH, EIGHTH), EIGHTH)]
+    for k, sent in enumerate(vector_sends):
+        sent.arrived()
+        total = total + vector_got[k]
+    vector_total[0] = total
+    z_near = p.send(vector_total.at[0], z_got.at[0], p.at(near=1)).start()
+    out.settle()
+    z_near.arrived()
+    vector_total[1] = total + z_got[0]
+    z_far = p.send(vector_total.at[1], z_got.at[1], p.at(far=1)).start()
+    thirds[1].relay()
+    thirds[0].settle()
+    z_far.arrived()
+    z_near.left()
+    z_far.left()
+    vector_total[0] = vector_total[1] + z_got[1]
+    vector_store = p.copy(vector_total.at[0], vector_grads).start()
+    bias_home[0].arrived()
+    bias_home[2].arrived(second)
+    for sent in bias_home:
+        sent.left()
+    pl.when(second)(lambda: combine(bias_got.at[2], [bias_got.at[2], bias_got.at[3]], 8))
+    pl.when(first)(lambda: combine(bias_got.at[2], [bias_got.at[2], bias_here], 8))
+    bias_store = p.copy(bias_got.at[2], bias_grad).start()
+    thirds[2].relay()
+    thirds[1].settle()
+    out.finish(out_owned)
+    thirds[0].finish(proj_owned.at[0])
+    thirds[2].settle()
+    thirds[1].finish(proj_owned.at[1])
+    thirds[2].finish(proj_owned.at[2])
+    for weight in [out, *thirds]:
+        weight.stored()
+    scatter.finish()
+    for sent in vector_sends:
+        sent.left()
+    wait_all(stores)
+    vector_store.wait()
+    bias_store.wait()
+
+
+def call(body, name, collective, inputs, in_specs, outs, scratch, counts):
+    bf16_bytes = sum(math.prod(o.shape) * o.dtype.itemsize for o in outs)
+    return pl.pallas_call(
+        body,
+        out_shape=outs,
+        in_specs=in_specs,
+        out_specs=[ANY] * len(outs),
+        scratch_shapes=[
+            *scratch,
+            pltpu.SemaphoreType.DMA((counts[0],)),
+            pltpu.SemaphoreType.DMA((counts[1],)),
+            pltpu.SemaphoreType.DMA((counts[2],)),
+        ],
+        compiler_params=pltpu.CompilerParams(
+            collective_id=collective, has_side_effects=True, vmem_limit_bytes=VMEM_BYTES
+        ),
+        cost_estimate=pl.CostEstimate(
+            flops=0, bytes_accessed=2 * bf16_bytes, transcendentals=0
+        ),
+        name=name,
+    )(*inputs)
+
+
+def bf16(*shape):
+    return jax.ShapeDtypeStruct(shape, jnp.bfloat16)
+
+
+def f32(*shape):
+    return jax.ShapeDtypeStruct(shape, jnp.float32)
+
+
+def held(shape_struct):
+    return pltpu.VMEM(shape_struct.shape, shape_struct.dtype)
+
+
+def weight_scratch(quarter, eighth):
+    return [
+        held(bf16(2, *quarter)), held(bf16(2, *quarter)), held(bf16(2, *eighth)),
+        held(bf16(2, *eighth)), held(f32(*eighth)),
+    ]
+
+
+WHOLE = pl.BlockSpec(memory_space=pltpu.VMEM)
+EIGHTH = 256
+
+
+def local_pairs(
+    inputs,
+    gain_first,
+    shift_first,
+    projections,
+    biases,
+    output_weight,
+    gain_second,
+    shift_second,
+    gate_up,
+    down_weight,
+    cotangent,
+):
+    dp_index, tensor_index = lax.axis_index("dp"), lax.axis_index("tensor")
+    first_core = dp_index % 2 == 0
+    late_half = tensor_index % 2 == 1
+    count, width = inputs.shape
+    rows = 4 * count
+    heads_width = output_weight.shape[0]
+    hidden_width = down_weight.shape[0]
+    local_heads = heads_width // HD
+    head_shape = (2, SEQ_LEN, local_heads, HD)
+    quarter_width = width // 4
+
+    def width_part(array, k):
+        return array[:, k * quarter_width : (k + 1) * quarter_width]
+
+    positions = jnp.arange(SEQ_LEN)
+    positions = jnp.where(late_half, (positions + SEQ_LEN // 2) % SEQ_LEN, positions)
+    cosine, sine = (
+        jnp.where(late_half, jnp.roll(table, SEQ_LEN // 2, axis=0), table)
+        for table in angle_tables()
+    )
+    vectors = jnp.pad(
+        jnp.stack([gain_first, shift_first, gain_second, shift_second]).astype(jnp.float32),
+        ((0, 4), (0, 0)),
+    )
+    quarter_biases = jnp.where(first_core, biases, own_quarter(biases)).astype(jnp.float32)
+
+    proj_full, out_full, gate_pair, vectors, gathered_one, gathered_cot = call(
+        front_kernel, "gather_first", 1,
+        (inputs, cotangent, vectors, projections, output_weight, gate_up),
+        [ANY] * 6,
+        [
+            bf16(3, width, heads_width), bf16(heads_width, width), bf16(2, EIGHTH, hidden_width),
+            f32(8, width), bf16(rows, width), bf16(rows, width),
+        ],
+        [held(bf16(count, width)), held(bf16(count, width)), held(bf16(count, width)), held(f32(8, width))],
+        (64, 64, 40),
+    )
+
+    pre_all = jnp.einsum("gd,jde->jge", gathered_one, proj_full, preferred_element_type=jnp.float32)
+    pre_all = pre_all + quarter_biases[:, None, :]
+    queries = rotate(pre_all[0].reshape(head_shape), cosine, sine, 1.0).astype(jnp.bfloat16)
+    key_rows = rotate(pre_all[1].reshape(head_shape), cosine, sine, 1.0).astype(jnp.bfloat16)
+    value_rows = pre_all[2].reshape(head_shape).astype(jnp.bfloat16)
+    mixed, log_totals = lax.map(
+        lambda pieces: attend_forward(pieces, positions), (queries, key_rows, value_rows)
+    )
+    mixed_rows = mixed.reshape(rows, heads_width)
+    term = jnp.dot(mixed_rows, out_full, preferred_element_type=jnp.float32).astype(jnp.bfloat16)
+
+    gu_full, down_full, middle, gathered_two = call(
+        middle_kernel, "gather_second", 2,
+        (term, inputs, vectors, gate_pair, gate_up, down_weight),
+        [ANY, ANY, WHOLE, ANY, ANY, ANY],
+        [
+            bf16(2, width, hidden_width), bf16(hidden_width, width), f32(count, width),
+            bf16(rows, width),
+        ],
+        [
+            held(bf16(count, width)), held(bf16(2 * count, width)), held(bf16(2 * count, width)),
+            held(bf16(count, width)), held(f32(count, width)), held(bf16(count, width)),
+        ],
+        (48, 48, 24),
+    )
+    gate_act = jnp.dot(gathered_two, gu_full[0], preferred_element_type=jnp.float32)
+    up_act = jnp.dot(gathered_two, gu_full[1], preferred_element_type=jnp.float32)
+    sigmoid_gate = jax.nn.sigmoid(gate_act)
+    hidden = (gate_act * sigmoid_gate * up_act).astype(jnp.bfloat16)
+    out_term = jnp.dot(hidden, down_full, preferred_element_type=jnp.float32).astype(jnp.bfloat16)
+
+    def quarters(product):
+        return [product(k).astype(jnp.bfloat16) for k in range(4)]
+
+    down_parts = quarters(
+        lambda k: jnp.einsum(
+            "gf,gd->fd", hidden, width_part(gathered_cot, k), preferred_element_type=jnp.float32
+        )
+    )
+    grad_hidden = jnp.einsum(
+        "gd,fd->gf", gathered_cot, down_full, preferred_element_type=jnp.float32
+    )
+    grad_up = (grad_hidden * gate_act * sigmoid_gate).astype(jnp.bfloat16)
+    grad_gate = (
+        grad_hidden * up_act * sigmoid_gate * (1.0 + gate_act * (1.0 - sigmoid_gate))
+    ).astype(jnp.bfloat16)
+    second_term = (
+        jnp.einsum("gf,df->gd", grad_gate, gu_full[0], preferred_element_type=jnp.float32)
+        + jnp.einsum("gf,df->gd", grad_up, gu_full[1], preferred_element_type=jnp.float32)
+    ).astype(jnp.bfloat16)
+    gate_parts, up_parts = (
+        quarters(
+            lambda k: jnp.einsum(
+                "gd,gf->df",
+                width_part(gathered_two, k),
+                incoming,
+                preferred_element_type=jnp.float32,
+            )
+        )
+        for incoming in (grad_gate, grad_up)
+    )
+
+    by_rows = ((2 * EIGHTH, hidden_width), (EIGHTH, hidden_width))
+    by_columns = ((hidden_width, 2 * EIGHTH), (hidden_width, EIGHTH))
+    outputs, grad_middle, gathered_branch, sums, gu_owned, down_owned = call(
+        back_kernel, "scatter_first", 3,
+        (second_term, out_term, middle, cotangent, vectors, *down_parts, *gate_parts, *up_parts),
+        [ANY] * 4 + [WHOLE] + [ANY] * 12,
+        [
+            bf16(count, width), f32(count, width), bf16(rows, width), f32(8, width),
+            f32(2, EIGHTH, hidden_width), f32(hidden_width, EIGHTH),
+        ],
+        [
+            held(f32(count, width)), held(bf16(count, width)),
+            held(bf16(2 * count, width)), held(bf16(2 * count, width)), held(bf16(count, width)),
+            held(bf16(2 * count, width)), held(bf16(2 * count, width)), held(bf16(count, width)),
+            held(bf16(count, width)), held(f32(count, width)), held(f32(8, width)), held(f32(8, width)),
+            *weight_scratch(*by_columns), *weight_scratch(*by_rows), *weight_scratch(*by_rows),
+        ],
+        (64, 64, 48),
+    )
+
+    grad_mixed = jnp.einsum(
+        "gd,ed->ge", gathered_branch, out_full, preferred_element_type=jnp.float32
+    ).astype(jnp.bfloat16)
+    out_parts = quarters(
+        lambda k: jnp.einsum(
+            "ge,gd->ed",
+            mixed_rows,
+            width_part(gathered_branch, k),
+            preferred_element_type=jnp.float32,
+        )
+    )
+    grad_queries, grad_keys, grad_values = lax.map(
+        lambda pieces: attend_back(pieces, positions),
+        (queries, key_rows, value_rows, grad_mixed.reshape(head_shape), log_totals),
+    )
+    grad_queries = rotate(grad_queries, cosine, sine, -1.0)
+    grad_keys = rotate(grad_keys, cosine, sine, -1.0)
+    grad_pre = (
+        jnp.stack([grad_queries, grad_keys, grad_values])
+        .reshape(3, rows, heads_width)
+        .astype(jnp.bfloat16)
+    )
+    proj_parts = quarters(
+        lambda k: jnp.einsum(
+            "gd,jge->jde",
+            width_part(gathered_one, k),
+            grad_pre,
+            preferred_element_type=jnp.float32,
+        )
+    )
+    first_term = jnp.einsum(
+        "jge,jde->gd", grad_pre, proj_full, preferred_element_type=jnp.float32
+    ).astype(jnp.bfloat16)
+    bias_part = jnp.pad(jnp.sum(grad_pre, axis=1, dtype=jnp.float32), ((0, 5), (0, 0)))
+
+    by_rows = ((2 * EIGHTH, heads_width), (EIGHTH, heads_width))
+    by_columns = ((heads_width, 2 * EIGHTH), (heads_width, EIGHTH))
+    input_grads, proj_owned, out_owned, vector_grads, bias_grad = call(
+        last_kernel, "scatter_second", 4,
+        (first_term, inputs, vectors, grad_middle, sums, bias_part, *out_parts, *proj_parts),
+        [ANY, ANY, WHOLE, ANY, WHOLE, ANY] + [ANY] * 8,
+        [
+            f32(count, width), f32(3, EIGHTH, heads_width), f32(heads_width, EIGHTH),
+            f32(8, EIGHTH), f32(8, heads_width),
+        ],
+        [
+            held(bf16(count, width)), held(bf16(2 * count, width)), held(bf16(2 * count, width)),
+            held(bf16(count, width)), held(f32(count, width)), held(f32(8, width)), held(f32(8, width)),
+            held(f32(7, 8, EIGHTH)), held(f32(2, 8, EIGHTH)), held(f32(2, 8, EIGHTH)),
+            held(f32(8, heads_width)), held(f32(4, 8, heads_width)),
+            *weight_scratch(*by_columns),
+            *weight_scratch(*by_rows), *weight_scratch(*by_rows), *weight_scratch(*by_rows),
+        ],
+        (64, 64, 48),
+    )
+    return (
+        outputs,
+        input_grads,
+        vector_grads[0],
+        vector_grads[1],
+        proj_owned,
+        bias_grad[:3],
+        out_owned,
+        vector_grads[2],
+        vector_grads[3],
+        gu_owned,
+        down_owned,
+    )
+
+
 def solution(mesh):
+    whole_pairs = dict(mesh.shape) == {"dp": 8, "tensor": 4}
     return jax.shard_map(
-        local,
+        local_pairs if whole_pairs else local,
         mesh=mesh,
         in_specs=(
             P(("dp", "tensor"), None),

time: 1220 us -> 834 us (0.68)
  waiting for transfers between devices: 818 us -> 0.01 us
  Pallas kernels: 0 us -> 561 us
  blocking collectives: 80.4 us -> 0 us
  other arithmetic: 53.3 us -> 14.9 us
  between operations: 15 us -> 1.33 us
    pallas_call x0 -> x4, Pallas kernels: none -> 561 us  [call(): pl.pallas_call(body, out_shape=outs, in_specs=in_specs, out_specs=[ANY] *...]
    all_gather x8 -> x0, waiting for transfers between devices: 422 us -> none  [the longest x1 79.9 us: local(): lax.all_gather(normed_two.astype(jnp.bfloat16), 'tensor', axis=0, tiled=T...]
    reduce_scatter x8 -> x0, waiting for transfers between devices: 392 us -> none  [scatter_sum(): lax.psum_scatter(terms.astype(jnp.bfloat16), axis, scatter_dimension=dime...]
    psum x1 -> x0, blocking collectives: 45.3 us -> none  [local(): lax.psum((gain_one_part, shift_one_part, gain_two_part, shift_two_part, s...]
    all_gather x4 -> x0, blocking collectives: 35.1 us -> none  [the longest x1 9.39 us: local(): lax.all_gather(shift_first, 'dp', axis=0, tiled=True)]
    convert_element_type x12 -> x1, other arithmetic: 13.6 us -> 0.01 us  [local_pairs(): jnp.where(first_core, biases, own_quarter(biases)).astype(jnp.float32)]
    reduce_sum x8 -> x1, other arithmetic: 13.3 us -> 0.46 us  [local_pairs(): jnp.sum(grad_pre, axis=1, dtype=jnp.float32)]
    dot_general x15 -> x30, matrix products: 148 us -> 151 us  [the longest x8 24 us: local_pairs(): jnp.einsum('gd,gf->df', width_part(gathered_two, k), incoming, preferred_...]
  transfers between devices with their start and end apart: 16 -> 1, of which waited for: 14 -> 0; matrix products, arithmetic and copies ran while one was open for 19% -> 1% of each run, Pallas kernels for 0% -> 14%
where the time goes in v3:
time: 834 us; the launch traced here: 822 us
  Pallas kernels  561 us (67%)
  matrix products  177 us (21%)
  local copies, waits for them, and re-layouts  66.8 us (8%)
  other arithmetic  14.9 us (2%)
    pallas_call x4, Pallas kernels, call(): pl.pallas_call(body, out_shape=outs, in_specs=in_specs, out_specs=[ANY] *...  561 us
    dot_general x8, matrix products, local_pairs(): jnp.einsum('gd,gf->df', width_part(gathered_two, k), incoming, preferred_...  24 us
  transfers between devices with their start and end apart: 1, of which 0 were waited for; matrix products, arithmetic and copies ran while one was open for 1% of the time, Pallas kernels for 14%

profile of v3, /device:TPU:9, one launch (start us, length us, event | category | flops | bytes accessed | tf_op | source)
XLA Modules:
  0.0 822.0 jit_solution(16679027149760281810)
XLA Ops:
  5.7 112.5 %gather_first.1 = (bf16[3,2048,512]{2,1,0:T(8,128)(2,1)}, bf16[512,2048]{1,0:T(8,128)(2,1)}, bf16[2,256,1408]{2,1,0:T(8,128)(2,1)}, f32[8,2048]{1,0:T(8,128)}, b...) custom-call(bf16[256,2048]{1,0:T(8,128)(2,1)} %inputs.5, bf16[256,2048]{1,0:T(8,128)(2,1)} %cotangent.3, ...), custom_call_target="tpu_custom_call" | custom-call | bytes 36569088 | tf_op jit(solution)/shard_map/gather_first/pallas_call | solution.py:1013
  118.3 10.3 %add_bitcast_fusion = f32[3,1024,512]{1,2,0:T(8,128)S(1)} fusion(f32[3,512]{1,0:T(4,128)S(1)} %select_convert_fusion, bf16[3,2048,512]{2,1,0:T(8,128)(2,1)} %get-tuple-element.125, bf16[1024,2048]{1,0:T(8,128)(2,1)} %get-tuple-element.126), kind=kOutput, calls=%fused_computation.76 | convolution fusion | flops 6444023808 | bytes 16783360 | tf_op jit(solution)/shard_map/gd,jde->jge/dot_general | solution.py:1108
  130.5 4.0 reshape_squeeze.7
  149.1 14.2 %while.28 = (s32[]{:T(128)}, bf16[2,512,8,64]{1,3,2,0:T(8,128)(2,1)}, f32[2,8,512]{2,1,0:T(8,128)S(1)}, bf16[2,512,8,64]{1,3,2,0:T(8,128)(2,1)S(1)}, bf16[2,512,...) while((s32[]{:T(128)}, ...), condition=%wide.region_3.4_spmd.clone, body=%wide.region_0.3_spmd.clone.sunk | while | flops 562563584 | bytes 36837528 | solution.py:1113
  166.3 4.4 convolution_convert_fusion.1.term
  170.8 151.8 %gather_second.1 = (bf16[2,2048,1408]{2,1,0:T(8,128)(2,1)}, bf16[1408,2048]{1,0:T(8,128)(2,1)}, f32[256,2048]{1,0:T(8,128)}, bf16[1024,2048]{1,0:T(8,128)(2,1)}) custom-call(bf16[1024,2048]{1,0:T(8,128)(2,1)} %convolution_convert_fusion.1.term, bf16[256,2048]{1,0:T(8,128)(2,1)} %inputs.5, f32[8,2048]{1,0:T(8,128)} %get-tuple-element.129.vectors, ...), custom_call_target="tpu_custom_call" | custom-call | bytes 47185920 | tf_op jit(solution)/shard_map/gather_second/pallas_call | solution.py:1013
  322.7 11.9 %fusion.64 = f32[1024,1408]{1,0:T(8,128)} fusion(bf16[1024,2048]{1,0:T(8,128)(2,1)} %get-tuple-element.132, bf16[2,2048,1408]{2,1,0:T(8,128)(2,1)} %get-tuple-element.133), kind=kOutput, calls=%fused_computation.79 | convolution fusion | flops 5905580032 | bytes 15728640 | tf_op jit(solution)/shard_map/dot_general | solution.py:1133
  334.6 8.9 %fusion.122 = f32[1024,1408]{1,0:T(8,128)} fusion(bf16[1024,2048]{1,0:T(8,128)(2,1)S(1)} %copy-done.30, bf16[1408,2048]{1,0:T(8,128)(2,1)S(1)} %copy-done.27), kind=kOutput, calls=%fused_computation.189 | convolution fusion | flops 5905580032 | bytes 15728640 | tf_op jit(solution)/shard_map/gd,fd->gf/dot_general | solution.py:1147
  343.6 14.5 %multiply_convert_fusion.1 = (bf16[1024,1408]{1,0:T(8,128)(2,1)}, bf16[1024,1408]{1,0:T(8,128)(2,1)}, bf16[1024,1408]{1,0:T(8,128)(2,1)}) fusion(f32[1024,1408]{1,0:T(8,128)} %fusion.64, f32[1024,1408]{1,0:T(8,128)} %fusion.122, bf16[1024,2048]{1,0:T(8,128)(2,1)} %get-tuple-element.132, bf16[2,2048,1408]{2,1,0:T(8,128)(2,1)S(1)} %bitcast.211), kind=kOutput, calls=%fused_computation.85 | convolution fusion | flops 5928648704 | bytes 30146560 | tf_op jit(solution)/shard_map/dot_general | solution.py:1134
  358.1 11.0 %convolution_convert_fusion.out_term = bf16[1024,2048]{1,0:T(8,128)(2,1)} fusion(bf16[1024,1408]{1,0:T(8,128)(2,1)} %get-tuple-element.264, bf16[1408,2048]{1,0:T(8,128)(2,1)} %get-tuple-element.131), kind=kOutput, calls=%fused_computation.95 | convolution fusion | flops 5907677184 | bytes 12845056 | tf_op jit(solution)/shard_map/dot_general | solution.py:1137
  380.3 9.2 %fusion.62 = f32[1024,2048]{1,0:T(8,128)} fusion(bf16[1024,1408]{1,0:T(8,128)(2,1)S(1)} %copy-done.35, bf16[2,2048,1408]{2,1,0:T(8,128)(2,1)S(1)} %bitcast.211), kind=kOutput, calls=%fused_computation.77 | convolution fusion | flops 5905580032 | bytes 17039360 | tf_op jit(solution)/shard_map/gf,df->gd/dot_general | solution.py:1155
  389.5 3.0 convolution_convert_fusion.9.rest_4_
  398.5 3.1 convolution_convert_fusion.6.rest_7_
  401.5 3.0 convolution_convert_fusion.5.rest_8_
  410.5 3.0 convolution_convert_fusion.2.rest_11_
  413.5 10.9 %add_convert_fusion.term = bf16[1024,2048]{1,0:T(8,128)(2,1)} fusion(f32[1024,2048]{1,0:T(8,128)} %fusion.62, bf16[1024,1408]{1,0:T(8,128)(2,1)S(1)} %copy-done.34, bf16[2,2048,1408]{2,1,0:T(8,128)(2,1)S(1)} %bitcast.211), kind=kOutput, calls=%fused_computation.74 | convolution fusion | flops 5909774336 | bytes 21233664 | tf_op jit(solution)/shard_map/gf,df->gd/dot_general | solution.py:1156
  424.4 198.5 %scatter_first.1 = (bf16[256,2048]{1,0:T(8,128)(2,1)}, f32[256,2048]{1,0:T(8,128)}, bf16[1024,2048]{1,0:T(8,128)(2,1)}, f32[8,2048]{1,0:T(8,128)}, f32[2,256,1408]{2,1,0:T(8,128)}, /*index=5*/f32[1408,256]{1,0:T(8,128)}) custom-call(bf16[1024,2048]{1,0:T(8,128)(2,1)} %add_convert_fusion.term, bf16[1024,2048]{1,0:T(8,128)(2,1)} %convolution_convert_fusion.out_term, ...), custom_call_target="tpu_custom_call" | custom-call | bytes 23461888 | tf_op jit(solution)/shard_map/scatter_first/pallas_call | solution.py:1013
  622.9 5.2 convolution_convert_fusion.18
  632.7 27.0 %while.29 = (s32[]{:T(128)}, f32[2,512,8,64]{1,3,2,0:T(8,128)}, f32[2,512,8,64]{1,3,2,0:T(8,128)}, bf16[2,512,8,64]{1,3,2,0:T(8,128)(2,1)}, bf16[2,512,8,64]{1,3...) while((s32[]{:T(128)}, f32[2,512,8,64]{1,3,2,0:T(8,128)}, ...), condition=%wide.region_6.7_spmd.clone, body=%wide.region_4.6_spmd.clone.sunk | while | flops 1374423552 | bytes 117040456 | solution.py:1201
  681.3 11.5 %bitcast_convert_fusion.term = bf16[1024,2048]{1,0:T(8,128)(2,1)} fusion(bf16[3,1024,512]{2,1,0:T(8,128)(2,1)} %constant_dynamic-update-slice_fusion, bf16[3,2048,512]{2,1,0:T(8,128)(2,1)} %get-tuple-element.125), kind=kOutput, calls=%fused_computation.73 | convolution fusion | flops 6444548096 | bytes 13631488 | tf_op jit(solution)/shard_map/jge,jde->gd/dot_general | solution.py:1220
  699.3 3.0 fusion.78.rest_4_
  708.3 3.0 fusion.81.rest_7_
  711.9 98.2 %scatter_second.1 = (f32[256,2048]{1,0:T(8,128)}, f32[3,256,512]{2,1,0:T(8,128)}, f32[512,256]{1,0:T(8,128)}, f32[8,256]{1,0:T(8,128)}, f32[8,512]{1,0:T(8,128)}) custom-call(bf16[1024,2048]{1,0:T(8,128)(2,1)} %bitcast_convert_fusion.term, bf16[256,2048]{1,0:T(8,128)(2,1)} %inputs.5, f32[8,2048]{1,0:T(8,128)} %get-tuple-element.129.vectors, ...), custom_call_target="tpu_custom_call" | custom-call | bytes 8437760 | tf_op jit(solution)/shard_map/scatter_second/pallas_call | solution.py:1013
  813.9 3.3 copy.154
  (203 shorter events, 135.7 us)
Async XLA Ops:
  0.6 117.6 %copy-start.26 = (bf16[3,512]{1,0:T(4,128)(2,1)S(1)}, bf16[3,512]{1,0:T(4,128)(2,1)}, u32[]{:S(2)}) copy-start(bf16[3,512]{1,0:T(4,128)(2,1)} %param.19) | copy-start | bytes 9220
  0.7 117.6 %collective-permute-start = (bf16[3,512]{1,0:T(4,128)(2,1)}, bf16[3,512]{1,0:T(4,128)(2,1)S(1)}, u32[]{:S(2)}, u32[]{:S(2)}) collective-permute-start(bf16[3,512]{1,0:T(4,128)(2,1)} %param.19), channel_id=1, source_target_pairs={{0,6},{1,7},{2,4},{3,5},{4,0},{5,1},{6,2},{7,3},{8,14},{9,15},{10,... | collective-permute-start | bytes 9224 | tf_op jit(solution)/shard_map/ppermute | solution.py:285
  4.3 144.3 %copy-start.23 = (f32[512,8]{0,1:T(8,128)}, f32[512,8]{0,1:T(8,128)S(1)}, u32[]{:S(2)}) copy-start(f32[512,8]{0,1:T(8,128)S(1)} %get-tuple-element.293) | copy-start | bytes 49156
  141.8 5.9 copy-start.3
  143.7 4.9 copy-start.15
  163.3 7.5 copy-start
  322.6 12.0 %copy-start.27 = (bf16[1408,2048]{1,0:T(8,128)(2,1)S(1)}, bf16[1408,2048]{1,0:T(8,128)(2,1)}, u32[]{:S(2)}) copy-start(bf16[1408,2048]{1,0:T(8,128)(2,1)} %get-tuple-element.131) | copy-start | bytes 17301508
  322.7 11.9 %copy-start.30 = (bf16[1024,2048]{1,0:T(8,128)(2,1)S(1)}, bf16[1024,2048]{1,0:T(8,128)(2,1)}, u32[]{:S(2)}) copy-start(bf16[1024,2048]{1,0:T(8,128)(2,1)} %get-tuple-element.124) | copy-start | bytes 12582916
  322.7 20.9 %slice-start = ((s8[11534336]{0:T(1024)(128)(4,1)}), s8[4194304]{0:T(1024)(128)(4,1)S(1)}, s32[]{:S(2)}) async-start(s8[11534336]{0:T(1024)(128)(4,1)} %bitcast.210), calls=%async_computation | async-start | bytes 8388608
  322.7 20.9 %slice-start.1 = ((s8[11534336]{0:T(1024)(128)(4,1)}), s8[4194304]{0:T(1024)(128)(4,1)S(1)}, s32[]{:S(2)}) async-start(s8[11534336]{0:T(1024)(128)(4,1)} %bitcast.210), calls=%async_computation.1 | async-start | bytes 8388608
  334.6 9.0 %slice-start.2 = ((s8[11534336]{0:T(1024)(128)(4,1)}), s8[3145728]{0:T(1024)(128)(4,1)S(1)}, s32[]{:S(2)}) async-start(s8[11534336]{0:T(1024)(128)(4,1)} %bitcast.210), calls=%async_computation.2 | async-start | bytes 6291456
  358.1 11.1 %copy-start.31 = (bf16[1024,2048]{1,0:T(8,128)(2,1)S(1)}, bf16[1024,2048]{1,0:T(8,128)(2,1)}, u32[]{:S(2)}) copy-start(bf16[1024,2048]{1,0:T(8,128)(2,1)} %get-tuple-element.124) | copy-start | bytes 12582916
  358.1 11.1 %copy-start.36 = (bf16[1024,1408]{1,0:T(8,128)(2,1)S(1)}, bf16[1024,1408]{1,0:T(8,128)(2,1)}, u32[]{:S(2)}) copy-start(bf16[1024,1408]{1,0:T(8,128)(2,1)} %get-tuple-element.264) | copy-start | bytes 8650756
  380.3 9.2 %copy-start.32 = (bf16[1024,2048]{1,0:T(8,128)(2,1)S(1)}, bf16[1024,2048]{1,0:T(8,128)(2,1)}, u32[]{:S(2)}) copy-start(bf16[1024,2048]{1,0:T(8,128)(2,1)} %get-tuple-element.132) | copy-start | bytes 12582916
  395.5 6.1 copy-start.34
  632.7 31.0 %copy-start.24 = (f32[512,8]{0,1:T(8,128)S(1)}, f32[512,8]{0,1:T(8,128)}, u32[]{:S(2)}) copy-start(f32[512,8]{0,1:T(8,128)} %copy-done.23) | copy-start | bytes 49156
  632.7 31.0 %copy-start.25 = (f32[512,8]{0,1:T(8,128)S(1)}, f32[512,8]{0,1:T(8,128)}, u32[]{:S(2)}) copy-start(f32[512,8]{0,1:T(8,128)} %get-tuple-element.258) | copy-start | bytes 49156
  681.3 11.5 %copy-start.2 = (bf16[3,1024,512]{2,1,0:T(8,128)(2,1)S(1)}, bf16[3,1024,512]{2,1,0:T(8,128)(2,1)}, u32[]{:S(2)}) copy-start(bf16[3,1024,512]{2,1,0:T(8,128)(2,1)} %constant_dynamic-update-slice_fusion) | copy-start | bytes 9437188
  681.3 12.0 %copy-start.11 = (bf16[64,8,2,512]{3,1,2,0:T(8,128)(2,1)S(1)}, bf16[64,8,2,512]{3,1,2,0:T(8,128)(2,1)}, u32[]{:S(2)}) copy-start(bf16[64,8,2,512]{3,1,2,0:T(8,128)(2,1)} %copy-done.10) | copy-start | bytes 3145732
  681.3 12.0 %copy-start.29 = (bf16[1024,2048]{1,0:T(8,128)(2,1)S(1)}, bf16[1024,2048]{1,0:T(8,128)(2,1)}, u32[]{:S(2)}) copy-start(bf16[1024,2048]{1,0:T(8,128)(2,1)} %get-tuple-element.137) | copy-start | bytes 12582916
  711.9 101.0 %copy-start.12 = (bf16[256,2048]{1,0:T(8,128)(2,1)S(1)}, bf16[256,2048]{1,0:T(8,128)(2,1)}, u32[]{:S(2)}) copy-start(bf16[256,2048]{1,0:T(8,128)(2,1)} %get-tuple-element.477) | copy-start | bytes 3145732
  810.1 7.0 copy-start.6
  812.9 5.4 copy-start.22
  813.9 5.2 copy-start.5
  (26 other events, 57.6 us)

commit v4 on v3

--- a/solution.py
+++ b/solution.py
@@ -299,7 +299,7 @@
 ORDER = ((1, 0, 0), (1, 1, 0), (0, 1, 1), (1, 1, 1), (0, 0, 0), (0, 1, 0), (0, 0, 1), (1, 0, 1))
 EVEN_Y, EVEN_XY, ODD_X, ODD_XY, EVEN, EVEN_X, ODD, ODD_Y = range(8)
 ANY = pl.BlockSpec(memory_space=pl.ANY)
-VMEM_BYTES = 60 * 1024 * 1024
+VMEM_BYTES = 63 * 1024 * 1024
 
 
 class Place:
@@ -491,20 +491,17 @@
 
 
 class ScatterRows:
-    def __init__(self, place, term, near, got, got_beside):
-        self.place, self.term, self.near = place, term, near
+    def __init__(self, place, far, near, got, got_beside):
+        self.place, self.far, self.near = place, far, near
         self.got, self.got_beside = got, got_beside
-        self.count = term.shape[0] // 4
+        self.count = near.shape[0] // 2
 
     def start(self):
-        p, n = self.place, self.count
-        self.sibling = p.send(self.term.at[pl.ds(2 * n, 2 * n)], self.got, p.at(core=1)).start()
-        self.load = p.copy(self.term.at[pl.ds(0, 2 * n)], self.near).start()
+        self.sibling = self.place.send(self.far, self.got, self.place.at(core=1)).start()
         return self
 
     def relay(self):
         p, n = self.place, self.count
-        self.load.wait()
         self.sibling.arrived()
         late = pl.ds(n, n)
         combine(self.near.at[late], [self.near.at[late], self.got.at[late]], 32)
@@ -527,9 +524,10 @@
 
 
 class ScatterWeight:
-    def __init__(self, place, parts, rows, keep, got, last, home, result):
-        self.place, self.parts, self.rows = place, parts, rows
-        self.keep, self.got, self.last, self.home, self.result = keep, got, last, home, result
+    def __init__(self, place, send, keep, rows, got, last, home, result):
+        self.place, self.parts, self.keep, self.rows = place, send, keep, rows
+        self.got, self.last, self.home, self.result = got, last, home, result
+        self.loads = []
 
     def half(self, ref, k):
         if self.rows:
@@ -538,46 +536,54 @@
         size = ref.shape[1] // 2
         return ref.at[:, pl.ds(k * size, size)]
 
-    def start(self):
+    def load(self, sources):
+        self.loads = [self.place.copy(a, b).start() for a, b in zip(sources, self.keep)]
+        return self
+
+    def start_even(self):
         p = self.place
         self.even = p.send(self.parts[0], self.got.at[0], p.at(y=1)).start()
+        return self
+
+    def start_odd(self):
+        p = self.place
         self.odd = p.send(self.parts[1], self.got.at[1], p.at(x=1)).start()
-        self.loads = [p.copy(self.parts[2 + k], self.keep.at[k]).start() for k in (0, 1)]
-        return self
+        return self
+
+    def start(self):
+        return self.start_even().start_odd()
 
     def relay(self):
         p = self.place
+        wait_all(self.loads)
+        self.second = []
         for k, arrival in enumerate((self.even, self.odd)):
-            self.loads[k].wait()
             arrival.arrived()
-            there = self.half(self.keep.at[k], 1)
+            there = self.half(self.keep[k], 1)
             combine(there, [there, self.half(self.got.at[k], 1)], 64)
-            sent = p.send(there, self.last.at[k], p.at(x=1) if k == 0 else p.at(y=1)).start()
-            if k == 0:
-                self.even_last = sent
-            else:
-                self.odd_last = sent
+            device = p.at(x=1) if k == 0 else p.at(y=1)
+            self.second.append(p.send(there, self.last.at[k], device).start())
         return self
 
     def settle(self):
         p = self.place
-        self.even_last.arrived()
-        self.odd_last.arrived()
 
         def terms(k):
-            return [self.half(self.keep.at[k], 0), self.half(self.got.at[k], 0), self.last.at[k]]
-
-        even_out, odd_out = self.half(self.keep.at[0], 0), self.half(self.keep.at[1], 0)
+            return [self.half(self.keep[k], 0), self.half(self.got.at[k], 0), self.last.at[k]]
+
+        even_out, odd_out = self.half(self.keep[0], 0), self.half(self.keep[1], 0)
+        first, second = p.core == 0, p.core == 1
+        near_sem, far_sem = p.take("recv"), p.take("recv")
+        self.second[1].arrived()
         combine(odd_out, terms(1), 64)
-        first, second = p.core == 0, p.core == 1
+        self.to_sibling = p.send(odd_out, self.home.at[0], p.at(core=1), near_sem, first).start()
+        self.to_far = p.send(odd_out, self.home.at[1], p.at(far=1), far_sem, second).start()
+        self.second[0].arrived()
         pl.when(first)(lambda: combine(self.result, terms(0), 64))
         pl.when(second)(lambda: combine(even_out, terms(0), 64))
-        near_sem, far_sem = p.take("recv"), p.take("recv")
-        self.to_sibling = p.send(odd_out, self.home.at[0], p.at(core=1), near_sem, first).start()
         self.to_first = p.send(
             even_out, self.home.at[0], p.at(core=1, far=1), near_sem, second
         ).start()
-        self.to_far = p.send(odd_out, self.home.at[1], p.at(far=1), far_sem, second).start()
         return self
 
     def finish(self, output):
@@ -588,10 +594,7 @@
         pl.when(first)(lambda: combine(self.result, [self.result, self.home.at[0]], 64))
         pl.when(second)(lambda: combine(self.result, [self.home.at[0], self.home.at[1]], 64))
         self.store = p.copy(self.result, output).start()
-        for copy in (
-            self.even, self.odd, self.even_last, self.odd_last,
-            self.to_sibling, self.to_first, self.to_far,
-        ):
+        for copy in (self.even, self.odd, *self.second, self.to_sibling, self.to_first, self.to_far):
             copy.left()
 
     def stored(self):
@@ -723,60 +726,100 @@
     vector_store.wait()
 
 
+def tiles(count, tile, body):
+    @pl.loop(0, count // tile)
+    def _(i):
+        body(pl.ds(pl.multiple_of(i * tile, tile), tile))
+
+
+def shifted(rows, offset):
+    return pl.ds(pl.multiple_of(rows.start + offset, 256), rows.size)
+
+
+def dot(left, right, contract):
+    return lax.dot_general(
+        left, right, (((contract[0],), (contract[1],)), ((), ())), preferred_element_type=jnp.float32
+    )
+
+
 def middle_kernel(
     term, inputs, vectors, gate_pair, gate_up, down_weight,
-    gu_full, down_full, middle, rows_two,
-    own, near, got, got_beside, total, normed, send_sems, recv_sems, local_sems,
+    gu_full, down_full, middle, rows_two, hidden_out, gate_out, up_out,
+    own, near, got, got_beside, total, normed, gu_here, rows_here, gate_wide, hidden, gate_act, up_act,
+    send_sems, recv_sems, local_sems,
 ):
     p = Place(send_sems, recv_sems, local_sems)
+    count = own.shape[0]
     loads = load_local(p, inputs, own)
-    p.greet()
-    scatter = ScatterRows(p, term, near, got, got_beside).start()
+    near_load = p.copy(term.at[pl.ds(0, 2 * count)], near).start()
 
     def gu_block(j):
-        return lambda k: gu_full.at[j, pl.ds(k * EIGHTH, EIGHTH)]
+        return lambda k: gu_here.at[j, pl.ds(k * EIGHTH, EIGHTH)]
 
     gate = GatherWeight(p, None, gu_block(0))
     up = GatherWeight(p, gate_up.at[1], gu_block(1))
     down = GatherWeight(p, down_weight, lambda k: down_full.at[:, pl.ds(k * EIGHTH, EIGHTH)])
+    p.greet()
+    scatter = ScatterRows(p, term.at[pl.ds(2 * count, 2 * count)], near, got, got_beside).start()
     gate.spread(gate_pair.at[0], gate_pair.at[1])
     places = [
         p.copy(gate_pair.at[0], gate.block(EVEN)).start(),
         p.copy(gate_pair.at[1], gate.block(ODD)).start(),
     ]
     up.fetch()
+    near_load.wait()
     scatter.relay()
+    gate.relay()
+    up.fetched()
+    up.spread()
     wait_all(loads)
     scatter.arrived()
-    count = own.shape[0]
     gain, shift = vectors[2:3], vectors[3:4]
 
-    @pl.loop(0, count // CHUNK)
-    def _(i):
-        rows = pl.ds(pl.multiple_of(i * CHUNK, CHUNK), CHUNK)
+    def norm(rows):
         value = own[rows].astype(jnp.float32) + scatter.total(rows)
         total[rows] = value
         normed[rows] = norm_rows(value, gain, shift)[0].astype(normed.dtype)
 
-    gather = GatherRows(p, normed, rows_two).start()
-    store = p.copy(total, middle).start()
-    up.fetched()
+    tiles(count, CHUNK, norm)
+    gather = GatherRows(p, normed, rows_here).start()
+    stores = [p.copy(total, middle).start()]
     down.fetch()
-    up.spread()
-    gate.relay()
     gather.relay()
+    up.relay()
     down.fetched()
-    up.relay()
     down.spread()
+    gate.finish()
+    wait_all(places)
+    gather.finish()
+    stores.append(p.copy(rows_here, rows_two).start())
+    stores.append(p.copy(gu_here.at[0], gu_full.at[0]).start())
+
+    def gate_rows(rows):
+        gate_wide[rows] = dot(rows_here[rows], gu_here[0], (1, 0))
+
+    tiles(4 * count, 256, gate_rows)
+    up.finish()
+    stores.append(p.copy(gu_here.at[1], gu_full.at[1]).start())
+
+    def up_rows(rows):
+        wide_up = dot(rows_here[rows], gu_here[1], (1, 0))
+        wide_gate = gate_wide[rows]
+        hidden[rows] = (wide_gate * jax.nn.sigmoid(wide_gate) * wide_up).astype(hidden.dtype)
+        gate_act[rows] = wide_gate.astype(gate_act.dtype)
+        up_act[rows] = wide_up.astype(up_act.dtype)
+
+    tiles(2 * count, 256, up_rows)
     down.relay()
-    for weight in (gate, up, down):
-        weight.finish()
+    tiles(2 * count, 256, lambda rows: up_rows(shifted(rows, 2 * count)))
+    stores.append(p.copy(hidden, hidden_out).start())
+    stores.append(p.copy(gate_act, gate_out).start())
+    stores.append(p.copy(up_act, up_out).start())
+    down.finish()
     up.fetch_left()
     down.fetch_left()
     scatter.finish()
-    gather.finish()
-    wait_all(places)
-    store.wait()
+    wait_all(stores)
 
 
 def norm_back_rows(value, incoming, gain):
@@ -798,117 +841,195 @@
 
 
 def back_kernel(
-    term, out_term, middle, cotangent, vectors, *rest,
+    hidden_in, gate_in, up_in, cot_rows, rows_two, gu_full, down_full, middle, vectors,
+    outputs, grad_middle, rows_branch, sums, down_owned, gate_owned, up_parts, down_parts, gate_parts,
+    hidden, gate_act, up_act, cot, rows_here, gate, up, down, value, near, got, got_beside,
+    got_out, got_out_beside, gain_sum, shift_sum, staging,
+    down_got, down_last, down_home, down_result, gate_got, gate_last, gate_home,
+    send_sems, recv_sems, local_sems,
 ):
-    down_parts, gate_parts, up_parts = rest[0:4], rest[4:8], rest[8:12]
-    (
-        outputs, grad_middle, rows_branch, sums, gu_owned, down_owned,
-        value, own_cot, near, got, got_beside, near_out, got_out, got_out_beside, branch, result,
-        gain_sum, shift_sum,
-        d_keep, d_got, d_last, d_home, d_result,
-        g_keep, g_got, g_last, g_home, g_result,
-        u_keep, u_got, u_last, u_home, u_result,
-        send_sems, recv_sems, local_sems,
-    ) = rest[12:]
     p = Place(send_sems, recv_sems, local_sems)
-    cot_loads = load_local(p, cotangent, own_cot)
-    value_load = p.copy(middle, value).start()
+    count, width = value.shape
+    hidden_width = hidden.shape[1]
+    quarter = width // 4
+    first_loads = [p.copy(hidden_in, hidden).start(), p.copy(cot_rows, cot).start()]
+    second_loads = [
+        p.copy(down_full, down).start(), p.copy(gate_in, gate_act).start(), p.copy(up_in, up_act).start(),
+    ]
+    third_loads = [p.copy(gu_full.at[0], gate).start(), p.copy(gu_full.at[1], up).start()]
+    last_loads = [p.copy(rows_two, rows_here).start(), p.copy(middle, value).start()]
     p.greet()
-    scatter = ScatterRows(p, term, near, got, got_beside).start()
-    out_scatter = ScatterRows(p, out_term, near_out, got_out, got_out_beside)
-    down = ScatterWeight(p, down_parts, False, d_keep, d_got, d_last, d_home, d_result).start()
-    gate = ScatterWeight(p, gate_parts, True, g_keep, g_got, g_last, g_home, g_result)
-    up = ScatterWeight(p, up_parts, True, u_keep, u_got, u_last, u_home, u_result)
+    down_sum = ScatterWeight(
+        p, [down_parts.at[0], down_parts.at[1]], [staging.at[0], staging.at[1]], False,
+        down_got, down_last, down_home, down_result,
+    )
+    gate_sum = ScatterWeight(
+        p, [gate_parts.at[0], gate_parts.at[1]],
+        [gate.at[pl.ds(k * quarter, quarter)] for k in (2, 3)], True,
+        gate_got, gate_last, gate_home, value.at[:, pl.ds(0, hidden_width)],
+    )
+    far = cot.at[pl.ds(2 * count, 2 * count)]
+    scatter = ScatterRows(p, far, near, got, got_beside)
+    out_scatter = ScatterRows(p, far, near, got_out, got_out_beside)
+
+    def down_part(k):
+        columns = pl.ds(k * quarter, quarter)
+        staging[k % 2] = dot(hidden[...], cot[:, columns], (0, 0)).astype(staging.dtype)
+
+    wait_all(first_loads)
+    down_part(0)
+    store_even = p.copy(staging.at[0], down_parts.at[0]).start()
+    down_part(1)
+    store_odd = p.copy(staging.at[1], down_parts.at[1]).start()
+    store_even.wait()
+    down_sum.start_even()
+    down_part(2)
+    store_odd.wait()
+    down_sum.start_odd()
+    down_part(3)
+    wait_all(second_loads)
+
+    def hidden_back(rows):
+        grad = dot(cot[rows], down[...], (1, 1))
+        gate_value = gate_act[rows].astype(jnp.float32)
+        up_value = up_act[rows].astype(jnp.float32)
+        sigmoid = jax.nn.sigmoid(gate_value)
+        scaled = grad * sigmoid
+        up_act[rows] = (scaled * gate_value).astype(up_act.dtype)
+        gate_act[rows] = (
+            scaled * up_value * (1.0 + gate_value * (1.0 - sigmoid))
+        ).astype(gate_act.dtype)
+
+    tiles(4 * count, 256, hidden_back)
+    wait_all(third_loads)
+
+    def second_rows(target, offset):
+        def part(rows):
+            here = shifted(rows, offset)
+            target[rows] = (
+                dot(gate_act[here], gate[...], (1, 1)) + dot(up_act[here], up[...], (1, 1))
+            ).astype(target.dtype)
+
+        return part
+
+    tiles(2 * count, 256, second_rows(far, 2 * count))
+    scatter.start()
+    tiles(2 * count, 256, second_rows(near, 0))
     scatter.relay()
-    out_scatter.start()
-    wait_all(cot_loads)
-    value_load.wait()
+    wait_all(last_loads)
+
+    def weight_part(target, grads, k):
+        here = pl.ds(k * quarter, quarter)
+        target[here] = dot(rows_here[:, here], grads[...], (0, 0)).astype(target.dtype)
+
+    weight_part(gate, gate_act, 0)
+    even_store = p.copy(gate.at[pl.ds(0, quarter)], gate_parts.at[0]).start()
+    down_sum.relay()
+    weight_part(gate, gate_act, 1)
+    odd_store = p.copy(gate.at[pl.ds(quarter, quarter)], gate_parts.at[1]).start()
+    even_store.wait()
+    gate_sum.start_even()
     scatter.arrived()
-    out_scatter.relay()
-    count = value.shape[0]
+    odd_store.wait()
+    gate_sum.start_odd()
     gain = vectors[2:3]
     gain_sum[...] = jnp.zeros_like(gain_sum)
     shift_sum[...] = jnp.zeros_like(shift_sum)
 
-    @pl.loop(0, count // CHUNK)
-    def _(i):
-        rows = pl.ds(pl.multiple_of(i * CHUNK, CHUNK), CHUNK)
+    def middle_back(rows):
         incoming = scatter.total(rows)
         back, product = norm_back_rows(value[rows], incoming, gain)
         gain_sum[...] += fold(product)
         shift_sum[...] += fold(incoming)
-        grad = own_cot[rows].astype(jnp.float32) + back
-        result[rows] = grad
-        branch[rows] = grad.astype(branch.dtype)
-
-    gather = GatherRows(p, branch, rows_branch).start()
-    grad_store = p.copy(result, grad_middle).start()
+        grad = cot[rows].astype(jnp.float32) + back
+        value[rows] = grad
+        cot[rows] = grad.astype(cot.dtype)
+
+    tiles(count, CHUNK, middle_back)
+    gather = GatherRows(p, cot.at[pl.ds(0, count)], rows_branch).start()
+    grad_store = p.copy(value, grad_middle).start()
     gain_sum[0:1] = jnp.sum(gain_sum[...], axis=0, keepdims=True)
     gain_sum[1:2] = jnp.sum(shift_sum[...], axis=0, keepdims=True)
-    sum_store = p.copy(gain_sum, sums).start()
-    gate.start()
-    down.relay()
+    stores = [p.copy(gain_sum, sums).start()]
+    scatter.finish()
+
+    def out_rows(target, offset):
+        def part(rows):
+            target[rows] = dot(hidden[shifted(rows, offset)], down[...], (1, 0)).astype(target.dtype)
+
+        return part
+
+    tiles(2 * count, 256, out_rows(far, 2 * count))
+    out_scatter.start()
+    tiles(2 * count, 256, out_rows(near, 0))
+    down_sum.settle()
+    grad_store.wait()
+    middle_load = p.copy(middle, value).start()
+    weight_part(gate, gate_act, 2)
+    out_scatter.relay()
+    weight_part(gate, gate_act, 3)
+    gather.relay()
+    weight_part(up, up_act, 0)
+    weight_part(up, up_act, 1)
+    gate_sum.relay()
+    weight_part(up, up_act, 2)
+    weight_part(up, up_act, 3)
+    stores.append(p.copy(up, up_parts).start())
     out_scatter.arrived()
-
-    @pl.loop(0, count // CHUNK)
-    def _(i):
-        rows = pl.ds(pl.multiple_of(i * CHUNK, CHUNK), CHUNK)
-        own_cot[rows] = (value[rows] + out_scatter.total(rows)).astype(own_cot.dtype)
-
-    out_stores = store_natural(p, own_cot, outputs)
-    gather.relay()
-    up.start()
-    gate.relay()
-    down.settle()
-    up.relay()
-    gate.settle()
-    down.finish(down_owned)
-    up.settle()
-    gate.finish(gu_owned.at[0])
-    up.finish(gu_owned.at[1])
-    for weight in (down, gate, up):
-        weight.stored()
-    scatter.finish()
+    middle_load.wait()
+    own_out = cot.at[pl.ds(count, count)]
+
+    def out_total(rows):
+        own_out[rows] = (value[rows] + out_scatter.total(rows)).astype(own_out.dtype)
+
+    tiles(count, CHUNK, out_total)
+    stores += store_natural(p, own_out, outputs)
+    down_sum.finish(down_owned)
+    gate_sum.settle()
+    gate_sum.finish(gate_owned)
+    down_sum.stored()
+    gate_sum.stored()
     out_scatter.finish()
     gather.finish()
-    wait_all(out_stores)
-    grad_store.wait()
-    sum_store.wait()
+    wait_all(stores)
 
 
 def last_kernel(
     term, inputs, vectors, grad_middle, sums, bias_part, *rest,
 ):
-    out_parts, proj_parts = rest[0:4], rest[4:8]
+    up_parts, out_parts, proj_parts = rest[0], rest[1:5], rest[5:9]
+    input_grads, proj_owned, out_owned, vector_grads, bias_grad, up_owned = rest[9:15]
     (
-        input_grads, proj_owned, out_owned, vector_grads, bias_grad,
         own, near, got, got_beside, result, all_sums, shift_sum, vector_got, vector_total, z_got,
         bias_here, bias_got,
-        o_keep, o_got, o_last, o_home, o_result,
-        q_keep, q_got, q_last, q_home, q_result,
-        k_keep, k_got, k_last, k_home, k_result,
-        v_keep, v_got, v_last, v_home, v_result,
-        send_sems, recv_sems, local_sems,
-    ) = rest[8:]
+    ) = rest[15:27]
+    weight_refs = [rest[27 + 5 * k : 32 + 5 * k] for k in range(5)]
+    send_sems, recv_sems, local_sems = rest[52:]
     p = Place(send_sems, recv_sems, local_sems)
     loads = load_local(p, inputs, own)
     loads.append(p.copy(grad_middle, result).start())
     p.greet()
     first, second = p.core == 0, p.core == 1
-    scatter = ScatterRows(p, term, near, got, got_beside).start()
-    out = ScatterWeight(p, out_parts, False, o_keep, o_got, o_last, o_home, o_result).start()
+    count = own.shape[0]
+    near_load = p.copy(term.at[pl.ds(0, 2 * count)], near).start()
+    scatter = ScatterRows(p, term.at[pl.ds(2 * count, 2 * count)], near, got, got_beside).start()
+    quarter = up_parts.shape[0] // 4
+
+    def weight_sum(parts, rows, refs):
+        keep, got_quarters, last, home, total = refs
+        return ScatterWeight(
+            p, parts[:2], [keep.at[0], keep.at[1]], rows, got_quarters, last, home, total
+        ).load(parts[2:])
+
+    up = weight_sum(
+        [up_parts.at[pl.ds(k * quarter, quarter)] for k in range(4)], True, weight_refs[0]
+    ).start()
+    out = weight_sum(out_parts, False, weight_refs[1])
     thirds = [
-        ScatterWeight(p, [part.at[j] for part in proj_parts], True, *refs)
-        for j, refs in enumerate(
-            (
-                (q_keep, q_got, q_last, q_home, q_result),
-                (k_keep, k_got, k_last, k_home, k_result),
-                (v_keep, v_got, v_last, v_home, v_result),
-            )
-        )
+        weight_sum([part.at[j] for part in proj_parts], True, weight_refs[2 + j]) for j in range(3)
     ]
-    thirds[0].start()
     bias_load = p.copy(bias_part, bias_here).start()
+    near_load.wait()
     scatter.relay()
     bias_load.wait()
     bias_x = p.send(bias_here, bias_got.at[0], p.at(x=1)).start()
@@ -916,8 +1037,9 @@
     bias_x.left()
     bias_here[...] += bias_got[0]
     bias_y = p.send(bias_here, bias_got.at[1], p.at(y=1)).start()
-    out.relay()
-    thirds[1].start()
+    up.relay()
+    out.start()
+    thirds[0].start()
     bias_y.arrived()
     bias_y.left()
     bias_here[...] += bias_got[1]
@@ -929,7 +1051,6 @@
     ]
     wait_all(loads)
     scatter.arrived()
-    count = own.shape[0]
     gain = vectors[0:1]
     all_sums[...] = jnp.zeros_like(all_sums)
     shift_sum[...] = jnp.zeros_like(shift_sum)
@@ -964,8 +1085,9 @@
                     ).start()
                 )
                 n += 1
-    thirds[0].relay()
-    thirds[2].start()
+    out.relay()
+    thirds[1].start()
+    up.settle()
     own_slot = slots[(0, 0, 0)] + p.core * (slots[(0, 0, 1)] - slots[(0, 0, 0)])
     total = all_sums[:, pl.ds(pl.multiple_of(own_slot * EIGHTH, EIGHTH), EIGHTH)]
     for k, sent in enumerate(vector_sends):
@@ -973,6 +1095,8 @@
         total = total + vector_got[k]
     vector_total[0] = total
     z_near = p.send(vector_total.at[0], z_got.at[0], p.at(near=1)).start()
+    thirds[0].relay()
+    thirds[2].start()
     out.settle()
     z_near.arrived()
     vector_total[1] = total + z_got[0]
@@ -991,6 +1115,7 @@
     pl.when(second)(lambda: combine(bias_got.at[2], [bias_got.at[2], bias_got.at[3]], 8))
     pl.when(first)(lambda: combine(bias_got.at[2], [bias_got.at[2], bias_here], 8))
     bias_store = p.copy(bias_got.at[2], bias_grad).start()
+    up.finish(up_owned)
     thirds[2].relay()
     thirds[1].settle()
     out.finish(out_owned)
@@ -998,7 +1123,7 @@
     thirds[2].settle()
     thirds[1].finish(proj_owned.at[1])
     thirds[2].finish(proj_owned.at[2])
-    for weight in [out, *thirds]:
+    for weight in (up, out, *thirds):
         weight.stored()
     scatter.finish()
     for sent in vector_sends:
@@ -1116,73 +1241,51 @@
     mixed_rows = mixed.reshape(rows, heads_width)
     term = jnp.dot(mixed_rows, out_full, preferred_element_type=jnp.float32).astype(jnp.bfloat16)
 
-    gu_full, down_full, middle, gathered_two = call(
+    (
+        gu_full, down_full, middle, gathered_two, hidden, gate_act, up_act,
+    ) = call(
         middle_kernel, "gather_second", 2,
         (term, inputs, vectors, gate_pair, gate_up, down_weight),
         [ANY, ANY, WHOLE, ANY, ANY, ANY],
         [
             bf16(2, width, hidden_width), bf16(hidden_width, width), f32(count, width),
-            bf16(rows, width),
+            bf16(rows, width), *[bf16(rows, hidden_width)] * 3,
         ],
         [
             held(bf16(count, width)), held(bf16(2 * count, width)), held(bf16(2 * count, width)),
             held(bf16(count, width)), held(f32(count, width)), held(bf16(count, width)),
+            held(bf16(2, width, hidden_width)), held(bf16(rows, width)), held(f32(rows, hidden_width)),
+            *[held(bf16(rows, hidden_width))] * 3,
         ],
-        (48, 48, 24),
-    )
-    gate_act = jnp.dot(gathered_two, gu_full[0], preferred_element_type=jnp.float32)
-    up_act = jnp.dot(gathered_two, gu_full[1], preferred_element_type=jnp.float32)
-    sigmoid_gate = jax.nn.sigmoid(gate_act)
-    hidden = (gate_act * sigmoid_gate * up_act).astype(jnp.bfloat16)
-    out_term = jnp.dot(hidden, down_full, preferred_element_type=jnp.float32).astype(jnp.bfloat16)
+        (48, 48, 32),
+    )
 
     def quarters(product):
         return [product(k).astype(jnp.bfloat16) for k in range(4)]
 
-    down_parts = quarters(
-        lambda k: jnp.einsum(
-            "gf,gd->fd", hidden, width_part(gathered_cot, k), preferred_element_type=jnp.float32
-        )
-    )
-    grad_hidden = jnp.einsum(
-        "gd,fd->gf", gathered_cot, down_full, preferred_element_type=jnp.float32
-    )
-    grad_up = (grad_hidden * gate_act * sigmoid_gate).astype(jnp.bfloat16)
-    grad_gate = (
-        grad_hidden * up_act * sigmoid_gate * (1.0 + gate_act * (1.0 - sigmoid_gate))
-    ).astype(jnp.bfloat16)
-    second_term = (
-        jnp.einsum("gf,df->gd", grad_gate, gu_full[0], preferred_element_type=jnp.float32)
-        + jnp.einsum("gf,df->gd", grad_up, gu_full[1], preferred_element_type=jnp.float32)
-    ).astype(jnp.bfloat16)
-    gate_parts, up_parts = (
-        quarters(
-            lambda k: jnp.einsum(
-                "gd,gf->df",
-                width_part(gathered_two, k),
-                incoming,
-                preferred_element_type=jnp.float32,
-            )
-        )
-        for incoming in (grad_gate, grad_up)
-    )
-
     by_rows = ((2 * EIGHTH, hidden_width), (EIGHTH, hidden_width))
     by_columns = ((hidden_width, 2 * EIGHTH), (hidden_width, EIGHTH))
-    outputs, grad_middle, gathered_branch, sums, gu_owned, down_owned = call(
+    (
+        outputs, grad_middle, gathered_branch, sums, down_owned, gate_owned, up_parts, *_,
+    ) = call(
         back_kernel, "scatter_first", 3,
-        (second_term, out_term, middle, cotangent, vectors, *down_parts, *gate_parts, *up_parts),
-        [ANY] * 4 + [WHOLE] + [ANY] * 12,
+        (
+            hidden, gate_act, up_act, gathered_cot, gathered_two, gu_full, down_full, middle, vectors,
+        ),
+        [ANY] * 8 + [WHOLE],
         [
             bf16(count, width), f32(count, width), bf16(rows, width), f32(8, width),
-            f32(2, EIGHTH, hidden_width), f32(hidden_width, EIGHTH),
+            f32(hidden_width, EIGHTH), f32(EIGHTH, hidden_width), bf16(width, hidden_width),
+            bf16(2, hidden_width, 2 * EIGHTH), bf16(2, 2 * EIGHTH, hidden_width),
         ],
         [
-            held(f32(count, width)), held(bf16(count, width)),
-            held(bf16(2 * count, width)), held(bf16(2 * count, width)), held(bf16(count, width)),
-            held(bf16(2 * count, width)), held(bf16(2 * count, width)), held(bf16(count, width)),
-            held(bf16(count, width)), held(f32(count, width)), held(f32(8, width)), held(f32(8, width)),
-            *weight_scratch(*by_columns), *weight_scratch(*by_rows), *weight_scratch(*by_rows),
+            *[held(bf16(rows, hidden_width))] * 3, held(bf16(rows, width)), held(bf16(rows, width)),
+            held(bf16(width, hidden_width)), held(bf16(width, hidden_width)),
+            held(bf16(hidden_width, width)), held(f32(count, width)),
+            held(bf16(2 * count, width)), held(bf16(2 * count, width)),
+            held(bf16(count, width)), held(bf16(2 * count, width)), held(bf16(count, width)),
+            held(f32(8, width)), held(f32(8, width)), held(bf16(2, hidden_width, 2 * EIGHTH)),
+            *weight_scratch(*by_columns)[1:], *weight_scratch(*by_rows)[1:4],
         ],
         (64, 64, 48),
     )
@@ -1222,23 +1325,26 @@
     ).astype(jnp.bfloat16)
     bias_part = jnp.pad(jnp.sum(grad_pre, axis=1, dtype=jnp.float32), ((0, 5), (0, 0)))
 
-    by_rows = ((2 * EIGHTH, heads_width), (EIGHTH, heads_width))
-    by_columns = ((heads_width, 2 * EIGHTH), (heads_width, EIGHTH))
-    input_grads, proj_owned, out_owned, vector_grads, bias_grad = call(
+    third = ((2 * EIGHTH, heads_width), (EIGHTH, heads_width))
+    input_grads, proj_owned, out_owned, vector_grads, bias_grad, up_owned = call(
         last_kernel, "scatter_second", 4,
-        (first_term, inputs, vectors, grad_middle, sums, bias_part, *out_parts, *proj_parts),
-        [ANY, ANY, WHOLE, ANY, WHOLE, ANY] + [ANY] * 8,
+        (
+            first_term, inputs, vectors, grad_middle, sums, bias_part, up_parts, *out_parts,
+            *proj_parts,
+        ),
+        [ANY, ANY, WHOLE, ANY, WHOLE, ANY] + [ANY] * 9,
         [
             f32(count, width), f32(3, EIGHTH, heads_width), f32(heads_width, EIGHTH),
-            f32(8, EIGHTH), f32(8, heads_width),
+            f32(8, EIGHTH), f32(8, heads_width), f32(EIGHTH, hidden_width),
         ],
         [
             held(bf16(count, width)), held(bf16(2 * count, width)), held(bf16(2 * count, width)),
             held(bf16(count, width)), held(f32(count, width)), held(f32(8, width)), held(f32(8, width)),
             held(f32(7, 8, EIGHTH)), held(f32(2, 8, EIGHTH)), held(f32(2, 8, EIGHTH)),
             held(f32(8, heads_width)), held(f32(4, 8, heads_width)),
-            *weight_scratch(*by_columns),
-            *weight_scratch(*by_rows), *weight_scratch(*by_rows), *weight_scratch(*by_rows),
+            *weight_scratch(*by_rows),
+            *weight_scratch((heads_width, 2 * EIGHTH), (heads_width, EIGHTH)),
+            *weight_scratch(*third), *weight_scratch(*third), *weight_scratch(*third),
         ],
         (64, 64, 48),
     )
@@ -1252,7 +1358,7 @@
         out_owned,
         vector_grads[2],
         vector_grads[3],
-        gu_owned,
+        jnp.stack([gate_owned, up_owned]),
         down_owned,
     )
 

time: 834 us -> 739 us (0.89)
  matrix products: 177 us -> 77.3 us
    dot_general x18 -> x0, matrix products: 102 us -> none  [the longest x8 24 us: local_pairs(): jnp.einsum('gd,gf->df', width_part(gathered_two, k), incoming, preferred_...]
  transfers between devices with their start and end apart: 1 -> 1, of which waited for: 0 -> 0; matrix products, arithmetic and copies ran while one was open for 1% -> 1% of each run, Pallas kernels for 14% -> 15%
where the time goes in v4:
time: 739 us; the launch traced here: 726 us
  Pallas kernels  559 us (76%)
  matrix products  77.3 us (10%)
  local copies, waits for them, and re-layouts  67.4 us (9%)
  other arithmetic  19.5 us (3%)
    pallas_call x4, Pallas kernels, call(): pl.pallas_call(body, out_shape=outs, in_specs=in_specs, out_specs=[ANY] *...  559 us
    unnamed x66, local copies, waits for them, and re-layouts  16 us
  transfers between devices with their start and end apart: 1, of which 0 were waited for; matrix products, arithmetic and copies ran while one was open for 1% of the time, Pallas kernels for 15%

profile of v4, /device:TPU:9, one launch (start us, length us, event | category | flops | bytes accessed | tf_op | source)
XLA Modules:
  0.0 725.9 jit_solution(1861247083037231039)
XLA Ops:
  5.7 112.5 %gather_first.1 = (bf16[3,2048,512]{2,1,0:T(8,128)(2,1)}, bf16[512,2048]{1,0:T(8,128)(2,1)}, bf16[2,256,1408]{2,1,0:T(8,128)(2,1)}, f32[8,2048]{1,0:T(8,128)}, b...) custom-call(bf16[256,2048]{1,0:T(8,128)(2,1)} %inputs.5, bf16[256,2048]{1,0:T(8,128)(2,1)} %cotangent.1, ...), custom_call_target="tpu_custom_call" | custom-call | bytes 36569088 | tf_op jit(solution)/shard_map/gather_first/pallas_call | solution.py:1138
  118.3 10.3 %add_bitcast_fusion = f32[3,1024,512]{1,2,0:T(8,128)S(1)} fusion(f32[3,512]{1,0:T(4,128)S(1)} %select_convert_fusion, bf16[3,2048,512]{2,1,0:T(8,128)(2,1)} %get-tuple-element.129, bf16[1024,2048]{1,0:T(8,128)(2,1)} %get-tuple-element.130), kind=kOutput, calls=%fused_computation.75 | convolution fusion | flops 6444023808 | bytes 16783360 | tf_op jit(solution)/shard_map/gd,jde->jge/dot_general | solution.py:1233
  131.8 4.0 reshape_squeeze.8
  138.9 2.8 reshape_squeeze.7
  151.6 13.9 %while.28 = (s32[]{:T(128)}, bf16[2,512,8,64]{1,3,2,0:T(8,128)(2,1)}, f32[2,8,512]{2,1,0:T(8,128)S(1)}, bf16[2,512,8,64]{1,3,2,0:T(8,128)(2,1)S(1)}, bf16[2,512,...) while((s32[]{:T(128)}, ...), condition=%wide.region_3.4_spmd.clone, body=%wide.region_0.3_spmd.clone.sunk | while | flops 562563584 | bytes 28448856 | solution.py:1238
  155.5 3.2 fusion.135
  162.2 3.2 fusion.135
  165.5 3.3 copy.59
  169.0 4.4 convolution_convert_fusion.term
  173.5 143.6 %gather_second.1 = (bf16[2,2048,1408]{2,1,0:T(8,128)(2,1)}, bf16[1408,2048]{1,0:T(8,128)(2,1)}, f32[256,2048]{1,0:T(8,128)}, bf16[1024,2048]{1,0:T(8,128)(2,1)},...) custom-call(bf16[1024,2048]{1,0:T(8,128)(2,1)} %convolution_convert_fusion.term, ...), custom_call_target="tpu_custom_call" | custom-call | bytes 64487424 | tf_op jit(solution)/shard_map/gather_second/pallas_call | solution.py:1138
  317.0 157.0 %scatter_first.1 = (bf16[256,2048]{1,0:T(8,128)(2,1)}, f32[256,2048]{1,0:T(8,128)}, bf16[1024,2048]{1,0:T(8,128)(2,1)}, f32[8,2048]{1,0:T(8,128)}, f32[1408,256]...) custom-call(bf16[1024,1408]{1,0:T(8,128)(2,1)} %get-tuple-element.13, ...), custom_call_target="tpu_custom_call" | custom-call | bytes 43646976 | tf_op jit(solution)/shard_map/scatter_first/pallas_call | solution.py:1138
  474.1 5.2 convolution_convert_fusion.5
  484.1 28.0 %while.29 = (s32[]{:T(128)}, f32[2,512,8,64]{1,3,2,0:T(8,128)}, f32[2,512,8,64]{1,3,2,0:T(8,128)}, bf16[2,512,8,64]{1,3,2,0:T(8,128)(2,1)}, bf16[2,512,8,64]{1,3...) while((s32[]{:T(128)}, f32[2,512,8,64]{1,3,2,0:T(8,128)}, ...), condition=%wide.region_6.7_spmd.clone, body=%wide.region_4.6_spmd.clone.sunk | while | flops 1374423552 | bytes 108651784 | solution.py:1304
  485.7 2.9 multiply_reduce_fusion.2
  495.0 3.1 fusion.148
  499.7 2.9 multiply_reduce_fusion.2
  509.0 3.1 fusion.148
  538.0 5.3 fusion.67.rest_8_
  543.3 3.0 fusion.66.rest_7_
  546.3 3.0 fusion.65.rest_6_
  549.3 3.0 fusion.64.rest_5_
  558.4 8.5 %bitcast_convert_fusion.term = bf16[1024,2048]{1,0:T(8,128)(2,1)} fusion(bf16[3,1024,512]{2,1,0:T(8,128)(2,1)S(1)} %copy-done.6, bf16[3,2048,512]{2,1,0:T(8,128)(2,1)S(1)} %bitcast.181), kind=kOutput, calls=%fused_computation.73 | convolution fusion | flops 6444548096 | bytes 13631488 | tf_op jit(solution)/shard_map/jge,jde->gd/dot_general | solution.py:1323
  567.9 145.6 %scatter_second.1 = (f32[256,2048]{1,0:T(8,128)}, f32[3,256,512]{2,1,0:T(8,128)}, f32[512,256]{1,0:T(8,128)}, f32[8,256]{1,0:T(8,128)}, f32[8,512]{1,0:T(8,128)}, /*index=5*/f32[256,1408]{1,0:T(8,128)}) custom-call(bf16[1024,2048]{1,0:T(8,128)(2,1)} %bitcast_convert_fusion.term, bf16[256,2048]{1,0:T(8,128)(2,1)} %inputs.5, ...), custom_call_target="tpu_custom_call" | custom-call | bytes 11321344 | tf_op jit(solution)/shard_map/scatter_second/pallas_call | solution.py:1138
  716.4 3.7 pad_maximum_fusion
  (161 shorter events, 89.9 us)
Async XLA Ops:
  0.6 117.6 %copy-start.26 = (bf16[3,512]{1,0:T(4,128)(2,1)S(1)}, bf16[3,512]{1,0:T(4,128)(2,1)}, u32[]{:S(2)}) copy-start(bf16[3,512]{1,0:T(4,128)(2,1)} %param.19) | copy-start | bytes 9220
  0.7 117.6 %collective-permute-start = (bf16[3,512]{1,0:T(4,128)(2,1)}, bf16[3,512]{1,0:T(4,128)(2,1)S(1)}, u32[]{:S(2)}, u32[]{:S(2)}) collective-permute-start(bf16[3,512]{1,0:T(4,128)(2,1)} %param.19), channel_id=1, source_target_pairs={{0,6},{1,7},{2,4},{3,5},{4,0},{5,1},{6,2},{7,3},{8,14},{9,15},{10,... | collective-permute-start | bytes 9224 | tf_op jit(solution)/shard_map/ppermute | solution.py:285
  4.3 145.9 %copy-start.23 = (f32[512,8]{0,1:T(8,128)}, f32[512,8]{0,1:T(8,128)S(1)}, u32[]{:S(2)}) copy-start(f32[512,8]{0,1:T(8,128)S(1)} %get-tuple-element.300) | copy-start | bytes 49156
  128.6 3.3 copy-start.7
  165.5 8.0 %copy-start = (bf16[2,512,8,64]{1,3,2,0:T(8,128)(2,1)}, bf16[2,512,8,64]{1,3,2,0:T(8,128)(2,1)S(1)}, u32[]{:S(2)}) copy-start(bf16[2,512,8,64]{1,3,2,0:T(8,128)(2,1)S(1)} %get-tuple-element.495) | copy-start | bytes 3145732
  165.5 8.0 %copy-start.2 = (bf16[2,512,8,64]{1,3,2,0:T(8,128)(2,1)}, bf16[2,512,8,64]{1,3,2,0:T(8,128)(2,1)S(1)}, u32[]{:S(2)}) copy-start(bf16[2,512,8,64]{1,3,2,0:T(8,128)(2,1)S(1)} %get-tuple-element.496) | copy-start | bytes 3145732
  165.5 8.0 %copy-start.4 = (bf16[2,512,8,64]{1,3,2,0:T(8,128)(2,1)}, bf16[2,512,8,64]{1,3,2,0:T(8,128)(2,1)S(1)}, u32[]{:S(2)}) copy-start(bf16[2,512,8,64]{1,3,2,0:T(8,128)(2,1)S(1)} %get-tuple-element.497) | copy-start | bytes 3145732
  165.5 3.5 copy-start.29
  169.0 4.5 copy-start.14
  479.3 4.8 copy-start.1
  479.3 4.8 copy-start.3
  488.6 2.7 copy-start.20
  502.6 2.7 copy-start.20
  512.1 4.0 copy-start.24
  512.1 4.0 copy-start.25
  538.0 5.3 copy-start.6
  538.0 5.3 copy-start.27
  549.3 3.0 copy-start.15
  549.3 3.0 copy-start.28
  549.3 9.0 %slice-start = ((s8[6291456]{0:T(1024)(128)(4,1)}), s8[4194304]{0:T(1024)(128)(4,1)S(1)}, s32[]{:S(2)}) async-start(s8[6291456]{0:T(1024)(128)(4,1)} %bitcast.180), calls=%async_computation | async-start | bytes 8388608
  552.3 6.0 slice-start.1
  713.6 6.6 copy-start.13
  716.4 4.7 copy-start.10
  721.1 3.3 copy-start.12
  (14 other events, 24.9 us)

commit v5 on v4

--- a/solution.py
+++ b/solution.py
@@ -279,23 +279,6 @@
     )
 
 
-def send_between(array, routes):
-    tensor_ways = lax.axis_size("tensor")
-    pairs = [(d * tensor_ways + t, e * tensor_ways + s) for (d, t), (e, s) in routes]
-    return lax.ppermute(array, ("dp", "tensor"), pairs)
-
-
-def places():
-    return [(d, t) for d in range(lax.axis_size("dp")) for t in range(lax.axis_size("tensor"))]
-
-
-def own_quarter(array):
-    return send_between(
-        array,
-        [((d, t), (d ^ 1, t) if d & 1 else (d ^ 1, t ^ 2)) for d, t in places()],
-    )
-
-
 ORDER = ((1, 0, 0), (1, 1, 0), (0, 1, 1), (1, 1, 1), (0, 0, 0), (0, 1, 0), (0, 0, 1), (1, 0, 1))
 EVEN_Y, EVEN_XY, ODD_X, ODD_XY, EVEN, EVEN_X, ODD, ODD_Y = range(8)
 ANY = pl.BlockSpec(memory_space=pl.ANY)
@@ -634,19 +617,136 @@
         target[rows] = norm_rows(rows_of(rows), gain, shift)[0].astype(target.dtype)
 
 
-def front_kernel(
-    inputs, cotangent, vectors, projections, output_weight, gate_up,
-    proj_full, out_full, gate_pair, vectors_full, rows_one, rows_cot,
-    own, normed, own_cot, vectors_here, send_sems, recv_sems, local_sems,
+def tiles(count, tile, body):
+    @pl.loop(0, count // tile)
+    def _(i):
+        body(pl.ds(pl.multiple_of(i * tile, tile), tile))
+
+
+def shifted(rows, offset):
+    return pl.ds(pl.multiple_of(rows.start + offset, 256), rows.size)
+
+
+def dot(left, right, contract):
+    return lax.dot_general(
+        left, right, (((contract[0],), (contract[1],)), ((), ())), preferred_element_type=jnp.float32
+    )
+
+
+def turned(pre, tables, rows, sign):
+    cosine, sine_first, sine_latter = (table[rows] for table in tables)
+    return (
+        pre * cosine
+        + pltpu.roll(pre, 128 - ROTARY // 2, 1) * (sine_first * sign)
+        + pltpu.roll(pre, ROTARY // 2, 1) * (sine_latter * sign)
+    )
+
+
+def swapped_half(index, late):
+    sequence, half = index // 2, lax.rem(index, 2)
+    half = half + late * (1 - 2 * half)
+    return half, pl.ds(pl.multiple_of(sequence * SEQ_LEN + half * HALF, HALF), HALF)
+
+
+HALF = SEQ_LEN // 2
+
+
+def head_lanes(array, head):
+    lanes = lax.broadcasted_iota(jnp.int32, array.shape, 1)
+    mine = (lanes < HD) if head == 0 else (lanes >= HD)
+    return jnp.where(mine, array, jnp.zeros_like(array))
+
+
+def side_by_side(first, second):
+    lanes = lax.broadcasted_iota(jnp.int32, first.shape, 1)
+    return jnp.where(lanes < HD, first, second)
+
+
+def probabilities(queries, key_rows, half):
+    scores = dot(queries, key_rows, (1, 1))
+    row = lax.broadcasted_iota(jnp.int32, scores.shape, 0) + half * HALF
+    column = lax.broadcasted_iota(jnp.int32, scores.shape, 1)
+    scores = jnp.where(row >= column, scores, NEGATIVE)
+    exponent = jnp.exp(scores - jnp.max(scores, axis=-1, keepdims=True))
+    return exponent * (1.0 / jnp.sum(exponent, axis=-1, keepdims=True))
+
+
+def attend_pair(heads, mixed, late):
+    @pl.loop(0, 2 * heads.shape[2] // 128)
+    def _(step):
+        pairs = heads.shape[2] // 128
+        sequence, lanes = step // pairs, pl.ds(pl.multiple_of(lax.rem(step, pairs) * 128, 128), 128)
+        start = pl.multiple_of(sequence * SEQ_LEN, SEQ_LEN)
+        for half in (0, 1):
+            past = pl.ds(start, HALF * (half + 1))
+            queries = heads[0, pl.ds(start + half * HALF, HALF), lanes]
+            results = []
+            for head in (0, 1):
+                probs = probabilities(head_lanes(queries, head), heads[1, past, lanes], half)
+                results.append(dot(probs.astype(jnp.bfloat16), heads[2, past, lanes], (1, 0)))
+            _, rows = swapped_half(sequence * 2 + half, late)
+            mixed[rows, lanes] = side_by_side(*results).astype(mixed.dtype)
+
+
+def attend_pair_back(heads, grad_mixed, grad_pre, tables, late):
+    @pl.loop(0, 2 * heads.shape[2] // 128)
+    def _(step):
+        pairs = heads.shape[2] // 128
+        sequence, lanes = step // pairs, pl.ds(pl.multiple_of(lax.rem(step, pairs) * 128, 128), 128)
+        start = pl.multiple_of(sequence * SEQ_LEN, SEQ_LEN)
+        grads = [[None, None], [None, None]]
+        for half in (0, 1):
+            past = pl.ds(start, HALF * (half + 1))
+            here = pl.ds(start + half * HALF, HALF)
+            queries, incoming = heads[0, here, lanes], grad_mixed[here, lanes]
+            key_rows, value_rows = heads[1, past, lanes], heads[2, past, lanes]
+            found = []
+            for head in (0, 1):
+                probs = probabilities(head_lanes(queries, head), key_rows, half)
+                grad_values = dot(probs.astype(jnp.bfloat16), incoming, (0, 0))
+                grad_probs = dot(head_lanes(incoming, head), value_rows, (1, 1))
+                product = probs * grad_probs
+                grad_scores = product - probs * jnp.sum(product, axis=-1, keepdims=True)
+                grad_scores = grad_scores.astype(jnp.bfloat16)
+                grad_queries = dot(grad_scores, key_rows, (1, 0))
+                grad_keys = dot(grad_scores, queries, (0, 0))
+                found.append((grad_queries, grad_keys, grad_values))
+            grad_queries, grad_keys, grad_values = (side_by_side(*two) for two in zip(*found))
+            at_half = pl.ds(half * HALF, HALF)
+            _, rows = swapped_half(sequence * 2 + half, late)
+            grad_queries = turned(grad_queries * (1.0 / math.sqrt(HD)), tables, at_half, -1.0)
+            grad_pre[0, rows, lanes] = grad_queries.astype(grad_pre.dtype)
+            if half == 0:
+                early = (grad_keys, grad_values)
+            else:
+                whole = [grad_keys[:HALF] + early[0], grad_keys[HALF:]]
+                whole_values = [grad_values[:HALF] + early[1], grad_values[HALF:]]
+                for k in (0, 1):
+                    _, rows = swapped_half(sequence * 2 + k, late)
+                    turned_keys = turned(whole[k], tables, pl.ds(k * HALF, HALF), -1.0)
+                    grad_pre[1, rows, lanes] = turned_keys.astype(grad_pre.dtype)
+                    grad_pre[2, rows, lanes] = whole_values[k].astype(grad_pre.dtype)
+
+
+def forward_kernel(
+    inputs, cotangent, vectors, biases, cosine, sine_first, sine_latter,
+    projections, output_weight, gate_up, down_weight,
+    proj_full, out_full, gu_full, down_full, vectors_full, rows_one, rows_cot, heads_out, mixed_out,
+    middle, rows_two, hidden_out, gate_out, up_out,
+    own, normed, own_cot, vectors_here, biases_here, proj_here, out_here, rows_here, heads, mixed,
+    near, far, got, got_beside, total, rows_later, gu_here, gate_wide, hidden, gate_act, up_act,
+    send_sems, recv_sems, local_sems,
 ):
     p = Place(send_sems, recv_sems, local_sems)
+    count = own.shape[0]
+    late = lax.rem(p.tensor, 2)
+    tables = (cosine, sine_first, sine_latter)
     loads = load_local(p, inputs, own)
     cot_loads = load_local(p, cotangent, own_cot)
     p.greet()
     slots = {key: j for j, key in enumerate(ORDER)}
-    vector_sem = [p.take("recv") for _ in ORDER]
-    del vector_sem
-    vector_base = p.used["recv"] - len(ORDER)
+    vector_base = p.used["recv"]
+    p.used["recv"] += len(ORDER)
 
     def vector_copy(dy, dx, core):
         here, there = slots[(dy, dx, 0)], slots[(dy, dx, 1)]
@@ -665,19 +765,24 @@
     own_vectors = p.copy(
         vectors, vectors_here.at[:, pl.ds(pl.multiple_of(own_slot * EIGHTH, EIGHTH), EIGHTH)]
     ).start()
-
-    def quarter(j):
+    own_biases = p.copy(biases, biases_here, p.core == 0).start()
+    far_biases = p.send(biases, biases_here, p.at(core=1, far=1), when=p.core == 0).start()
+
+    def third(j):
         return GatherWeight(
-            p, projections.at[j], lambda k: proj_full.at[j, pl.ds(k * EIGHTH, EIGHTH)]
+            p, projections.at[j], lambda k: proj_here.at[j, pl.ds(k * EIGHTH, EIGHTH)]
         )
 
-    weights = [quarter(0), quarter(1), quarter(2)]
-    weights.append(
-        GatherWeight(p, output_weight, lambda k: out_full.at[:, pl.ds(k * EIGHTH, EIGHTH)])
-    )
-    gate = GatherWeight(p, gate_up.at[0], lambda k: gate_pair.at[k])
-    weights[0].fetch()
-    weights[1].fetch()
+    def gu_block(j):
+        return lambda k: gu_here.at[j, pl.ds(k * EIGHTH, EIGHTH)]
+
+    thirds = [third(0), third(1), third(2)]
+    out = GatherWeight(p, output_weight, lambda k: out_here.at[:, pl.ds(k * EIGHTH, EIGHTH)])
+    gate = GatherWeight(p, gate_up.at[0], gu_block(0))
+    up = GatherWeight(p, gate_up.at[1], gu_block(1))
+    down = GatherWeight(p, down_weight, lambda k: down_full.at[:, pl.ds(k * EIGHTH, EIGHTH)])
+    thirds[0].fetch()
+    thirds[1].fetch()
     wait_all(cot_loads)
     wait_all(loads)
     own_vectors.wait()
@@ -694,116 +799,104 @@
                 pltpu.make_async_copy(
                     vectors, vectors_here.at[:, pl.ds(0, EIGHTH)], recv_sems.at[vector_base + slot]
                 ).wait()
-    gain, shift = vectors_here[0:1], vectors_here[1:2]
-    norm_into(own.shape[0], lambda rows: own[rows].astype(jnp.float32), gain, shift, normed)
-    gather_one = GatherRows(p, normed, rows_one).start()
+    gain_one, shift_one = vectors_here[0:1], vectors_here[1:2]
+    norm_into(count, lambda rows: own[rows].astype(jnp.float32), gain_one, shift_one, normed)
+    gather_one = GatherRows(p, normed, rows_here).start()
     gather_cot = GatherRows(p, own_cot, rows_cot)
-    vector_store = p.copy(vectors_here, vectors_full).start()
-
-    weights[0].fetched().spread()
-    weights[2].fetch()
-    weights[1].fetched().spread()
-    weights[3].fetch()
-    weights[0].relay()
-    weights[2].fetched().spread()
+    stores = [p.copy(vectors_here, vectors_full).start()]
+
+    thirds[0].fetched().spread()
+    thirds[2].fetch()
+    thirds[1].fetched().spread()
+    out.fetch()
+    thirds[0].relay()
+    thirds[2].fetched().spread()
+    gate.fetch()
     gather_one.relay()
     gather_cot.start()
-    weights[1].relay()
-    gate.fetch(gate_pair.at[0], gate_pair.at[1])
-    weights[3].fetched().spread()
-    weights[2].relay()
-    weights[3].relay()
+    thirds[1].relay()
+    out.fetched().spread()
+    thirds[2].relay()
+    up.fetch()
+    own_biases.wait()
+    far_biases.arrived(p.core == 1)
+    far_biases.left()
+
+    def project(j):
+        thirds[j].finish()
+        stores.append(p.copy(proj_here.at[j], proj_full.at[j]).start())
+
+        @pl.loop(0, 4)
+        def _(index):
+            rows = pl.ds(pl.multiple_of(index * HALF, HALF), HALF)
+            half, target = swapped_half(index, late)
+            positions = pl.ds(pl.multiple_of(half * HALF, HALF), HALF)
+            pre = dot(rows_here[rows], proj_here[j], (1, 0)) + biases_here[j : j + 1]
+            for k in range(pre.shape[1] // 128):
+                lanes = slice(k * 128, (k + 1) * 128)
+                part = pre[:, lanes]
+                if j < 2:
+                    part = turned(part, tables, positions, 1.0)
+                if j == 0:
+                    part = part * (1.0 / math.sqrt(HD))
+                heads[j, target, lanes] = part.astype(heads.dtype)
+
+    gather_one.finish()
+    stores.append(p.copy(rows_here, rows_one).start())
+    project(0)
+    gate.fetched().spread()
+    project(1)
+    out.relay()
+    project(2)
     gather_cot.relay()
-    for weight in weights:
-        weight.finish()
-        weight.fetch_left()
-    gather_one.finish()
-    gather_cot.finish()
-    gate.fetched()
-    gate.fetch_left()
-    for sent in vector_sends:
-        sent.left()
-    vector_store.wait()
-
-
-def tiles(count, tile, body):
-    @pl.loop(0, count // tile)
-    def _(i):
-        body(pl.ds(pl.multiple_of(i * tile, tile), tile))
-
-
-def shifted(rows, offset):
-    return pl.ds(pl.multiple_of(rows.start + offset, 256), rows.size)
-
-
-def dot(left, right, contract):
-    return lax.dot_general(
-        left, right, (((contract[0],), (contract[1],)), ((), ())), preferred_element_type=jnp.float32
-    )
-
-
-def middle_kernel(
-    term, inputs, vectors, gate_pair, gate_up, down_weight,
-    gu_full, down_full, middle, rows_two, hidden_out, gate_out, up_out,
-    own, near, got, got_beside, total, normed, gu_here, rows_here, gate_wide, hidden, gate_act, up_act,
-    send_sems, recv_sems, local_sems,
-):
-    p = Place(send_sems, recv_sems, local_sems)
-    count = own.shape[0]
-    loads = load_local(p, inputs, own)
-    near_load = p.copy(term.at[pl.ds(0, 2 * count)], near).start()
-
-    def gu_block(j):
-        return lambda k: gu_here.at[j, pl.ds(k * EIGHTH, EIGHTH)]
-
-    gate = GatherWeight(p, None, gu_block(0))
-    up = GatherWeight(p, gate_up.at[1], gu_block(1))
-    down = GatherWeight(p, down_weight, lambda k: down_full.at[:, pl.ds(k * EIGHTH, EIGHTH)])
-    p.greet()
-    scatter = ScatterRows(p, term.at[pl.ds(2 * count, 2 * count)], near, got, got_beside).start()
-    gate.spread(gate_pair.at[0], gate_pair.at[1])
-    places = [
-        p.copy(gate_pair.at[0], gate.block(EVEN)).start(),
-        p.copy(gate_pair.at[1], gate.block(ODD)).start(),
-    ]
-    up.fetch()
-    near_load.wait()
+    stores.append(p.copy(heads, heads_out).start())
+    attend_pair(heads, mixed, late)
+    out.finish()
+    stores += [p.copy(out_here, out_full).start(), p.copy(mixed, mixed_out).start()]
+
+    def out_rows(target, offset):
+        def part(rows):
+            target[rows] = dot(mixed[shifted(rows, offset)], out_here[...], (1, 0)).astype(target.dtype)
+
+        return part
+
+    scatter = ScatterRows(p, far, near, got, got_beside)
+    tiles(2 * count, 256, out_rows(far, 2 * count))
+    scatter.start()
+    tiles(2 * count, 256, out_rows(near, 0))
     scatter.relay()
     gate.relay()
-    up.fetched()
-    up.spread()
-    wait_all(loads)
+    up.fetched().spread()
     scatter.arrived()
-    gain, shift = vectors[2:3], vectors[3:4]
+    gain_two, shift_two = vectors_here[2:3], vectors_here[3:4]
 
     def norm(rows):
         value = own[rows].astype(jnp.float32) + scatter.total(rows)
         total[rows] = value
-        normed[rows] = norm_rows(value, gain, shift)[0].astype(normed.dtype)
+        normed[rows] = norm_rows(value, gain_two, shift_two)[0].astype(normed.dtype)
 
     tiles(count, CHUNK, norm)
-    gather = GatherRows(p, normed, rows_here).start()
-    stores = [p.copy(total, middle).start()]
+    gather = GatherRows(p, normed, rows_later).start()
+    stores.append(p.copy(total, middle).start())
     down.fetch()
+    gather_cot.finish()
     gather.relay()
     up.relay()
-    down.fetched()
-    down.spread()
+    down.fetched().spread()
     gate.finish()
-    wait_all(places)
     gather.finish()
-    stores.append(p.copy(rows_here, rows_two).start())
+    stores.append(p.copy(rows_later, rows_two).start())
     stores.append(p.copy(gu_here.at[0], gu_full.at[0]).start())
 
     def gate_rows(rows):
-        gate_wide[rows] = dot(rows_here[rows], gu_here[0], (1, 0))
+        gate_wide[rows] = dot(rows_later[rows], gu_here[0], (1, 0))
 
     tiles(4 * count, 256, gate_rows)
     up.finish()
     stores.append(p.copy(gu_here.at[1], gu_full.at[1]).start())
 
     def up_rows(rows):
-        wide_up = dot(rows_here[rows], gu_here[1], (1, 0))
+        wide_up = dot(rows_later[rows], gu_here[1], (1, 0))
         wide_gate = gate_wide[rows]
         hidden[rows] = (wide_gate * jax.nn.sigmoid(wide_gate) * wide_up).astype(hidden.dtype)
         gate_act[rows] = wide_gate.astype(gate_act.dtype)
@@ -816,8 +909,10 @@
     stores.append(p.copy(gate_act, gate_out).start())
     stores.append(p.copy(up_act, up_out).start())
     down.finish()
-    up.fetch_left()
-    down.fetch_left()
+    for weight in (*thirds, out, gate, up, down):
+        weight.fetch_left()
+    for sent in vector_sends:
+        sent.left()
     scatter.finish()
     wait_all(stores)
 
@@ -995,51 +1090,111 @@
 
 
 def last_kernel(
-    term, inputs, vectors, grad_middle, sums, bias_part, *rest,
+    rows_branch, out_full, heads_in, mixed_in, rows_one, proj_full, inputs, vectors,
+    cosine, sine_first, sine_latter, grad_middle, sums, up_parts,
+    input_grads, proj_owned, out_owned, vector_grads, bias_grad, up_owned,
+    branch, out_here, heads, mixed, grad_mixed, grad_pre, rows_here, proj_here, out_send, proj_send,
+    own, got, got_beside, result, all_sums, shift_sum, vector_got, vector_total, z_got,
+    bias_here, bias_got, *rest,
 ):
-    up_parts, out_parts, proj_parts = rest[0], rest[1:5], rest[5:9]
-    input_grads, proj_owned, out_owned, vector_grads, bias_grad, up_owned = rest[9:15]
-    (
-        own, near, got, got_beside, result, all_sums, shift_sum, vector_got, vector_total, z_got,
-        bias_here, bias_got,
-    ) = rest[15:27]
-    weight_refs = [rest[27 + 5 * k : 32 + 5 * k] for k in range(5)]
-    send_sems, recv_sems, local_sems = rest[52:]
-    p = Place(send_sems, recv_sems, local_sems)
+    weight_refs = [rest[5 * k : 5 * k + 5] for k in range(5)]
+    p = Place(*rest[25:])
+    count, width = own.shape
+    quarter = width // 4
+    late = lax.rem(p.tensor, 2)
+    tables = (cosine, sine_first, sine_latter)
+    first, second = p.core == 0, p.core == 1
+    first_loads = [p.copy(rows_branch, branch).start(), p.copy(out_full, out_here).start()]
+    head_load = p.copy(heads_in, heads).start()
+    mixed_load = p.copy(mixed_in, mixed).start()
+    later_loads = [p.copy(proj_full, proj_here).start(), p.copy(rows_one, rows_here).start()]
     loads = load_local(p, inputs, own)
     loads.append(p.copy(grad_middle, result).start())
     p.greet()
-    first, second = p.core == 0, p.core == 1
-    count = own.shape[0]
-    near_load = p.copy(term.at[pl.ds(0, 2 * count)], near).start()
-    scatter = ScatterRows(p, term.at[pl.ds(2 * count, 2 * count)], near, got, got_beside).start()
-    quarter = up_parts.shape[0] // 4
-
-    def weight_sum(parts, rows, refs):
+
+    def weight_sum(send, rows, refs):
         keep, got_quarters, last, home, total = refs
         return ScatterWeight(
-            p, parts[:2], [keep.at[0], keep.at[1]], rows, got_quarters, last, home, total
-        ).load(parts[2:])
-
-    up = weight_sum(
-        [up_parts.at[pl.ds(k * quarter, quarter)] for k in range(4)], True, weight_refs[0]
-    ).start()
-    out = weight_sum(out_parts, False, weight_refs[1])
+            p, send, [keep.at[0], keep.at[1]], rows, got_quarters, last, home, total
+        )
+
+    up_quarters = [up_parts.at[pl.ds(k * quarter, quarter)] for k in range(4)]
+    up = weight_sum(up_quarters[:2], True, weight_refs[0]).load(up_quarters[2:]).start()
+    out = weight_sum([out_send.at[0], out_send.at[1]], False, weight_refs[1])
     thirds = [
-        weight_sum([part.at[j] for part in proj_parts], True, weight_refs[2 + j]) for j in range(3)
+        weight_sum([proj_send.at[j, 0], proj_send.at[j, 1]], True, weight_refs[2 + j])
+        for j in range(3)
     ]
-    bias_load = p.copy(bias_part, bias_here).start()
-    near_load.wait()
+    wait_all(first_loads)
+
+    @pl.loop(0, 4)
+    def _(index):
+        rows = pl.ds(pl.multiple_of(index * HALF, HALF), HALF)
+        _, target = swapped_half(index, late)
+        grad_mixed[target] = dot(branch[rows], out_here[...], (1, 1)).astype(grad_mixed.dtype)
+
+    mixed_load.wait()
+
+    def out_part(k):
+        target = out_send.at[k] if k < 2 else weight_refs[1][0].at[k - 2]
+        target[...] = dot(
+            mixed[...], branch[:, pl.ds(k * quarter, quarter)], (0, 0)
+        ).astype(target.dtype)
+
+    for k in range(4):
+        out_part(k)
+    out.start()
+    head_load.wait()
+    attend_pair_back(heads, grad_mixed, grad_pre, tables, late)
+    wait_all(later_loads)
+    up.relay()
+    near, far = branch.at[pl.ds(0, 2 * count)], branch.at[pl.ds(2 * count, 2 * count)]
+    scatter = ScatterRows(p, far, near, got, got_beside)
+
+    def term_rows(target, offset):
+        def part(rows):
+            here = shifted(rows, offset)
+            total = dot(grad_pre[0, here], proj_here[0], (1, 1))
+            for j in (1, 2):
+                total = total + dot(grad_pre[j, here], proj_here[j], (1, 1))
+            target[rows] = total.astype(target.dtype)
+
+        return part
+
+    def proj_part(j, k):
+        target = proj_send.at[j, k] if k < 2 else weight_refs[2 + j][0].at[k - 2]
+        target[...] = dot(
+            rows_here[:, pl.ds(k * quarter, quarter)], grad_pre[j], (0, 0)
+        ).astype(target.dtype)
+
+    tiles(2 * count, 256, term_rows(far, 2 * count))
+    scatter.start()
+    out.relay()
+    for j in range(3):
+        proj_part(j, 0)
+        thirds[j].start_even()
+        proj_part(j, 1)
+        thirds[j].start_odd()
+    tiles(2 * count, 256, term_rows(near, 0))
     scatter.relay()
-    bias_load.wait()
+
+    bias_here[...] = jnp.zeros_like(bias_here)
+    for j in range(3):
+        def bias_rows(rows):
+            bias_here[j : j + 1] += jnp.sum(
+                grad_pre[j, rows].astype(jnp.float32), axis=0, keepdims=True
+            )
+
+        tiles(4 * count, 256, bias_rows)
     bias_x = p.send(bias_here, bias_got.at[0], p.at(x=1)).start()
+    for j in range(3):
+        proj_part(j, 2)
+        proj_part(j, 3)
     bias_x.arrived()
     bias_x.left()
     bias_here[...] += bias_got[0]
     bias_y = p.send(bias_here, bias_got.at[1], p.at(y=1)).start()
-    up.relay()
-    out.start()
-    thirds[0].start()
+    up.settle()
     bias_y.arrived()
     bias_y.left()
     bias_here[...] += bias_got[1]
@@ -1050,27 +1205,26 @@
         p.send(bias_here, bias_got.at[3], p.at(far=1), far_sem, second).start(),
     ]
     wait_all(loads)
+    thirds[0].relay()
     scatter.arrived()
     gain = vectors[0:1]
     all_sums[...] = jnp.zeros_like(all_sums)
     shift_sum[...] = jnp.zeros_like(shift_sum)
 
-    @pl.loop(0, count // CHUNK)
-    def _(i):
-        rows = pl.ds(pl.multiple_of(i * CHUNK, CHUNK), CHUNK)
+    def first_back(rows):
         incoming = scatter.total(rows)
         back, product = norm_back_rows(own[rows].astype(jnp.float32), incoming, gain)
         all_sums[...] += fold(product)
         shift_sum[...] += fold(incoming)
         result[rows] = result[rows] + back
 
+    tiles(count, CHUNK, first_back)
     stores = store_natural(p, result, input_grads)
     all_sums[0:1] = jnp.sum(all_sums[...], axis=0, keepdims=True)
     all_sums[1:2] = jnp.sum(shift_sum[...], axis=0, keepdims=True)
     all_sums[2:4] = sums[0:2]
     slots = {key: j for j, key in enumerate(ORDER)}
     vector_sends = []
-    n = 0
     for dy in (0, 1):
         for dx in (0, 1):
             for core in (0, 1):
@@ -1081,13 +1235,12 @@
                 columns = pl.ds(pl.multiple_of(slot * EIGHTH, EIGHTH), EIGHTH)
                 vector_sends.append(
                     p.send(
-                        all_sums.at[:, columns], vector_got.at[n], p.at(x=dx, y=dy, core=core)
+                        all_sums.at[:, columns], vector_got.at[len(vector_sends)],
+                        p.at(x=dx, y=dy, core=core),
                     ).start()
                 )
-                n += 1
-    out.relay()
-    thirds[1].start()
-    up.settle()
+    out.settle()
+    thirds[1].relay()
     own_slot = slots[(0, 0, 0)] + p.core * (slots[(0, 0, 1)] - slots[(0, 0, 0)])
     total = all_sums[:, pl.ds(pl.multiple_of(own_slot * EIGHTH, EIGHTH), EIGHTH)]
     for k, sent in enumerate(vector_sends):
@@ -1095,14 +1248,12 @@
         total = total + vector_got[k]
     vector_total[0] = total
     z_near = p.send(vector_total.at[0], z_got.at[0], p.at(near=1)).start()
-    thirds[0].relay()
-    thirds[2].start()
-    out.settle()
+    thirds[0].settle()
+    thirds[2].relay()
     z_near.arrived()
-    vector_total[1] = total + z_got[0]
+    vector_total[1] = vector_total[0] + z_got[0]
     z_far = p.send(vector_total.at[1], z_got.at[1], p.at(far=1)).start()
-    thirds[1].relay()
-    thirds[0].settle()
+    thirds[1].settle()
     z_far.arrived()
     z_near.left()
     z_far.left()
@@ -1115,14 +1266,11 @@
     pl.when(second)(lambda: combine(bias_got.at[2], [bias_got.at[2], bias_got.at[3]], 8))
     pl.when(first)(lambda: combine(bias_got.at[2], [bias_got.at[2], bias_here], 8))
     bias_store = p.copy(bias_got.at[2], bias_grad).start()
+    thirds[2].settle()
     up.finish(up_owned)
-    thirds[2].relay()
-    thirds[1].settle()
     out.finish(out_owned)
-    thirds[0].finish(proj_owned.at[0])
-    thirds[2].settle()
-    thirds[1].finish(proj_owned.at[1])
-    thirds[2].finish(proj_owned.at[2])
+    for j in range(3):
+        thirds[j].finish(proj_owned.at[j])
     for weight in (up, out, *thirds):
         weight.stored()
     scatter.finish()
@@ -1192,76 +1340,54 @@
     down_weight,
     cotangent,
 ):
-    dp_index, tensor_index = lax.axis_index("dp"), lax.axis_index("tensor")
-    first_core = dp_index % 2 == 0
-    late_half = tensor_index % 2 == 1
     count, width = inputs.shape
     rows = 4 * count
     heads_width = output_weight.shape[0]
     hidden_width = down_weight.shape[0]
-    local_heads = heads_width // HD
-    head_shape = (2, SEQ_LEN, local_heads, HD)
-    quarter_width = width // 4
-
-    def width_part(array, k):
-        return array[:, k * quarter_width : (k + 1) * quarter_width]
-
-    positions = jnp.arange(SEQ_LEN)
-    positions = jnp.where(late_half, (positions + SEQ_LEN // 2) % SEQ_LEN, positions)
-    cosine, sine = (
-        jnp.where(late_half, jnp.roll(table, SEQ_LEN // 2, axis=0), table)
-        for table in angle_tables()
+    cosine, sine = angle_tables()
+    rest = ((0, 0), (0, HD - ROTARY))
+    cosine_table, sine_first, sine_latter = (
+        jnp.tile(jnp.pad(table, rest, constant_values=fill), (1, 128 // HD))
+        for table, fill in (
+            (jnp.concatenate([cosine, cosine], axis=1), 1.0),
+            (jnp.concatenate([-sine, jnp.zeros_like(sine)], axis=1), 0.0),
+            (jnp.concatenate([jnp.zeros_like(sine), sine], axis=1), 0.0),
+        )
     )
     vectors = jnp.pad(
         jnp.stack([gain_first, shift_first, gain_second, shift_second]).astype(jnp.float32),
         ((0, 4), (0, 0)),
     )
-    quarter_biases = jnp.where(first_core, biases, own_quarter(biases)).astype(jnp.float32)
-
-    proj_full, out_full, gate_pair, vectors, gathered_one, gathered_cot = call(
-        front_kernel, "gather_first", 1,
-        (inputs, cotangent, vectors, projections, output_weight, gate_up),
-        [ANY] * 6,
+    wide_biases = jnp.pad(biases.astype(jnp.float32), ((0, 5), (0, 0)))
+    wide = bf16(rows, width)
+    inner = bf16(rows, hidden_width)
+    own = bf16(count, width)
+    half_rows = bf16(2 * count, width)
+    (
+        proj_full, out_full, gu_full, down_full, vectors, gathered_one, gathered_cot, heads, mixed_rows,
+        middle, gathered_two, hidden, gate_act, up_act,
+    ) = call(
+        forward_kernel, "forward", 1,
+        (
+            inputs, cotangent, vectors, wide_biases, cosine_table, sine_first, sine_latter,
+            projections, output_weight, gate_up, down_weight,
+        ),
+        [ANY] * 4 + [WHOLE] * 3 + [ANY] * 4,
         [
-            bf16(3, width, heads_width), bf16(heads_width, width), bf16(2, EIGHTH, hidden_width),
-            f32(8, width), bf16(rows, width), bf16(rows, width),
-        ],
-        [held(bf16(count, width)), held(bf16(count, width)), held(bf16(count, width)), held(f32(8, width))],
-        (64, 64, 40),
-    )
-
-    pre_all = jnp.einsum("gd,jde->jge", gathered_one, proj_full, preferred_element_type=jnp.float32)
-    pre_all = pre_all + quarter_biases[:, None, :]
-    queries = rotate(pre_all[0].reshape(head_shape), cosine, sine, 1.0).astype(jnp.bfloat16)
-    key_rows = rotate(pre_all[1].reshape(head_shape), cosine, sine, 1.0).astype(jnp.bfloat16)
-    value_rows = pre_all[2].reshape(head_shape).astype(jnp.bfloat16)
-    mixed, log_totals = lax.map(
-        lambda pieces: attend_forward(pieces, positions), (queries, key_rows, value_rows)
-    )
-    mixed_rows = mixed.reshape(rows, heads_width)
-    term = jnp.dot(mixed_rows, out_full, preferred_element_type=jnp.float32).astype(jnp.bfloat16)
-
-    (
-        gu_full, down_full, middle, gathered_two, hidden, gate_act, up_act,
-    ) = call(
-        middle_kernel, "gather_second", 2,
-        (term, inputs, vectors, gate_pair, gate_up, down_weight),
-        [ANY, ANY, WHOLE, ANY, ANY, ANY],
-        [
-            bf16(2, width, hidden_width), bf16(hidden_width, width), f32(count, width),
-            bf16(rows, width), *[bf16(rows, hidden_width)] * 3,
+            bf16(3, width, heads_width), bf16(heads_width, width), bf16(2, width, hidden_width),
+            bf16(hidden_width, width), f32(8, width), wide, wide, bf16(3, rows, heads_width),
+            bf16(rows, heads_width), f32(count, width), wide, inner, inner, inner,
         ],
         [
-            held(bf16(count, width)), held(bf16(2 * count, width)), held(bf16(2 * count, width)),
-            held(bf16(count, width)), held(f32(count, width)), held(bf16(count, width)),
-            held(bf16(2, width, hidden_width)), held(bf16(rows, width)), held(f32(rows, hidden_width)),
-            *[held(bf16(rows, hidden_width))] * 3,
+            held(own), held(own), held(own), held(f32(8, width)), held(f32(8, heads_width)),
+            held(bf16(3, width, heads_width)), held(bf16(heads_width, width)), held(wide),
+            held(bf16(3, rows, heads_width)), held(bf16(rows, heads_width)),
+            held(half_rows), held(half_rows), held(half_rows), held(own), held(f32(count, width)),
+            held(wide), held(bf16(2, width, hidden_width)), held(f32(rows, hidden_width)),
+            held(inner), held(inner), held(inner),
         ],
-        (48, 48, 32),
-    )
-
-    def quarters(product):
-        return [product(k).astype(jnp.bfloat16) for k in range(4)]
+        (96, 96, 64),
+    )
 
     by_rows = ((2 * EIGHTH, hidden_width), (EIGHTH, hidden_width))
     by_columns = ((hidden_width, 2 * EIGHTH), (hidden_width, EIGHTH))
@@ -1290,56 +1416,25 @@
         (64, 64, 48),
     )
 
-    grad_mixed = jnp.einsum(
-        "gd,ed->ge", gathered_branch, out_full, preferred_element_type=jnp.float32
-    ).astype(jnp.bfloat16)
-    out_parts = quarters(
-        lambda k: jnp.einsum(
-            "ge,gd->ed",
-            mixed_rows,
-            width_part(gathered_branch, k),
-            preferred_element_type=jnp.float32,
-        )
-    )
-    grad_queries, grad_keys, grad_values = lax.map(
-        lambda pieces: attend_back(pieces, positions),
-        (queries, key_rows, value_rows, grad_mixed.reshape(head_shape), log_totals),
-    )
-    grad_queries = rotate(grad_queries, cosine, sine, -1.0)
-    grad_keys = rotate(grad_keys, cosine, sine, -1.0)
-    grad_pre = (
-        jnp.stack([grad_queries, grad_keys, grad_values])
-        .reshape(3, rows, heads_width)
-        .astype(jnp.bfloat16)
-    )
-    proj_parts = quarters(
-        lambda k: jnp.einsum(
-            "gd,jge->jde",
-            width_part(gathered_one, k),
-            grad_pre,
-            preferred_element_type=jnp.float32,
-        )
-    )
-    first_term = jnp.einsum(
-        "jge,jde->gd", grad_pre, proj_full, preferred_element_type=jnp.float32
-    ).astype(jnp.bfloat16)
-    bias_part = jnp.pad(jnp.sum(grad_pre, axis=1, dtype=jnp.float32), ((0, 5), (0, 0)))
-
     third = ((2 * EIGHTH, heads_width), (EIGHTH, heads_width))
     input_grads, proj_owned, out_owned, vector_grads, bias_grad, up_owned = call(
         last_kernel, "scatter_second", 4,
         (
-            first_term, inputs, vectors, grad_middle, sums, bias_part, up_parts, *out_parts,
-            *proj_parts,
+            gathered_branch, out_full, heads, mixed_rows, gathered_one, proj_full, inputs, vectors,
+            cosine_table, sine_first, sine_latter, grad_middle, sums, up_parts,
         ),
-        [ANY, ANY, WHOLE, ANY, WHOLE, ANY] + [ANY] * 9,
+        [ANY] * 7 + [WHOLE] * 4 + [ANY, WHOLE, ANY],
         [
             f32(count, width), f32(3, EIGHTH, heads_width), f32(heads_width, EIGHTH),
             f32(8, EIGHTH), f32(8, heads_width), f32(EIGHTH, hidden_width),
         ],
         [
-            held(bf16(count, width)), held(bf16(2 * count, width)), held(bf16(2 * count, width)),
-            held(bf16(count, width)), held(f32(count, width)), held(f32(8, width)), held(f32(8, width)),
+            held(wide), held(bf16(heads_width, width)), held(bf16(3, rows, heads_width)),
+            held(bf16(rows, heads_width)), held(bf16(rows, heads_width)),
+            held(bf16(3, rows, heads_width)), held(wide), held(bf16(3, width, heads_width)),
+            held(bf16(2, heads_width, 2 * EIGHTH)), held(bf16(3, 2, 2 * EIGHTH, heads_width)),
+            held(own), held(half_rows), held(own), held(f32(count, width)),
+            held(f32(8, width)), held(f32(8, width)),
             held(f32(7, 8, EIGHTH)), held(f32(2, 8, EIGHTH)), held(f32(2, 8, EIGHTH)),
             held(f32(8, heads_width)), held(f32(4, 8, heads_width)),
             *weight_scratch(*by_rows),

time: 739 us -> 623 us (0.84)
  the two profiles are of different devices: /device:TPU:9 before, /device:TPU:0 now
where the time goes in v5:
time: 623 us; the launch traced here: 616 us
  Pallas kernels  596 us (96%)
  local copies, waits for them, and re-layouts  13.3 us (2%)
    pallas_call x3, Pallas kernels, call(): pl.pallas_call(body, out_shape=outs, in_specs=in_specs, out_specs=[ANY] *...  596 us

profile of v5, /device:TPU:0, one launch (start us, length us, event | category | flops | bytes accessed | tf_op | source)
XLA Modules:
  0.0 615.6 jit_solution(18076698826770909574)
XLA Ops:
  0.7 0.7 stack.24
  1.3 0.7 stack.25
  2.0 0.7 stack.26
  2.6 0.7 stack.27
  3.3 0.6 fusion.7.vectors
  3.9 1.3 pad_convert_fusion.biases
  5.2 0.1 multiply_sine_fusion
  5.4 0.8 copy.23.sine_first
  6.3 0.8 copy.24.sine_latter
  7.1 0.8 copy.22.cosine
  8.0 254.6 %forward.1 = (bf16[3,2048,512]{2,1,0:T(8,128)(2,1)}, bf16[512,2048]{1,0:T(8,128)(2,1)}, bf16[2,2048,1408]{2,1,0:T(8,128)(2,1)}, bf16[1408,2048]{1,0:T(8,128)(2,1...) custom-call(bf16[256,2048]{1,0:T(8,128)(2,1)} %inputs.3, ...), custom_call_target="tpu_custom_call" | custom-call | bytes 106561536 | tf_op jit(solution)/shard_map/forward/pallas_call | solution.py:1286
  262.6 157.1 %scatter_first.1 = (bf16[256,2048]{1,0:T(8,128)(2,1)}, f32[256,2048]{1,0:T(8,128)}, bf16[1024,2048]{1,0:T(8,128)(2,1)}, f32[8,2048]{1,0:T(8,128)}, f32[1408,256]...) custom-call(bf16[1024,1408]{1,0:T(8,128)(2,1)} %get-tuple-element.38, ...), custom_call_target="tpu_custom_call" | custom-call | bytes 43646976 | tf_op jit(solution)/shard_map/scatter_first/pallas_call | solution.py:1286
  419.7 183.8 %scatter_second.1 = (f32[256,2048]{1,0:T(8,128)}, f32[3,256,512]{2,1,0:T(8,128)}, f32[512,256]{1,0:T(8,128)}, f32[8,256]{1,0:T(8,128)}, f32[8,512]{1,0:T(8,128)}, /*index=5*/f32[256,1408]{1,0:T(8,128)}) custom-call(bf16[1024,2048]{1,0:T(8,128)(2,1)} %get-tuple-element.48.rows_branch, bf16[512,2048]{1,0:T(8,128)(2,1)} %get-tuple-element.49.out_full, ...), custom_call_target="tpu_custom_call" | custom-call | bytes 11321344 | tf_op jit(solution)/shard_map/scatter_second/pallas_call | solution.py:1286
  603.5 1.4 fusion.9
  604.9 1.3 slice.17
  606.3 3.7 pad_maximum_fusion
  610.0 0.0 copy-done.3
  610.0 1.0 copy.33
  610.9 0.0 copy-done
  611.0 1.3 copy.34
  612.3 1.1 copy.35
  613.4 0.8 copy.36
  614.2 0.0 copy-done.2
  614.2 1.1 copy.37
  (15 shorter events, 0.1 us)
Async XLA Ops:
  606.3 3.7 copy-start.3
  606.3 4.7 copy-start
  610.0 2.3 copy-start.1
  611.0 2.5 copy-start.4
  612.3 2.0 copy-start.2

commit v6 on v5

--- a/solution.py
+++ b/solution.py
@@ -548,36 +548,55 @@
             self.second.append(p.send(there, self.last.at[k], device).start())
         return self
 
+    def gather(self):
+        for k in (1, 0):
+            self.second[k].arrived()
+            here = self.half(self.keep[k], 0)
+            combine(here, [here, self.half(self.got.at[k], 0), self.last.at[k]], 64)
+        return self
+
     def settle(self):
+        self.gather()
+        even, odd = self.half(self.keep[0], 0), self.half(self.keep[1], 0)
+        self.way_home = HomeSum(self.place, even, odd, even, self.home, self.result).start()
+        return self
+
+    def finish(self, output):
+        self.way_home.finish(output)
+        self.left()
+
+    def left(self):
+        for copy in (self.even, self.odd, *self.second):
+            copy.left()
+
+    def stored(self):
+        self.way_home.stored()
+
+
+class HomeSum:
+    def __init__(self, place, even, odd, here, home, result):
+        self.place, self.even, self.odd, self.here = place, even, odd, here
+        self.home, self.result = home, result
+
+    def start(self):
         p = self.place
-
-        def terms(k):
-            return [self.half(self.keep[k], 0), self.half(self.got.at[k], 0), self.last.at[k]]
-
-        even_out, odd_out = self.half(self.keep[0], 0), self.half(self.keep[1], 0)
         first, second = p.core == 0, p.core == 1
         near_sem, far_sem = p.take("recv"), p.take("recv")
-        self.second[1].arrived()
-        combine(odd_out, terms(1), 64)
-        self.to_sibling = p.send(odd_out, self.home.at[0], p.at(core=1), near_sem, first).start()
-        self.to_far = p.send(odd_out, self.home.at[1], p.at(far=1), far_sem, second).start()
-        self.second[0].arrived()
-        pl.when(first)(lambda: combine(self.result, terms(0), 64))
-        pl.when(second)(lambda: combine(even_out, terms(0), 64))
-        self.to_first = p.send(
-            even_out, self.home.at[0], p.at(core=1, far=1), near_sem, second
-        ).start()
+        home = self.home
+        self.to_sibling = p.send(self.odd, home.at[0], p.at(core=1), near_sem, first).start()
+        self.to_first = p.send(self.even, home.at[0], p.at(core=1, far=1), near_sem, second).start()
+        self.to_far = p.send(self.odd, home.at[1], p.at(far=1), far_sem, second).start()
         return self
 
     def finish(self, output):
-        p = self.place
+        p, home = self.place, self.home
         first, second = p.core == 0, p.core == 1
         self.to_sibling.arrived()
         self.to_far.arrived(second)
-        pl.when(first)(lambda: combine(self.result, [self.result, self.home.at[0]], 64))
-        pl.when(second)(lambda: combine(self.result, [self.home.at[0], self.home.at[1]], 64))
+        pl.when(first)(lambda: combine(self.result, [self.here, home.at[0]], 64))
+        pl.when(second)(lambda: combine(self.result, [home.at[0], home.at[1]], 64))
         self.store = p.copy(self.result, output).start()
-        for copy in (self.even, self.odd, *self.second, self.to_sibling, self.to_first, self.to_far):
+        for copy in (self.to_sibling, self.to_first, self.to_far):
             copy.left()
 
     def stored(self):
@@ -812,11 +831,11 @@
     thirds[0].relay()
     thirds[2].fetched().spread()
     gate.fetch()
-    gather_one.relay()
-    gather_cot.start()
     thirds[1].relay()
     out.fetched().spread()
     thirds[2].relay()
+    gather_one.relay()
+    gather_cot.start()
     up.fetch()
     own_biases.wait()
     far_biases.arrived(p.core == 1)
@@ -937,10 +956,10 @@
 
 def back_kernel(
     hidden_in, gate_in, up_in, cot_rows, rows_two, gu_full, down_full, middle, vectors,
-    outputs, grad_middle, rows_branch, sums, down_owned, gate_owned, up_parts, down_parts, gate_parts,
+    outputs, grad_middle, rows_branch, sums, down_owned, gate_sums, up_parts, down_parts,
     hidden, gate_act, up_act, cot, rows_here, gate, up, down, value, near, got, got_beside,
     got_out, got_out_beside, gain_sum, shift_sum, staging,
-    down_got, down_last, down_home, down_result, gate_got, gate_last, gate_home,
+    down_got, down_last, down_home, down_result, gate_got, gate_last,
     send_sems, recv_sems, local_sems,
 ):
     p = Place(send_sems, recv_sems, local_sems)
@@ -948,30 +967,28 @@
     hidden_width = hidden.shape[1]
     quarter = width // 4
     first_loads = [p.copy(hidden_in, hidden).start(), p.copy(cot_rows, cot).start()]
-    second_loads = [
-        p.copy(down_full, down).start(), p.copy(gate_in, gate_act).start(), p.copy(up_in, up_act).start(),
-    ]
-    third_loads = [p.copy(gu_full.at[0], gate).start(), p.copy(gu_full.at[1], up).start()]
-    last_loads = [p.copy(rows_two, rows_here).start(), p.copy(middle, value).start()]
     p.greet()
     down_sum = ScatterWeight(
         p, [down_parts.at[0], down_parts.at[1]], [staging.at[0], staging.at[1]], False,
         down_got, down_last, down_home, down_result,
     )
+    gate_quarters = [gate.at[pl.ds(k * quarter, quarter)] for k in range(4)]
     gate_sum = ScatterWeight(
-        p, [gate_parts.at[0], gate_parts.at[1]],
-        [gate.at[pl.ds(k * quarter, quarter)] for k in (2, 3)], True,
-        gate_got, gate_last, gate_home, value.at[:, pl.ds(0, hidden_width)],
+        p, gate_quarters[:2], gate_quarters[2:], True, gate_got, gate_last, None, None
     )
     far = cot.at[pl.ds(2 * count, 2 * count)]
     scatter = ScatterRows(p, far, near, got, got_beside)
-    out_scatter = ScatterRows(p, far, near, got_out, got_out_beside)
+    near_out = rows_here.at[pl.ds(0, 2 * count)]
+    out_scatter = ScatterRows(p, far, near_out, got_out, got_out_beside)
 
     def down_part(k):
         columns = pl.ds(k * quarter, quarter)
         staging[k % 2] = dot(hidden[...], cot[:, columns], (0, 0)).astype(staging.dtype)
 
     wait_all(first_loads)
+    second_loads = [
+        p.copy(down_full, down).start(), p.copy(gate_in, gate_act).start(), p.copy(up_in, up_act).start(),
+    ]
     down_part(0)
     store_even = p.copy(staging.at[0], down_parts.at[0]).start()
     down_part(1)
@@ -983,6 +1000,7 @@
     down_sum.start_odd()
     down_part(3)
     wait_all(second_loads)
+    third_loads = [p.copy(gu_full.at[0], gate).start(), p.copy(gu_full.at[1], up).start()]
 
     def hidden_back(rows):
         grad = dot(cot[rows], down[...], (1, 1))
@@ -997,6 +1015,7 @@
 
     tiles(4 * count, 256, hidden_back)
     wait_all(third_loads)
+    last_loads = [p.copy(rows_two, rows_here).start(), p.copy(middle, value).start()]
 
     def second_rows(target, offset):
         def part(rows):
@@ -1018,15 +1037,26 @@
         target[here] = dot(rows_here[:, here], grads[...], (0, 0)).astype(target.dtype)
 
     weight_part(gate, gate_act, 0)
-    even_store = p.copy(gate.at[pl.ds(0, quarter)], gate_parts.at[0]).start()
+    weight_part(gate, gate_act, 1)
     down_sum.relay()
-    weight_part(gate, gate_act, 1)
-    odd_store = p.copy(gate.at[pl.ds(quarter, quarter)], gate_parts.at[1]).start()
-    even_store.wait()
-    gate_sum.start_even()
+    gate_sum.start()
+    weight_part(gate, gate_act, 2)
+    weight_part(gate, gate_act, 3)
+
+    def out_rows(target, offset):
+        def part(rows):
+            target[rows] = dot(hidden[shifted(rows, offset)], down[...], (1, 0)).astype(target.dtype)
+
+        return part
+
+    for k in range(4):
+        weight_part(up, up_act, k)
+    stores = [p.copy(up, up_parts).start()]
+    scatter.sibling.left()
+    tiles(2 * count, 256, out_rows(far, 2 * count))
+    out_scatter.start()
+    tiles(2 * count, 256, out_rows(near_out, 0))
     scatter.arrived()
-    odd_store.wait()
-    gate_sum.start_odd()
     gain = vectors[2:3]
     gain_sum[...] = jnp.zeros_like(gain_sum)
     shift_sum[...] = jnp.zeros_like(shift_sum)
@@ -1045,34 +1075,17 @@
     grad_store = p.copy(value, grad_middle).start()
     gain_sum[0:1] = jnp.sum(gain_sum[...], axis=0, keepdims=True)
     gain_sum[1:2] = jnp.sum(shift_sum[...], axis=0, keepdims=True)
-    stores = [p.copy(gain_sum, sums).start()]
-    scatter.finish()
-
-    def out_rows(target, offset):
-        def part(rows):
-            target[rows] = dot(hidden[shifted(rows, offset)], down[...], (1, 0)).astype(target.dtype)
-
-        return part
-
-    tiles(2 * count, 256, out_rows(far, 2 * count))
-    out_scatter.start()
-    tiles(2 * count, 256, out_rows(near, 0))
-    down_sum.settle()
+    stores.append(p.copy(gain_sum, sums).start())
+    scatter.beside.left()
     grad_store.wait()
     middle_load = p.copy(middle, value).start()
-    weight_part(gate, gate_act, 2)
+    down_sum.settle()
+    gather.relay()
     out_scatter.relay()
-    weight_part(gate, gate_act, 3)
-    gather.relay()
-    weight_part(up, up_act, 0)
-    weight_part(up, up_act, 1)
     gate_sum.relay()
-    weight_part(up, up_act, 2)
-    weight_part(up, up_act, 3)
-    stores.append(p.copy(up, up_parts).start())
+    middle_load.wait()
     out_scatter.arrived()
-    middle_load.wait()
-    own_out = cot.at[pl.ds(count, count)]
+    own_out = near_out.at[pl.ds(0, count)]
 
     def out_total(rows):
         own_out[rows] = (value[rows] + out_scatter.total(rows)).astype(own_out.dtype)
@@ -1080,52 +1093,51 @@
     tiles(count, CHUNK, out_total)
     stores += store_natural(p, own_out, outputs)
     down_sum.finish(down_owned)
-    gate_sum.settle()
-    gate_sum.finish(gate_owned)
+    gate_sum.gather()
+    for k in (0, 1):
+        stores.append(p.copy(gate_sum.half(gate_quarters[2 + k], 0), gate_sums.at[k]).start())
+    gate_sum.left()
     down_sum.stored()
-    gate_sum.stored()
+    gather.finish()
     out_scatter.finish()
-    gather.finish()
     wait_all(stores)
 
 
 def last_kernel(
     rows_branch, out_full, heads_in, mixed_in, rows_one, proj_full, inputs, vectors,
-    cosine, sine_first, sine_latter, grad_middle, sums, up_parts,
-    input_grads, proj_owned, out_owned, vector_grads, bias_grad, up_owned,
-    branch, out_here, heads, mixed, grad_mixed, grad_pre, rows_here, proj_here, out_send, proj_send,
+    cosine, sine_first, sine_latter, grad_middle, sums, up_parts, gate_sums,
+    input_grads, proj_owned, out_owned, vector_grads, bias_grad, gu_owned,
+    branch, out_here, heads, mixed, grad_mixed, grad_pre, rows_here, proj_here, out_send,
     own, got, got_beside, result, all_sums, shift_sum, vector_got, vector_total, z_got,
-    bias_here, bias_got, *rest,
+    bias_here, bias_got, gate_home, gate_even, up_result, out_result, third_result, *rest,
 ):
-    weight_refs = [rest[5 * k : 5 * k + 5] for k in range(5)]
-    p = Place(*rest[25:])
+    weight_refs = [rest[4 * k : 4 * k + 4] for k in range(5)]
+    p = Place(*rest[20:])
     count, width = own.shape
     quarter = width // 4
     late = lax.rem(p.tensor, 2)
     tables = (cosine, sine_first, sine_latter)
     first, second = p.core == 0, p.core == 1
     first_loads = [p.copy(rows_branch, branch).start(), p.copy(out_full, out_here).start()]
-    head_load = p.copy(heads_in, heads).start()
-    mixed_load = p.copy(mixed_in, mixed).start()
-    later_loads = [p.copy(proj_full, proj_here).start(), p.copy(rows_one, rows_here).start()]
-    loads = load_local(p, inputs, own)
-    loads.append(p.copy(grad_middle, result).start())
     p.greet()
 
-    def weight_sum(send, rows, refs):
-        keep, got_quarters, last, home, total = refs
+    def weight_sum(send, rows, refs, total):
+        keep, got_quarters, last, home = refs
         return ScatterWeight(
             p, send, [keep.at[0], keep.at[1]], rows, got_quarters, last, home, total
         )
 
     up_quarters = [up_parts.at[pl.ds(k * quarter, quarter)] for k in range(4)]
-    up = weight_sum(up_quarters[:2], True, weight_refs[0]).load(up_quarters[2:]).start()
-    out = weight_sum([out_send.at[0], out_send.at[1]], False, weight_refs[1])
+    up = weight_sum(up_quarters[:2], True, weight_refs[0], up_result).start()
+    gate = HomeSum(p, gate_sums.at[0], gate_sums.at[1], gate_even, gate_home, up_result).start()
+    out = weight_sum([out_send.at[0], out_send.at[1]], False, weight_refs[1], out_result)
+    proj_send = [[heads.at[j, pl.ds(k * quarter, quarter)] for k in (0, 1)] for j in range(3)]
     thirds = [
-        weight_sum([proj_send.at[j, 0], proj_send.at[j, 1]], True, weight_refs[2 + j])
-        for j in range(3)
+        weight_sum(proj_send[j], True, weight_refs[2 + j], third_result.at[j]) for j in range(3)
     ]
     wait_all(first_loads)
+    mixed_load = p.copy(mixed_in, mixed).start()
+    head_load = p.copy(heads_in, heads).start()
 
     @pl.loop(0, 4)
     def _(index):
@@ -1143,8 +1155,12 @@
 
     for k in range(4):
         out_part(k)
-    out.start()
     head_load.wait()
+    later_loads = [p.copy(proj_full, proj_here).start(), p.copy(rows_one, rows_here).start()]
+    loads = load_local(p, inputs, own)
+    loads.append(p.copy(grad_middle, result).start())
+    gate_load = p.copy(gate_sums.at[0], gate_even).start()
+    up.load(up_quarters[2:])
     attend_pair_back(heads, grad_mixed, grad_pre, tables, late)
     wait_all(later_loads)
     up.relay()
@@ -1162,21 +1178,26 @@
         return part
 
     def proj_part(j, k):
-        target = proj_send.at[j, k] if k < 2 else weight_refs[2 + j][0].at[k - 2]
+        target = proj_send[j][k] if k < 2 else weight_refs[2 + j][0].at[k - 2]
         target[...] = dot(
             rows_here[:, pl.ds(k * quarter, quarter)], grad_pre[j], (0, 0)
         ).astype(target.dtype)
 
     tiles(2 * count, 256, term_rows(far, 2 * count))
     scatter.start()
-    out.relay()
+    tiles(2 * count, 256, term_rows(near, 0))
+    scatter.relay()
+    out.start()
     for j in range(3):
         proj_part(j, 0)
-        thirds[j].start_even()
         proj_part(j, 1)
-        thirds[j].start_odd()
-    tiles(2 * count, 256, term_rows(near, 0))
-    scatter.relay()
+    up.settle()
+    thirds[0].start()
+    for j in range(3):
+        proj_part(j, 2)
+        proj_part(j, 3)
+    out.relay()
+    thirds[1].start()
 
     bias_here[...] = jnp.zeros_like(bias_here)
     for j in range(3):
@@ -1187,14 +1208,12 @@
 
         tiles(4 * count, 256, bias_rows)
     bias_x = p.send(bias_here, bias_got.at[0], p.at(x=1)).start()
-    for j in range(3):
-        proj_part(j, 2)
-        proj_part(j, 3)
     bias_x.arrived()
     bias_x.left()
     bias_here[...] += bias_got[0]
     bias_y = p.send(bias_here, bias_got.at[1], p.at(y=1)).start()
-    up.settle()
+    gate_load.wait()
+    gate.finish(gu_owned.at[0])
     bias_y.arrived()
     bias_y.left()
     bias_here[...] += bias_got[1]
@@ -1204,8 +1223,10 @@
         p.send(bias_here, bias_got.at[2], p.at(core=1, far=1), near_sem, second).start(),
         p.send(bias_here, bias_got.at[3], p.at(far=1), far_sem, second).start(),
     ]
+    thirds[0].relay()
+    thirds[2].start()
+    out.settle()
     wait_all(loads)
-    thirds[0].relay()
     scatter.arrived()
     gain = vectors[0:1]
     all_sums[...] = jnp.zeros_like(all_sums)
@@ -1239,8 +1260,8 @@
                         p.at(x=dx, y=dy, core=core),
                     ).start()
                 )
-    out.settle()
     thirds[1].relay()
+    thirds[0].settle()
     own_slot = slots[(0, 0, 0)] + p.core * (slots[(0, 0, 1)] - slots[(0, 0, 0)])
     total = all_sums[:, pl.ds(pl.multiple_of(own_slot * EIGHTH, EIGHTH), EIGHTH)]
     for k, sent in enumerate(vector_sends):
@@ -1248,12 +1269,12 @@
         total = total + vector_got[k]
     vector_total[0] = total
     z_near = p.send(vector_total.at[0], z_got.at[0], p.at(near=1)).start()
-    thirds[0].settle()
     thirds[2].relay()
+    thirds[1].settle()
     z_near.arrived()
     vector_total[1] = vector_total[0] + z_got[0]
     z_far = p.send(vector_total.at[1], z_got.at[1], p.at(far=1)).start()
-    thirds[1].settle()
+    thirds[2].settle()
     z_far.arrived()
     z_near.left()
     z_far.left()
@@ -1266,8 +1287,8 @@
     pl.when(second)(lambda: combine(bias_got.at[2], [bias_got.at[2], bias_got.at[3]], 8))
     pl.when(first)(lambda: combine(bias_got.at[2], [bias_got.at[2], bias_here], 8))
     bias_store = p.copy(bias_got.at[2], bias_grad).start()
-    thirds[2].settle()
-    up.finish(up_owned)
+    gate.stored()
+    up.finish(gu_owned.at[1])
     out.finish(out_owned)
     for j in range(3):
         thirds[j].finish(proj_owned.at[j])
@@ -1319,7 +1340,7 @@
 def weight_scratch(quarter, eighth):
     return [
         held(bf16(2, *quarter)), held(bf16(2, *quarter)), held(bf16(2, *eighth)),
-        held(bf16(2, *eighth)), held(f32(*eighth)),
+        held(bf16(2, *eighth)),
     ]
 
 
@@ -1392,51 +1413,53 @@
     by_rows = ((2 * EIGHTH, hidden_width), (EIGHTH, hidden_width))
     by_columns = ((hidden_width, 2 * EIGHTH), (hidden_width, EIGHTH))
     (
-        outputs, grad_middle, gathered_branch, sums, down_owned, gate_owned, up_parts, *_,
+        outputs, grad_middle, gathered_branch, sums, down_owned, gate_sums, up_parts, _,
     ) = call(
-        back_kernel, "scatter_first", 3,
+        back_kernel, "backward_first", 2,
         (
             hidden, gate_act, up_act, gathered_cot, gathered_two, gu_full, down_full, middle, vectors,
         ),
         [ANY] * 8 + [WHOLE],
         [
-            bf16(count, width), f32(count, width), bf16(rows, width), f32(8, width),
-            f32(hidden_width, EIGHTH), f32(EIGHTH, hidden_width), bf16(width, hidden_width),
-            bf16(2, hidden_width, 2 * EIGHTH), bf16(2, 2 * EIGHTH, hidden_width),
+            own, f32(count, width), wide, f32(8, width), f32(hidden_width, EIGHTH),
+            bf16(2, EIGHTH, hidden_width), bf16(width, hidden_width),
+            bf16(2, hidden_width, 2 * EIGHTH),
         ],
         [
-            *[held(bf16(rows, hidden_width))] * 3, held(bf16(rows, width)), held(bf16(rows, width)),
+            held(inner), held(inner), held(inner), held(wide), held(wide),
             held(bf16(width, hidden_width)), held(bf16(width, hidden_width)),
             held(bf16(hidden_width, width)), held(f32(count, width)),
-            held(bf16(2 * count, width)), held(bf16(2 * count, width)),
-            held(bf16(count, width)), held(bf16(2 * count, width)), held(bf16(count, width)),
+            held(half_rows), held(half_rows), held(own), held(half_rows), held(own),
             held(f32(8, width)), held(f32(8, width)), held(bf16(2, hidden_width, 2 * EIGHTH)),
-            *weight_scratch(*by_columns)[1:], *weight_scratch(*by_rows)[1:4],
+            *weight_scratch(*by_columns)[1:], held(f32(hidden_width, EIGHTH)),
+            *weight_scratch(*by_rows)[1:3],
         ],
         (64, 64, 48),
     )
-
     third = ((2 * EIGHTH, heads_width), (EIGHTH, heads_width))
-    input_grads, proj_owned, out_owned, vector_grads, bias_grad, up_owned = call(
-        last_kernel, "scatter_second", 4,
+    input_grads, proj_owned, out_owned, vector_grads, bias_grad, gu_owned = call(
+        last_kernel, "backward_last", 3,
         (
             gathered_branch, out_full, heads, mixed_rows, gathered_one, proj_full, inputs, vectors,
-            cosine_table, sine_first, sine_latter, grad_middle, sums, up_parts,
+            cosine_table, sine_first, sine_latter, grad_middle, sums, up_parts, gate_sums,
         ),
-        [ANY] * 7 + [WHOLE] * 4 + [ANY, WHOLE, ANY],
+        [ANY] * 7 + [WHOLE] * 4 + [ANY, WHOLE, ANY, ANY],
         [
             f32(count, width), f32(3, EIGHTH, heads_width), f32(heads_width, EIGHTH),
-            f32(8, EIGHTH), f32(8, heads_width), f32(EIGHTH, hidden_width),
+            f32(8, EIGHTH), f32(8, heads_width), f32(2, EIGHTH, hidden_width),
         ],
         [
             held(wide), held(bf16(heads_width, width)), held(bf16(3, rows, heads_width)),
             held(bf16(rows, heads_width)), held(bf16(rows, heads_width)),
             held(bf16(3, rows, heads_width)), held(wide), held(bf16(3, width, heads_width)),
-            held(bf16(2, heads_width, 2 * EIGHTH)), held(bf16(3, 2, 2 * EIGHTH, heads_width)),
+            held(bf16(2, heads_width, 2 * EIGHTH)),
             held(own), held(half_rows), held(own), held(f32(count, width)),
             held(f32(8, width)), held(f32(8, width)),
             held(f32(7, 8, EIGHTH)), held(f32(2, 8, EIGHTH)), held(f32(2, 8, EIGHTH)),
             held(f32(8, heads_width)), held(f32(4, 8, heads_width)),
+            held(bf16(2, EIGHTH, hidden_width)), held(bf16(EIGHTH, hidden_width)),
+            held(f32(EIGHTH, hidden_width)), held(f32(heads_width, EIGHTH)),
+            held(f32(3, EIGHTH, heads_width)),
             *weight_scratch(*by_rows),
             *weight_scratch((heads_width, 2 * EIGHTH), (heads_width, EIGHTH)),
             *weight_scratch(*third), *weight_scratch(*third), *weight_scratch(*third),
@@ -1453,7 +1476,7 @@
         out_owned,
         vector_grads[2],
         vector_grads[3],
-        jnp.stack([gate_owned, up_owned]),
+        gu_owned,
         down_owned,
     )
 

time: 623 us -> 556 us (0.89)
  the two profiles are of different devices: /device:TPU:0 before, /device:TPU:1 now
where the time goes in v6:
time: 556 us; the launch traced here: 548 us
  Pallas kernels  527 us (95%)
  local copies, waits for them, and re-layouts  17.9 us (3%)
    pallas_call x3, Pallas kernels, call(): pl.pallas_call(body, out_shape=outs, in_specs=in_specs, out_specs=[ANY] *...  527 us

profile of v6, /device:TPU:1, one launch (start us, length us, event | category | flops | bytes accessed | tf_op | source)
XLA Modules:
  0.0 548.5 jit_solution(5791999007044337286)
XLA Ops:
  0.7 0.7 stack.15
  1.3 0.7 stack.16
  2.0 0.7 stack.17
  2.6 0.7 stack.18
  3.3 0.6 fusion.7.vectors
  3.9 1.3 pad_convert_fusion.biases
  5.2 0.1 multiply_sine_fusion
  5.4 0.8 copy.23.sine_first
  6.3 0.8 copy.24.sine_latter
  7.1 0.8 copy.22.cosine
  8.0 254.0 %forward.1 = (bf16[3,2048,512]{2,1,0:T(8,128)(2,1)}, bf16[512,2048]{1,0:T(8,128)(2,1)}, bf16[2,2048,1408]{2,1,0:T(8,128)(2,1)}, bf16[1408,2048]{1,0:T(8,128)(2,1...) custom-call(bf16[256,2048]{1,0:T(8,128)(2,1)} %inputs.3, ...), custom_call_target="tpu_custom_call" | custom-call | bytes 106561536 | tf_op jit(solution)/shard_map/forward/pallas_call | solution.py:1307
  262.0 127.0 %backward_first.1 = (bf16[256,2048]{1,0:T(8,128)(2,1)}, f32[256,2048]{1,0:T(8,128)}, bf16[1024,2048]{1,0:T(8,128)(2,1)}, f32[8,2048]{1,0:T(8,128)}, f32[1408,256...) custom-call(bf16[1024,1408]{1,0:T(8,128)(2,1)} %get-tuple-element.38.hidden, ...), custom_call_target="tpu_custom_call" | custom-call | bytes 37879808 | tf_op jit(solution)/shard_map/backward_first/pallas_call | solution.py:1307
  389.0 146.4 %backward_last.1 = (f32[256,2048]{1,0:T(8,128)}, f32[3,256,512]{2,1,0:T(8,128)}, f32[512,256]{1,0:T(8,128)}, f32[8,256]{1,0:T(8,128)}, f32[8,512]{1,0:T(8,128)}, /*index=5*/f32[2,256,1408]{2,1,0:T(8,128)}) custom-call(bf16[1024,2048]{1,0:T(8,128)(2,1)} %get-tuple-element.48.rows_branch, bf16[512,2048]{1,0:T(8,128)(2,1)} %get-tuple-element.49.out_full, ...), custom_call_target="tpu_custom_call" | custom-call | bytes 14204928 | tf_op jit(solution)/shard_map/backward_last/pallas_call | solution.py:1307
  535.4 1.5 fusion.9
  536.9 1.3 slice.17
  538.2 2.4 copy.34
  540.6 1.3 copy.35
  542.0 1.1 copy.36
  543.1 0.0 copy-done.4
  543.1 0.8 copy.37
  543.9 0.6 copy-done
  544.6 1.6 copy.38
  546.1 0.8 copy-done.3
  547.0 1.1 copy.39
  (15 shorter events, 0.1 us)
Async XLA Ops:
  535.4 5.2 copy-start.1
  538.2 3.8 copy-start.2
  540.6 2.5 copy-start.4
  542.0 2.6 copy-start
  544.5 2.4 copy-start.3

commit v7 on v6

--- a/solution.py
+++ b/solution.py
@@ -302,7 +302,7 @@
         dp = self.dp
         dp = dp + x * (2 - 4 * self.x) + y * (4 - 8 * self.y) + core * (1 - 2 * self.core)
         tensor = self.tensor
-        tensor = tensor + near * (1 - 2 * lax.rem(tensor, 2)) + far * (2 - 4 * (tensor // 2))
+        tensor = tensor + near * (1 - 2 * lax.rem(tensor, 2)) + far * (3 - 2 * tensor)
         return (dp, tensor)
 
     def column(self, key):
@@ -378,15 +378,13 @@
 
 
 class GatherWeight:
-    def __init__(self, place, shard, block, pair=None):
+    def __init__(self, place, shard, block):
         self.place, self.shard, self.block = place, shard, block
-        self.sent = []
-        self.pair = pair
-
-    def fetch(self, even=None, odd=None):
+        self.spreads, self.arrivals = [], {}
+
+    def fetch(self):
         p = self.place
-        even = self.block(EVEN) if even is None else even
-        odd = self.block(ODD) if odd is None else odd
+        even, odd = self.block(EVEN), self.block(ODD)
         first, second = p.core == 0, p.core == 1
         self.own = p.copy(self.shard, even, first).start()
         even_sem, odd_sem = p.take("recv"), p.take("recv")
@@ -395,41 +393,43 @@
         self.to_far_odd = p.send(self.shard, odd, p.at(far=1), odd_sem, second).start()
         return self
 
-    def fetched(self):
-        p = self.place
-        self.own.wait()
-        self.to_far_even.arrived(p.core == 1)
-        self.to_sibling.arrived()
-        return self
-
-    def fetch_left(self):
-        self.to_far_even.left()
-        self.to_sibling.left()
-        self.to_far_odd.left()
-
-    def spread(self, even=None, odd=None):
+    def spread(self, core):
         p, block = self.place, self.block
-        even = block(EVEN) if even is None else even
-        odd = block(ODD) if odd is None else odd
-        self.even_x = p.send(even, block(EVEN_X), p.at(x=1)).start()
-        self.odd_y = p.send(odd, block(ODD_Y), p.at(y=1)).start()
-        self.odd_x = p.send(odd, block(ODD_X), p.at(x=1)).start()
-        self.even_y = p.send(even, block(EVEN_Y), p.at(y=1)).start()
+        here = p.core == core
+        if core:
+            self.to_far_even.arrived(here)
+        self.to_sibling.arrived(here)
+        even = block(EVEN) if core else self.shard
+        routes = (
+            (even, EVEN_X, p.at(x=1)), (block(ODD), ODD_Y, p.at(y=1)),
+            (block(ODD), ODD_X, p.at(x=1)), (even, EVEN_Y, p.at(y=1)),
+        )
+        for source, target, device in routes:
+            if target not in self.arrivals:
+                self.arrivals[target] = p.take("recv")
+            self.spreads.append(
+                p.send(source, block(target), device, self.arrivals[target], here).start()
+            )
         return self
 
     def relay(self):
         p, block = self.place, self.block
-        self.even_x.arrived()
+        even_x, odd_y, self.odd_x, self.even_y = self.spreads[:4]
+        even_x.arrived()
         self.even_xy = p.send(block(EVEN_X), block(EVEN_XY), p.at(y=1)).start()
-        self.odd_y.arrived()
+        odd_y.arrived()
         self.odd_xy = p.send(block(ODD_Y), block(ODD_XY), p.at(x=1)).start()
         return self
 
     def finish(self):
+        self.own.wait()
         for copy in (self.odd_x, self.even_y, self.even_xy, self.odd_xy):
             copy.arrived()
+
+    def left(self):
         for copy in (
-            self.even_x, self.odd_y, self.odd_x, self.even_y, self.even_xy, self.odd_xy,
+            *self.spreads, self.even_xy, self.odd_xy,
+            self.to_far_even, self.to_sibling, self.to_far_odd,
         ):
             copy.left()
 
@@ -748,19 +748,25 @@
 
 
 def forward_kernel(
-    inputs, cotangent, vectors, biases, cosine, sine_first, sine_latter,
+    inputs, cotangent, gain_first, shift_first, gain_second, shift_second, biases, turns,
     projections, output_weight, gate_up, down_weight,
     proj_full, out_full, gu_full, down_full, vectors_full, rows_one, rows_cot, heads_out, mixed_out,
     middle, rows_two, hidden_out, gate_out, up_out,
     own, normed, own_cot, vectors_here, biases_here, proj_here, out_here, rows_here, heads, mixed,
     near, far, got, got_beside, total, rows_later, gu_here, gate_wide, hidden, gate_act, up_act,
-    send_sems, recv_sems, local_sems,
+    vectors, own_bias, turns_here, send_sems, recv_sems, local_sems,
 ):
     p = Place(send_sems, recv_sems, local_sems)
     count = own.shape[0]
     late = lax.rem(p.tensor, 2)
-    tables = (cosine, sine_first, sine_latter)
+    tables = [turns_here.at[k] for k in range(3)]
     loads = load_local(p, inputs, own)
+    loads.append(p.copy(turns, turns_here).start())
+    vectors[...] = jnp.zeros_like(vectors)
+    for k, vector in enumerate((gain_first, shift_first, gain_second, shift_second)):
+        vectors[k : k + 1] = vector[...].astype(jnp.float32)
+    own_bias[...] = jnp.zeros_like(own_bias)
+    own_bias[0:3] = biases[...].astype(jnp.float32)
     cot_loads = load_local(p, cotangent, own_cot)
     p.greet()
     slots = {key: j for j, key in enumerate(ORDER)}
@@ -784,8 +790,8 @@
     own_vectors = p.copy(
         vectors, vectors_here.at[:, pl.ds(pl.multiple_of(own_slot * EIGHTH, EIGHTH), EIGHTH)]
     ).start()
-    own_biases = p.copy(biases, biases_here, p.core == 0).start()
-    far_biases = p.send(biases, biases_here, p.at(core=1, far=1), when=p.core == 0).start()
+    own_biases = p.copy(own_bias, biases_here, p.core == 0).start()
+    far_biases = p.send(own_bias, biases_here, p.at(core=1, far=1), when=p.core == 0).start()
 
     def third(j):
         return GatherWeight(
@@ -802,6 +808,8 @@
     down = GatherWeight(p, down_weight, lambda k: down_full.at[:, pl.ds(k * EIGHTH, EIGHTH)])
     thirds[0].fetch()
     thirds[1].fetch()
+    thirds[0].spread(0)
+    thirds[1].spread(0)
     wait_all(cot_loads)
     wait_all(loads)
     own_vectors.wait()
@@ -824,15 +832,16 @@
     gather_cot = GatherRows(p, own_cot, rows_cot)
     stores = [p.copy(vectors_here, vectors_full).start()]
 
-    thirds[0].fetched().spread()
-    thirds[2].fetch()
-    thirds[1].fetched().spread()
-    out.fetch()
+    thirds[0].spread(1)
+    thirds[2].fetch().spread(0)
+    thirds[1].spread(1)
+    out.fetch().spread(0)
     thirds[0].relay()
-    thirds[2].fetched().spread()
+    thirds[2].spread(1)
     gate.fetch()
     thirds[1].relay()
-    out.fetched().spread()
+    out.spread(1)
+    gate.spread(0)
     thirds[2].relay()
     gather_one.relay()
     gather_cot.start()
@@ -863,10 +872,11 @@
     gather_one.finish()
     stores.append(p.copy(rows_here, rows_one).start())
     project(0)
-    gate.fetched().spread()
+    gate.spread(1)
     project(1)
     out.relay()
     project(2)
+    up.spread(0)
     gather_cot.relay()
     stores.append(p.copy(heads, heads_out).start())
     attend_pair(heads, mixed, late)
@@ -884,8 +894,10 @@
     scatter.start()
     tiles(2 * count, 256, out_rows(near, 0))
     scatter.relay()
+    down.fetch()
     gate.relay()
-    up.fetched().spread()
+    up.spread(1)
+    down.spread(0)
     scatter.arrived()
     gain_two, shift_two = vectors_here[2:3], vectors_here[3:4]
 
@@ -897,11 +909,10 @@
     tiles(count, CHUNK, norm)
     gather = GatherRows(p, normed, rows_later).start()
     stores.append(p.copy(total, middle).start())
-    down.fetch()
     gather_cot.finish()
     gather.relay()
     up.relay()
-    down.fetched().spread()
+    down.spread(1)
     gate.finish()
     gather.finish()
     stores.append(p.copy(rows_later, rows_two).start())
@@ -929,7 +940,7 @@
     stores.append(p.copy(up_act, up_out).start())
     down.finish()
     for weight in (*thirds, out, gate, up, down):
-        weight.fetch_left()
+        weight.left()
     for sent in vector_sends:
         sent.left()
     scatter.finish()
@@ -956,9 +967,9 @@
 
 def back_kernel(
     hidden_in, gate_in, up_in, cot_rows, rows_two, gu_full, down_full, middle, vectors,
-    outputs, grad_middle, rows_branch, sums, down_owned, gate_sums, up_parts, down_parts,
+    out_half, grad_middle, rows_branch, sums, down_owned, gate_sums, up_parts, down_parts,
     hidden, gate_act, up_act, cot, rows_here, gate, up, down, value, near, got, got_beside,
-    got_out, got_out_beside, gain_sum, shift_sum, staging,
+    got_out, gain_sum, shift_sum, staging,
     down_got, down_last, down_home, down_result, gate_got, gate_last,
     send_sems, recv_sems, local_sems,
 ):
@@ -979,7 +990,7 @@
     far = cot.at[pl.ds(2 * count, 2 * count)]
     scatter = ScatterRows(p, far, near, got, got_beside)
     near_out = rows_here.at[pl.ds(0, 2 * count)]
-    out_scatter = ScatterRows(p, far, near_out, got_out, got_out_beside)
+    out_scatter = ScatterRows(p, far, near_out, got_out, None)
 
     def down_part(k):
         columns = pl.ds(k * quarter, quarter)
@@ -1039,7 +1050,6 @@
     weight_part(gate, gate_act, 0)
     weight_part(gate, gate_act, 1)
     down_sum.relay()
-    gate_sum.start()
     weight_part(gate, gate_act, 2)
     weight_part(gate, gate_act, 3)
 
@@ -1055,6 +1065,8 @@
     scatter.sibling.left()
     tiles(2 * count, 256, out_rows(far, 2 * count))
     out_scatter.start()
+    down_sum.settle()
+    gate_sum.start()
     tiles(2 * count, 256, out_rows(near_out, 0))
     scatter.arrived()
     gain = vectors[2:3]
@@ -1072,26 +1084,16 @@
 
     tiles(count, CHUNK, middle_back)
     gather = GatherRows(p, cot.at[pl.ds(0, count)], rows_branch).start()
-    grad_store = p.copy(value, grad_middle).start()
+    stores.append(p.copy(value, grad_middle).start())
     gain_sum[0:1] = jnp.sum(gain_sum[...], axis=0, keepdims=True)
     gain_sum[1:2] = jnp.sum(shift_sum[...], axis=0, keepdims=True)
     stores.append(p.copy(gain_sum, sums).start())
     scatter.beside.left()
-    grad_store.wait()
-    middle_load = p.copy(middle, value).start()
-    down_sum.settle()
+    out_scatter.sibling.arrived()
+    combine(near_out, [near_out, got_out], 32)
+    stores.append(p.copy(near_out, out_half).start())
     gather.relay()
-    out_scatter.relay()
     gate_sum.relay()
-    middle_load.wait()
-    out_scatter.arrived()
-    own_out = near_out.at[pl.ds(0, count)]
-
-    def out_total(rows):
-        own_out[rows] = (value[rows] + out_scatter.total(rows)).astype(own_out.dtype)
-
-    tiles(count, CHUNK, out_total)
-    stores += store_natural(p, own_out, outputs)
     down_sum.finish(down_owned)
     gate_sum.gather()
     for k in (0, 1):
@@ -1099,24 +1101,24 @@
     gate_sum.left()
     down_sum.stored()
     gather.finish()
-    out_scatter.finish()
+    out_scatter.sibling.left()
     wait_all(stores)
 
 
 def last_kernel(
     rows_branch, out_full, heads_in, mixed_in, rows_one, proj_full, inputs, vectors,
-    cosine, sine_first, sine_latter, grad_middle, sums, up_parts, gate_sums,
-    input_grads, proj_owned, out_owned, vector_grads, bias_grad, gu_owned,
+    turns, grad_middle, sums, up_parts, gate_sums, out_half, middle,
+    outputs, input_grads, proj_owned, out_owned, vector_grads, bias_grad, gu_owned,
     branch, out_here, heads, mixed, grad_mixed, grad_pre, rows_here, proj_here, out_send,
     own, got, got_beside, result, all_sums, shift_sum, vector_got, vector_total, z_got,
-    bias_here, bias_got, gate_home, gate_even, up_result, out_result, third_result, *rest,
+    bias_here, bias_got, turns_here, got_out, gate_home, gate_even, up_result, out_result, third_result, *rest,
 ):
     weight_refs = [rest[4 * k : 4 * k + 4] for k in range(5)]
     p = Place(*rest[20:])
     count, width = own.shape
     quarter = width // 4
     late = lax.rem(p.tensor, 2)
-    tables = (cosine, sine_first, sine_latter)
+    tables = [turns_here.at[k] for k in range(3)]
     first, second = p.core == 0, p.core == 1
     first_loads = [p.copy(rows_branch, branch).start(), p.copy(out_full, out_here).start()]
     p.greet()
@@ -1135,9 +1137,12 @@
     thirds = [
         weight_sum(proj_send[j], True, weight_refs[2 + j], third_result.at[j]) for j in range(3)
     ]
+    out_beside = p.send(out_half.at[pl.ds(count, count)], got_out, p.at(near=1)).start()
+    out_loads = [p.copy(out_half.at[pl.ds(0, count)], own).start(), p.copy(middle, result).start()]
     wait_all(first_loads)
     mixed_load = p.copy(mixed_in, mixed).start()
     head_load = p.copy(heads_in, heads).start()
+    out_loads.append(p.copy(turns, turns_here).start())
 
     @pl.loop(0, 4)
     def _(index):
@@ -1157,8 +1162,7 @@
         out_part(k)
     head_load.wait()
     later_loads = [p.copy(proj_full, proj_here).start(), p.copy(rows_one, rows_here).start()]
-    loads = load_local(p, inputs, own)
-    loads.append(p.copy(grad_middle, result).start())
+    wait_all(out_loads)
     gate_load = p.copy(gate_sums.at[0], gate_even).start()
     up.load(up_quarters[2:])
     attend_pair_back(heads, grad_mixed, grad_pre, tables, late)
@@ -1187,17 +1191,28 @@
     scatter.start()
     tiles(2 * count, 256, term_rows(near, 0))
     scatter.relay()
-    out.start()
+    out_beside.arrived()
+
+    def out_total(rows):
+        total = result[rows] + own[rows].astype(jnp.float32) + got_out[rows].astype(jnp.float32)
+        own[rows] = total.astype(own.dtype)
+
+    tiles(count, CHUNK, out_total)
+    stores = store_natural(p, own, outputs)
     for j in range(3):
         proj_part(j, 0)
         proj_part(j, 1)
     up.settle()
+    out.start()
     thirds[0].start()
+    thirds[1].start()
+    wait_all(stores)
+    loads = load_local(p, inputs, own)
+    loads.append(p.copy(grad_middle, result).start())
     for j in range(3):
         proj_part(j, 2)
         proj_part(j, 3)
     out.relay()
-    thirds[1].start()
 
     bias_here[...] = jnp.zeros_like(bias_here)
     for j in range(3):
@@ -1297,6 +1312,7 @@
     scatter.finish()
     for sent in vector_sends:
         sent.left()
+    out_beside.left()
     wait_all(stores)
     vector_store.wait()
     bias_store.wait()
@@ -1367,19 +1383,14 @@
     hidden_width = down_weight.shape[0]
     cosine, sine = angle_tables()
     rest = ((0, 0), (0, HD - ROTARY))
-    cosine_table, sine_first, sine_latter = (
+    turns = jnp.stack([
         jnp.tile(jnp.pad(table, rest, constant_values=fill), (1, 128 // HD))
         for table, fill in (
             (jnp.concatenate([cosine, cosine], axis=1), 1.0),
             (jnp.concatenate([-sine, jnp.zeros_like(sine)], axis=1), 0.0),
             (jnp.concatenate([jnp.zeros_like(sine), sine], axis=1), 0.0),
         )
-    )
-    vectors = jnp.pad(
-        jnp.stack([gain_first, shift_first, gain_second, shift_second]).astype(jnp.float32),
-        ((0, 4), (0, 0)),
-    )
-    wide_biases = jnp.pad(biases.astype(jnp.float32), ((0, 5), (0, 0)))
+    ])
     wide = bf16(rows, width)
     inner = bf16(rows, hidden_width)
     own = bf16(count, width)
@@ -1390,10 +1401,11 @@
     ) = call(
         forward_kernel, "forward", 1,
         (
-            inputs, cotangent, vectors, wide_biases, cosine_table, sine_first, sine_latter,
+            inputs, cotangent,
+            *(v[None] for v in (gain_first, shift_first, gain_second, shift_second)), biases, turns,
             projections, output_weight, gate_up, down_weight,
         ),
-        [ANY] * 4 + [WHOLE] * 3 + [ANY] * 4,
+        [ANY] * 2 + [WHOLE] * 5 + [ANY] * 5,
         [
             bf16(3, width, heads_width), bf16(heads_width, width), bf16(2, width, hidden_width),
             bf16(hidden_width, width), f32(8, width), wide, wide, bf16(3, rows, heads_width),
@@ -1405,15 +1417,16 @@
             held(bf16(3, rows, heads_width)), held(bf16(rows, heads_width)),
             held(half_rows), held(half_rows), held(half_rows), held(own), held(f32(count, width)),
             held(wide), held(bf16(2, width, hidden_width)), held(f32(rows, hidden_width)),
-            held(inner), held(inner), held(inner),
+            held(inner), held(inner), held(inner), held(f32(8, EIGHTH)), held(f32(8, heads_width)),
+            held(f32(*turns.shape)),
         ],
-        (96, 96, 64),
+        (128, 96, 64),
     )
 
     by_rows = ((2 * EIGHTH, hidden_width), (EIGHTH, hidden_width))
     by_columns = ((hidden_width, 2 * EIGHTH), (hidden_width, EIGHTH))
     (
-        outputs, grad_middle, gathered_branch, sums, down_owned, gate_sums, up_parts, _,
+        out_half, grad_middle, gathered_branch, sums, down_owned, gate_sums, up_parts, _,
     ) = call(
         back_kernel, "backward_first", 2,
         (
@@ -1421,7 +1434,7 @@
         ),
         [ANY] * 8 + [WHOLE],
         [
-            own, f32(count, width), wide, f32(8, width), f32(hidden_width, EIGHTH),
+            half_rows, f32(count, width), wide, f32(8, width), f32(hidden_width, EIGHTH),
             bf16(2, EIGHTH, hidden_width), bf16(width, hidden_width),
             bf16(2, hidden_width, 2 * EIGHTH),
         ],
@@ -1429,7 +1442,7 @@
             held(inner), held(inner), held(inner), held(wide), held(wide),
             held(bf16(width, hidden_width)), held(bf16(width, hidden_width)),
             held(bf16(hidden_width, width)), held(f32(count, width)),
-            held(half_rows), held(half_rows), held(own), held(half_rows), held(own),
+            held(half_rows), held(half_rows), held(own), held(half_rows),
             held(f32(8, width)), held(f32(8, width)), held(bf16(2, hidden_width, 2 * EIGHTH)),
             *weight_scratch(*by_columns)[1:], held(f32(hidden_width, EIGHTH)),
             *weight_scratch(*by_rows)[1:3],
@@ -1437,15 +1450,16 @@
         (64, 64, 48),
     )
     third = ((2 * EIGHTH, heads_width), (EIGHTH, heads_width))
-    input_grads, proj_owned, out_owned, vector_grads, bias_grad, gu_owned = call(
+    outputs, input_grads, proj_owned, out_owned, vector_grads, bias_grad, gu_owned = call(
         last_kernel, "backward_last", 3,
         (
             gathered_branch, out_full, heads, mixed_rows, gathered_one, proj_full, inputs, vectors,
-            cosine_table, sine_first, sine_latter, grad_middle, sums, up_parts, gate_sums,
+            turns, grad_middle, sums, up_parts, gate_sums,
+            out_half, middle,
         ),
-        [ANY] * 7 + [WHOLE] * 4 + [ANY, WHOLE, ANY, ANY],
+        [ANY] * 7 + [WHOLE] + [ANY] * 2 + [WHOLE] + [ANY] * 4,
         [
-            f32(count, width), f32(3, EIGHTH, heads_width), f32(heads_width, EIGHTH),
+            own, f32(count, width), f32(3, EIGHTH, heads_width), f32(heads_width, EIGHTH),
             f32(8, EIGHTH), f32(8, heads_width), f32(2, EIGHTH, hidden_width),
         ],
         [
@@ -1456,7 +1470,8 @@
             held(own), held(half_rows), held(own), held(f32(count, width)),
             held(f32(8, width)), held(f32(8, width)),
             held(f32(7, 8, EIGHTH)), held(f32(2, 8, EIGHTH)), held(f32(2, 8, EIGHTH)),
-            held(f32(8, heads_width)), held(f32(4, 8, heads_width)),
+            held(f32(8, heads_width)), held(f32(4, 8, heads_width)), held(f32(*turns.shape)),
+            held(own),
             held(bf16(2, EIGHTH, hidden_width)), held(bf16(EIGHTH, hidden_width)),
             held(f32(EIGHTH, hidden_width)), held(f32(heads_width, EIGHTH)),
             held(f32(3, EIGHTH, heads_width)),

time: 556 us -> 524 us (0.942)
  the two profiles are of different devices: /device:TPU:1 before, /device:TPU:9 now
where the time goes in v7:
time: 524 us; the launch traced here: 517 us
  Pallas kernels  497 us (95%)
  local copies, waits for them, and re-layouts  18 us (3%)
    pallas_call x3, Pallas kernels, call(): pl.pallas_call(body, out_shape=outs, in_specs=in_specs, out_specs=[ANY] *...  497 us

profile of v7, /device:TPU:9, one launch (start us, length us, event | category | flops | bytes accessed | tf_op | source)
XLA Modules:
  0.0 517.0 jit_solution(638473268703997178)
XLA Ops:
  0.7 1.2 broadcast_in_dim.14.gain_first
  1.9 1.2 broadcast_in_dim.15.shift_first
  3.1 1.2 broadcast_in_dim.16.gain_second
  4.3 1.2 broadcast_in_dim.17.shift_second
  5.5 0.1 multiply_cosine_fusion
  5.7 0.1 copy.22
  5.9 0.1 copy.24
  6.1 0.1 copy.23
  6.2 0.9 pad_maximum_fusion.turns
  7.2 222.9 %forward.1 = (bf16[3,2048,512]{2,1,0:T(8,128)(2,1)}, bf16[512,2048]{1,0:T(8,128)(2,1)}, bf16[2,2048,1408]{2,1,0:T(8,128)(2,1)}, bf16[1408,2048]{1,0:T(8,128)(2,1...) custom-call(bf16[256,2048]{1,0:T(8,128)(2,1)} %inputs.3, ...), custom_call_target="tpu_custom_call" | custom-call | bytes 106561536 | tf_op jit(solution)/shard_map/forward/pallas_call | solution.py:1323
  230.0 123.8 %backward_first.1 = (bf16[512,2048]{1,0:T(8,128)(2,1)}, f32[256,2048]{1,0:T(8,128)}, bf16[1024,2048]{1,0:T(8,128)(2,1)}, f32[8,2048]{1,0:T(8,128)}, f32[1408,256...) custom-call(bf16[1024,1408]{1,0:T(8,128)(2,1)} %get-tuple-element.39.hidden, ...), custom_call_target="tpu_custom_call" | custom-call | bytes 39976960 | tf_op jit(solution)/shard_map/backward_first/pallas_call | solution.py:1323
  353.9 150.0 %backward_last.1 = (bf16[256,2048]{1,0:T(8,128)(2,1)}, f32[256,2048]{1,0:T(8,128)}, f32[3,256,512]{2,1,0:T(8,128)}, f32[512,256]{1,0:T(8,128)}, f32[8,256]{1,0:T...) custom-call(bf16[1024,2048]{1,0:T(8,128)(2,1)} %get-tuple-element.48.rows_branch, ...), custom_call_target="tpu_custom_call" | custom-call | bytes 16302080 | tf_op jit(solution)/shard_map/backward_last/pallas_call | solution.py:1323
  503.9 0.0 copy-start.1
  503.9 1.5 fusion.1
  505.4 1.3 slice.17
  506.7 2.4 copy.31
  509.1 1.3 copy.32
  510.4 0.0 copy-done.2
  510.4 1.1 copy.33
  511.6 0.8 copy.34
  512.4 0.6 copy-done
  513.0 1.6 copy.35
  514.6 0.8 copy-done.3
  515.4 1.1 copy.36
  (14 shorter events, 0.1 us)
Async XLA Ops:
  503.9 5.2 %copy-start.1 = (f32[256,2048]{1,0:T(8,128)S(1)}, f32[256,2048]{1,0:T(8,128)}, u32[]{:S(2)}) copy-start(f32[256,2048]{1,0:T(8,128)} %get-tuple-element.86) | copy-start | bytes 6291460
  506.7 3.8 copy-start.2
  509.1 2.5 copy-start.4
  510.4 2.6 copy-start
  513.0 2.4 copy-start.3

commit v8 on v7

--- a/solution.py
+++ b/solution.py
@@ -748,10 +748,10 @@
 
 
 def forward_kernel(
-    inputs, cotangent, gain_first, shift_first, gain_second, shift_second, biases, turns,
+    inputs, cotangent, parameters, biases, turns,
     projections, output_weight, gate_up, down_weight,
     proj_full, out_full, gu_full, down_full, vectors_full, rows_one, rows_cot, heads_out, mixed_out,
-    middle, rows_two, hidden_out, gate_out, up_out,
+    middle, rows_two, hidden_out, gate_out, up_out, down_parts,
     own, normed, own_cot, vectors_here, biases_here, proj_here, out_here, rows_here, heads, mixed,
     near, far, got, got_beside, total, rows_later, gu_here, gate_wide, hidden, gate_act, up_act,
     vectors, own_bias, turns_here, send_sems, recv_sems, local_sems,
@@ -763,8 +763,7 @@
     loads = load_local(p, inputs, own)
     loads.append(p.copy(turns, turns_here).start())
     vectors[...] = jnp.zeros_like(vectors)
-    for k, vector in enumerate((gain_first, shift_first, gain_second, shift_second)):
-        vectors[k : k + 1] = vector[...].astype(jnp.float32)
+    vectors[0:4] = parameters[...].astype(jnp.float32)
     own_bias[...] = jnp.zeros_like(own_bias)
     own_bias[0:3] = biases[...].astype(jnp.float32)
     cot_loads = load_local(p, cotangent, own_cot)
@@ -870,7 +869,7 @@
                 heads[j, target, lanes] = part.astype(heads.dtype)
 
     gather_one.finish()
-    stores.append(p.copy(rows_here, rows_one).start())
+    rows_store = p.copy(rows_here, rows_one).start()
     project(0)
     gate.spread(1)
     project(1)
@@ -916,14 +915,16 @@
     gate.finish()
     gather.finish()
     stores.append(p.copy(rows_later, rows_two).start())
-    stores.append(p.copy(gu_here.at[0], gu_full.at[0]).start())
+    gate_store = p.copy(gu_here.at[0], gu_full.at[0]).start()
+    rows_store.wait()
+    cot_load = p.copy(rows_cot, rows_here).start()
 
     def gate_rows(rows):
         gate_wide[rows] = dot(rows_later[rows], gu_here[0], (1, 0))
 
     tiles(4 * count, 256, gate_rows)
     up.finish()
-    stores.append(p.copy(gu_here.at[1], gu_full.at[1]).start())
+    up_store = p.copy(gu_here.at[1], gu_full.at[1]).start()
 
     def up_rows(rows):
         wide_up = dot(rows_later[rows], gu_here[1], (1, 0))
@@ -938,8 +939,20 @@
     stores.append(p.copy(hidden, hidden_out).start())
     stores.append(p.copy(gate_act, gate_out).start())
     stores.append(p.copy(up_act, up_out).start())
+    cot_load.wait()
+    gate_store.wait()
+    gate.left()
+    quarter = down_parts.shape[2]
+    for k in range(4):
+        if k == 2:
+            up_store.wait()
+            up.left()
+        columns = pl.ds((k % 2) * quarter, quarter)
+        part = gu_here.at[k // 2, pl.ds(0, hidden.shape[1]), columns]
+        part[...] = dot(hidden[...], rows_here[:, pl.ds(k * quarter, quarter)], (0, 0)).astype(part.dtype)
+        stores.append(p.copy(part, down_parts.at[k]).start())
     down.finish()
-    for weight in (*thirds, out, gate, up, down):
+    for weight in (*thirds, out, down):
         weight.left()
     for sent in vector_sends:
         sent.left()
@@ -966,8 +979,8 @@
 
 
 def back_kernel(
-    hidden_in, gate_in, up_in, cot_rows, rows_two, gu_full, down_full, middle, vectors,
-    out_half, grad_middle, rows_branch, sums, down_owned, gate_sums, up_parts, down_parts,
+    hidden_in, gate_in, up_in, cot_rows, rows_two, gu_full, down_full, down_parts, middle, vectors,
+    out_half, grad_middle, rows_branch, sums, down_owned, gate_sums, up_parts,
     hidden, gate_act, up_act, cot, rows_here, gate, up, down, value, near, got, got_beside,
     got_out, gain_sum, shift_sum, staging,
     down_got, down_last, down_home, down_result, gate_got, gate_last,
@@ -977,7 +990,10 @@
     count, width = value.shape
     hidden_width = hidden.shape[1]
     quarter = width // 4
-    first_loads = [p.copy(hidden_in, hidden).start(), p.copy(cot_rows, cot).start()]
+    first_loads = [
+        p.copy(cot_rows, cot).start(), p.copy(down_full, down).start(),
+        p.copy(gate_in, gate_act).start(), p.copy(up_in, up_act).start(),
+    ]
     p.greet()
     down_sum = ScatterWeight(
         p, [down_parts.at[0], down_parts.at[1]], [staging.at[0], staging.at[1]], False,
@@ -992,25 +1008,8 @@
     near_out = rows_here.at[pl.ds(0, 2 * count)]
     out_scatter = ScatterRows(p, far, near_out, got_out, None)
 
-    def down_part(k):
-        columns = pl.ds(k * quarter, quarter)
-        staging[k % 2] = dot(hidden[...], cot[:, columns], (0, 0)).astype(staging.dtype)
-
+    down_sum.start()
     wait_all(first_loads)
-    second_loads = [
-        p.copy(down_full, down).start(), p.copy(gate_in, gate_act).start(), p.copy(up_in, up_act).start(),
-    ]
-    down_part(0)
-    store_even = p.copy(staging.at[0], down_parts.at[0]).start()
-    down_part(1)
-    store_odd = p.copy(staging.at[1], down_parts.at[1]).start()
-    store_even.wait()
-    down_sum.start_even()
-    down_part(2)
-    store_odd.wait()
-    down_sum.start_odd()
-    down_part(3)
-    wait_all(second_loads)
     third_loads = [p.copy(gu_full.at[0], gate).start(), p.copy(gu_full.at[1], up).start()]
 
     def hidden_back(rows):
@@ -1026,7 +1025,11 @@
 
     tiles(4 * count, 256, hidden_back)
     wait_all(third_loads)
-    last_loads = [p.copy(rows_two, rows_here).start(), p.copy(middle, value).start()]
+    last_loads = [
+        p.copy(rows_two, rows_here).start(), p.copy(middle, value).start(),
+        p.copy(hidden_in, hidden).start(),
+    ]
+    down_sum.load([down_parts.at[2], down_parts.at[3]])
 
     def second_rows(target, offset):
         def part(rows):
@@ -1397,19 +1400,21 @@
     half_rows = bf16(2 * count, width)
     (
         proj_full, out_full, gu_full, down_full, vectors, gathered_one, gathered_cot, heads, mixed_rows,
-        middle, gathered_two, hidden, gate_act, up_act,
+        middle, gathered_two, hidden, gate_act, up_act, down_parts,
     ) = call(
         forward_kernel, "forward", 1,
         (
             inputs, cotangent,
-            *(v[None] for v in (gain_first, shift_first, gain_second, shift_second)), biases, turns,
+            jnp.concatenate([gain_first, shift_first, gain_second, shift_second]).reshape(4, -1),
+            biases, turns,
             projections, output_weight, gate_up, down_weight,
         ),
-        [ANY] * 2 + [WHOLE] * 5 + [ANY] * 5,
+        [ANY] * 2 + [WHOLE] * 2 + [ANY] * 5,
         [
             bf16(3, width, heads_width), bf16(heads_width, width), bf16(2, width, hidden_width),
             bf16(hidden_width, width), f32(8, width), wide, wide, bf16(3, rows, heads_width),
             bf16(rows, heads_width), f32(count, width), wide, inner, inner, inner,
+            bf16(4, hidden_width, 2 * EIGHTH),
         ],
         [
             held(own), held(own), held(own), held(f32(8, width)), held(f32(8, heads_width)),
@@ -1426,17 +1431,17 @@
     by_rows = ((2 * EIGHTH, hidden_width), (EIGHTH, hidden_width))
     by_columns = ((hidden_width, 2 * EIGHTH), (hidden_width, EIGHTH))
     (
-        out_half, grad_middle, gathered_branch, sums, down_owned, gate_sums, up_parts, _,
+        out_half, grad_middle, gathered_branch, sums, down_owned, gate_sums, up_parts,
     ) = call(
         back_kernel, "backward_first", 2,
         (
-            hidden, gate_act, up_act, gathered_cot, gathered_two, gu_full, down_full, middle, vectors,
+            hidden, gate_act, up_act, gathered_cot, gathered_two, gu_full, down_full, down_parts,
+            middle, vectors,
         ),
-        [ANY] * 8 + [WHOLE],
+        [ANY] * 9 + [WHOLE],
         [
             half_rows, f32(count, width), wide, f32(8, width), f32(hidden_width, EIGHTH),
             bf16(2, EIGHTH, hidden_width), bf16(width, hidden_width),
-            bf16(2, hidden_width, 2 * EIGHTH),
         ],
         [
             held(inner), held(inner), held(inner), held(wide), held(wide),

time: 524 us -> 515 us (0.983)
  Pallas kernels: 497 us -> 490 us
    pallas_call x3, Pallas kernels: 497 us -> 490 us  [call(): pl.pallas_call(body, out_shape=outs, in_specs=in_specs, out_specs=[ANY] *...]
where the time goes in v8:
time: 515 us; the launch traced here: 507 us
  Pallas kernels  490 us (95%)
  local copies, waits for them, and re-layouts  13.7 us (3%)
    pallas_call x3, Pallas kernels, call(): pl.pallas_call(body, out_shape=outs, in_specs=in_specs, out_specs=[ANY] *...  490 us

profile of v8, /device:TPU:9, one launch (start us, length us, event | category | flops | bytes accessed | tf_op | source)
XLA Modules:
  0.0 507.2 jit_solution(17541791237232505523)
XLA Ops:
  0.7 0.7 pad_maximum_fusion.1
  1.4 0.6 reshape.55.parameters
  2.0 0.1 multiply_cosine_fusion
  2.2 0.1 copy.22
  2.4 0.1 copy.24
  2.5 0.1 copy.23
  2.6 0.9 pad_maximum_fusion.turns
  3.6 222.8 %forward.1 = (bf16[3,2048,512]{2,1,0:T(8,128)(2,1)}, bf16[512,2048]{1,0:T(8,128)(2,1)}, bf16[2,2048,1408]{2,1,0:T(8,128)(2,1)}, bf16[1408,2048]{1,0:T(8,128)(2,1...) custom-call(bf16[256,2048]{1,0:T(8,128)(2,1)} %inputs.3, ...), custom_call_target="tpu_custom_call" | custom-call | bytes 118095872 | tf_op jit(solution)/shard_map/forward/pallas_call | solution.py:1326
  226.4 118.7 %backward_first.1 = (bf16[512,2048]{1,0:T(8,128)(2,1)}, f32[256,2048]{1,0:T(8,128)}, bf16[1024,2048]{1,0:T(8,128)(2,1)}, f32[8,2048]{1,0:T(8,128)}, f32[1408,256...) custom-call(bf16[1024,1408]{1,0:T(8,128)(2,1)} %get-tuple-element.40.hidden_in, ...), custom_call_target="tpu_custom_call" | custom-call | bytes 34209792 | tf_op jit(solution)/shard_map/backward_first/pallas_call | solution.py:1326
  345.0 149.1 %backward_last.1 = (bf16[256,2048]{1,0:T(8,128)(2,1)}, f32[256,2048]{1,0:T(8,128)}, f32[3,256,512]{2,1,0:T(8,128)}, f32[512,256]{1,0:T(8,128)}, f32[8,256]{1,0:T...) custom-call(bf16[1024,2048]{1,0:T(8,128)(2,1)} %get-tuple-element.50.rows_branch, ...), custom_call_target="tpu_custom_call" | custom-call | bytes 16302080 | tf_op jit(solution)/shard_map/backward_last/pallas_call | solution.py:1326
  494.1 0.0 copy-start.1
  494.1 1.5 fusion.1
  495.6 1.3 slice.17
  496.9 2.4 copy.31
  499.3 0.0 copy-done.1
  499.3 1.3 copy.32
  500.7 0.0 copy-done.2
  500.7 1.1 copy.33
  501.8 0.0 copy-done.4
  501.8 0.8 copy.34
  502.6 0.6 copy-done
  503.2 1.6 copy.35
  504.8 0.8 copy-done.3
  505.7 1.1 copy.36
  (12 shorter events, 0.1 us)
Async XLA Ops:
  494.1 5.2 %copy-start.1 = (f32[256,2048]{1,0:T(8,128)S(1)}, f32[256,2048]{1,0:T(8,128)}, u32[]{:S(2)}) copy-start(f32[256,2048]{1,0:T(8,128)} %get-tuple-element.88) | copy-start | bytes 6291460
  496.9 3.8 copy-start.2
  499.3 2.5 copy-start.4
  500.7 2.6 copy-start
  503.2 2.4 copy-start.3

commit v9 on v8

--- a/solution.py
+++ b/solution.py
@@ -842,6 +842,7 @@
     out.spread(1)
     gate.spread(0)
     thirds[2].relay()
+    out.relay()
     gather_one.relay()
     gather_cot.start()
     up.fetch()
@@ -873,7 +874,6 @@
     project(0)
     gate.spread(1)
     project(1)
-    out.relay()
     project(2)
     up.spread(0)
     gather_cot.relay()
@@ -893,10 +893,8 @@
     scatter.start()
     tiles(2 * count, 256, out_rows(near, 0))
     scatter.relay()
-    down.fetch()
     gate.relay()
     up.spread(1)
-    down.spread(0)
     scatter.arrived()
     gain_two, shift_two = vectors_here[2:3], vectors_here[3:4]
 
@@ -907,6 +905,7 @@
 
     tiles(count, CHUNK, norm)
     gather = GatherRows(p, normed, rows_later).start()
+    down.fetch().spread(0)
     stores.append(p.copy(total, middle).start())
     gather_cot.finish()
     gather.relay()

time: 515 us -> 502 us (0.975)
  Pallas kernels: 490 us -> 478 us
    pallas_call x3, Pallas kernels: 490 us -> 478 us  [call(): pl.pallas_call(body, out_shape=outs, in_specs=in_specs, out_specs=[ANY] *...]
where the time goes in v9:
time: 502 us; the launch traced here: 495 us
  Pallas kernels  478 us (95%)
  local copies, waits for them, and re-layouts  13.7 us (3%)
    pallas_call x3, Pallas kernels, call(): pl.pallas_call(body, out_shape=outs, in_specs=in_specs, out_specs=[ANY] *...  478 us

profile of v9, /device:TPU:9, one launch (start us, length us, event | category | flops | bytes accessed | tf_op | source)
XLA Modules:
  0.0 494.6 jit_solution(4915796521791569565)
XLA Ops:
  0.7 0.7 pad_maximum_fusion.1
  1.4 0.6 reshape.55.parameters
  2.0 0.1 multiply_cosine_fusion
  2.2 0.1 copy.22
  2.4 0.1 copy.24
  2.5 0.1 copy.23
  2.6 0.9 pad_maximum_fusion.turns
  3.6 223.2 %forward.1 = (bf16[3,2048,512]{2,1,0:T(8,128)(2,1)}, bf16[512,2048]{1,0:T(8,128)(2,1)}, bf16[2,2048,1408]{2,1,0:T(8,128)(2,1)}, bf16[1408,2048]{1,0:T(8,128)(2,1...) custom-call(bf16[256,2048]{1,0:T(8,128)(2,1)} %inputs.3, ...), custom_call_target="tpu_custom_call" | custom-call | bytes 118095872 | tf_op jit(solution)/shard_map/forward/pallas_call | solution.py:1325
  226.8 106.4 %backward_first.1 = (bf16[512,2048]{1,0:T(8,128)(2,1)}, f32[256,2048]{1,0:T(8,128)}, bf16[1024,2048]{1,0:T(8,128)(2,1)}, f32[8,2048]{1,0:T(8,128)}, f32[1408,256...) custom-call(bf16[1024,1408]{1,0:T(8,128)(2,1)} %get-tuple-element.40.hidden_in, ...), custom_call_target="tpu_custom_call" | custom-call | bytes 34209792 | tf_op jit(solution)/shard_map/backward_first/pallas_call | solution.py:1325
  333.2 148.3 %backward_last.1 = (bf16[256,2048]{1,0:T(8,128)(2,1)}, f32[256,2048]{1,0:T(8,128)}, f32[3,256,512]{2,1,0:T(8,128)}, f32[512,256]{1,0:T(8,128)}, f32[8,256]{1,0:T...) custom-call(bf16[1024,2048]{1,0:T(8,128)(2,1)} %get-tuple-element.50.rows_branch, ...), custom_call_target="tpu_custom_call" | custom-call | bytes 16302080 | tf_op jit(solution)/shard_map/backward_last/pallas_call | solution.py:1325
  481.5 0.0 copy-start.1
  481.5 1.5 fusion.1
  483.0 1.3 slice.17
  484.3 2.4 copy.31
  486.7 0.0 copy-done.1
  486.7 1.3 copy.32
  488.0 0.0 copy-done.2
  488.0 1.1 copy.33
  489.2 0.0 copy-done.4
  489.2 0.8 copy.34
  490.0 0.6 copy-done
  490.6 1.6 copy.35
  492.2 0.8 copy-done.3
  493.0 1.1 copy.36
  (12 shorter events, 0.1 us)
Async XLA Ops:
  481.5 5.2 %copy-start.1 = (f32[256,2048]{1,0:T(8,128)S(1)}, f32[256,2048]{1,0:T(8,128)}, u32[]{:S(2)}) copy-start(f32[256,2048]{1,0:T(8,128)} %get-tuple-element.88) | copy-start | bytes 6291460
  484.3 3.8 copy-start.2
  486.7 2.5 copy-start.4
  488.0 2.6 copy-start
  490.6 2.4 copy-start.3

commit v10 on v9

--- a/solution.py
+++ b/solution.py
@@ -905,10 +905,10 @@
 
     tiles(count, CHUNK, norm)
     gather = GatherRows(p, normed, rows_later).start()
-    down.fetch().spread(0)
     stores.append(p.copy(total, middle).start())
     gather_cot.finish()
     gather.relay()
+    down.fetch().spread(0)
     up.relay()
     down.spread(1)
     gate.finish()

time: 502 us -> 512 us (1.020)
  Pallas kernels: 478 us -> 487 us
    pallas_call x3, Pallas kernels: 478 us -> 487 us  [call(): pl.pallas_call(body, out_shape=outs, in_specs=in_specs, out_specs=[ANY] *...]
where the time goes in v10:
time: 512 us; the launch traced here: 504 us
  Pallas kernels  487 us (95%)
  local copies, waits for them, and re-layouts  13.7 us (3%)
    pallas_call x3, Pallas kernels, call(): pl.pallas_call(body, out_shape=outs, in_specs=in_specs, out_specs=[ANY] *...  487 us

profile of v10, /device:TPU:9, one launch (start us, length us, event | category | flops | bytes accessed | tf_op | source)
XLA Modules:
  0.0 504.2 jit_solution(4412166874595977990)
XLA Ops:
  0.7 0.7 pad_maximum_fusion.1
  1.4 0.6 reshape.55.parameters
  2.0 0.1 multiply_cosine_fusion
  2.2 0.1 copy.22
  2.4 0.1 copy.24
  2.5 0.1 copy.23
  2.6 0.9 pad_maximum_fusion.turns
  3.6 235.5 %forward.1 = (bf16[3,2048,512]{2,1,0:T(8,128)(2,1)}, bf16[512,2048]{1,0:T(8,128)(2,1)}, bf16[2,2048,1408]{2,1,0:T(8,128)(2,1)}, bf16[1408,2048]{1,0:T(8,128)(2,1...) custom-call(bf16[256,2048]{1,0:T(8,128)(2,1)} %inputs.3, ...), custom_call_target="tpu_custom_call" | custom-call | bytes 118095872 | tf_op jit(solution)/shard_map/forward/pallas_call | solution.py:1325
  239.0 106.4 %backward_first.1 = (bf16[512,2048]{1,0:T(8,128)(2,1)}, f32[256,2048]{1,0:T(8,128)}, bf16[1024,2048]{1,0:T(8,128)(2,1)}, f32[8,2048]{1,0:T(8,128)}, f32[1408,256...) custom-call(bf16[1024,1408]{1,0:T(8,128)(2,1)} %get-tuple-element.40.hidden_in, ...), custom_call_target="tpu_custom_call" | custom-call | bytes 34209792 | tf_op jit(solution)/shard_map/backward_first/pallas_call | solution.py:1325
  345.4 145.7 %backward_last.1 = (bf16[256,2048]{1,0:T(8,128)(2,1)}, f32[256,2048]{1,0:T(8,128)}, f32[3,256,512]{2,1,0:T(8,128)}, f32[512,256]{1,0:T(8,128)}, f32[8,256]{1,0:T...) custom-call(bf16[1024,2048]{1,0:T(8,128)(2,1)} %get-tuple-element.50.rows_branch, ...), custom_call_target="tpu_custom_call" | custom-call | bytes 16302080 | tf_op jit(solution)/shard_map/backward_last/pallas_call | solution.py:1325
  491.1 0.0 copy-start.1
  491.1 1.5 fusion.1
  492.6 1.3 slice.17
  493.9 2.4 copy.31
  496.3 0.0 copy-done.1
  496.3 1.3 copy.32
  497.7 0.0 copy-done.2
  497.7 1.1 copy.33
  498.8 0.0 copy-done.4
  498.8 0.8 copy.34
  499.6 0.6 copy-done
  500.2 1.6 copy.35
  501.8 0.8 copy-done.3
  502.7 1.1 copy.36
  (12 shorter events, 0.1 us)
Async XLA Ops:
  491.1 5.2 %copy-start.1 = (f32[256,2048]{1,0:T(8,128)S(1)}, f32[256,2048]{1,0:T(8,128)}, u32[]{:S(2)}) copy-start(f32[256,2048]{1,0:T(8,128)} %get-tuple-element.88) | copy-start | bytes 6291460
  493.9 3.8 copy-start.2
  496.3 2.5 copy-start.4
  497.7 2.6 copy-start
  500.2 2.4 copy-start.3
